TPU v7x, 32 devices: a whole 2x2x4 slice. The times are simulated.
32 devices in a mesh: dp: 8 (over z, core), tensor: 4 (over y, x).
Axes of the slice: x: 2, y: 2, z: 4, core: 2. Of those that a mesh axis runs over, the one named last changes fastest.
Arguments:
- tokens: bfloat16 [8192, 1536], P(('dp', 'tensor')), may hold values from -6 to 6
- norm_gain: float32 [1536], replicated, may hold values from 0.5 to 1.5
- gate_proj: bfloat16 [1536, 3072], P('dp', 'tensor'), may hold values from -0.15625 to 0.15625
- inner_proj: bfloat16 [1536, 3072], P('dp', 'tensor'), may hold values from -0.15625 to 0.15625
- shared_proj: bfloat16 [1536, 256], P('dp'), may hold values from -0.15625 to 0.15625
- step_proj: bfloat16 [1536, 48], P('dp', 'tensor'), may hold values from -0.15625 to 0.15625
- conv_inner: float32 [4, 3072], P(None, 'tensor'), may hold values from -3 to 3
- conv_inner_bias: float32 [3072], P('tensor'), may hold values from -3 to 3
- conv_shared: float32 [4, 256], replicated, may hold values from -3 to 3
- conv_shared_bias: float32 [256], replicated, may hold values from -3 to 3
- step_bias: float32 [48], P('tensor'), may hold values from -4.5 to -1.5
- decay_log: float32 [48], P('tensor'), may hold values from 0 to 2.77
- skip_gain: float32 [48], P('tensor'), may hold values from 0.5 to 1.5
- out_gain: float32 [3072], P('tensor'), may hold values from 0.5 to 1.5
- out_proj: bfloat16 [3072, 1536], P('tensor', 'dp'), may hold values from -0.109375 to 0.109375
- cotangent: bfloat16 [8192, 1536], P(('dp', 'tensor')), may hold values from -6 to 6
Outputs:
- mixed: bfloat16 [8192, 1536], P(('dp', 'tensor'))
- grad_tokens: float32 [8192, 1536], P(('dp', 'tensor'))
- grad_norm_gain: float32 [1536], replicated
- grad_gate_proj: float32 [1536, 3072], P('dp', 'tensor')
- grad_inner_proj: float32 [1536, 3072], P('dp', 'tensor')
- grad_shared_proj: float32 [1536, 256], P('dp')
- grad_step_proj: float32 [1536, 48], P('dp', 'tensor')
- grad_conv_inner: float32 [4, 3072], P(None, 'tensor')
- grad_conv_inner_bias: float32 [3072], P('tensor')
- grad_conv_shared: float32 [4, 256], replicated
- grad_conv_shared_bias: float32 [256], replicated
- grad_step_bias: float32 [48], P('tensor')
- grad_decay_log: float32 [48], P('tensor')
- grad_skip_gain: float32 [48], P('tensor')
- grad_out_gain: float32 [3072], P('tensor')
- grad_out_proj: float32 [3072, 1536], P('tensor', 'dp')
All inputs are finite; a program needn't handle non-finite values.
Results may differ from a plain program's by a relative error of at most 0.012.
Values may be sent and summed in bfloat16 or wider, within the bound.
No kernel may reach another device: no remote copies, remote signals or barrier semaphores. Data moves between devices by JAX's collectives and lax.ppermute only.
A program may use at most 128 MiB of HBM per device.

v0:
```python
import jax
import jax.numpy as jnp
from jax import lax
from jax.sharding import PartitionSpec as P

HEAD_DIM = 64
STATE = 128
CONV = 4
SPAN = 256
SEQ = 1024
DI = 3072


epsilon = 1e-05
highest = lax.Precision.HIGHEST


def conv_silu(values, weight, conv_bias):
    channels = values.shape[-1]
    blocks = values.reshape(-1, SEQ, channels)
    padded = jnp.pad(blocks, ((0, 0), (CONV - 1, 0), (0, 0)))
    summed = conv_bias + weight[0] * padded[:, 0:SEQ]
    for offset in range(1, CONV):
        summed = summed + weight[offset] * padded[:, offset : offset + SEQ]
    return jax.nn.silu(summed).reshape(-1, channels)


def scan_heads(values, step_sizes, decay_rates, write_state, read_state, skip_gain):
    head_count = step_sizes.shape[-1]
    spans = SEQ // SPAN
    shaped = values.reshape(-1, spans, SPAN, head_count, HEAD_DIM)
    step_blocks = step_sizes.reshape(-1, spans, SPAN, head_count)
    write_blocks = write_state.reshape(-1, spans, SPAN, STATE)
    read_blocks = read_state.reshape(-1, spans, SPAN, STATE)
    cumulated = jnp.cumsum(step_blocks * decay_rates, axis=2)
    places = jnp.arange(SPAN)
    causal = (places[:, None] >= places[None, :])[None, None, :, :, None]
    log_gaps = cumulated[:, :, :, None, :] - cumulated[:, :, None, :, :]
    kernel = jnp.exp(jnp.where(causal, log_gaps, -1e30))
    scores = jnp.einsum("sctn,scun->sctu", read_blocks, write_blocks, precision=highest)
    weighted = shaped * step_blocks[..., None]
    within = jnp.einsum(
        "sctuh,scuhp->scthp", scores[..., None] * kernel, weighted, precision=highest
    )
    final_log = cumulated[:, :, -1, :]
    tail_decay = jnp.exp(final_log[:, :, None, :] - cumulated)
    states = jnp.einsum(
        "scuhp,scun->schpn", tail_decay[..., None] * weighted, write_blocks, precision=highest
    )
    carried = jnp.zeros_like(states[:, 0])
    entering = []
    for span_index in range(spans):
        entering.append(carried)
        carried = (
            jnp.exp(final_log[:, span_index])[:, :, None, None] * carried + states[:, span_index]
        )
    entering = jnp.stack(entering, axis=1)
    across = (
        jnp.einsum("sctn,schpn->scthp", read_blocks, entering, precision=highest)
        * jnp.exp(cumulated)[..., None]
    )
    result = within + across + skip_gain[:, None] * shaped
    return result.reshape(values.shape)


def gated_scan(inner_conv, shared_conv, gate_values, step_values, step_bias, decay_log, skip_gain):
    step_sizes = jax.nn.softplus(step_values + step_bias)
    scanned = scan_heads(
        inner_conv,
        step_sizes,
        -jnp.exp(decay_log),
        shared_conv[:, :STATE],
        shared_conv[:, STATE:],
        skip_gain,
    )
    return scanned * jax.nn.silu(gate_values)


def out_norm(gated_rows, squares, out_gain):
    return gated_rows * lax.rsqrt(squares[:, None] / DI + epsilon) * out_gain


def pre_norm(token_rows, norm_gain):
    inverse = lax.rsqrt(jnp.mean(token_rows * token_rows, axis=-1, keepdims=True) + epsilon)
    return token_rows * inverse * norm_gain


def fetch_inputs(gate_proj, inner_proj, shared_proj, step_proj):
    return (
        lax.all_gather(gate_proj, "dp", axis=0, tiled=True),
        lax.all_gather(inner_proj, "dp", axis=0, tiled=True),
        lax.all_gather(shared_proj, "dp", axis=0, tiled=True),
        lax.all_gather(step_proj, "dp", axis=0, tiled=True),
    )


def fetch_output(out_proj):
    return lax.all_gather(out_proj, "dp", axis=1, tiled=True)


def transposed(first_operand, second_operand):
    return lax.dot_general(
        first_operand, second_operand, (((1,), (1,)), ((), ())), preferred_element_type=jnp.float32
    )


def leading(first_operand, second_operand):
    return lax.dot_general(
        first_operand, second_operand, (((0,), (0,)), ((), ())), preferred_element_type=jnp.float32
    )


def rounded_copy(values):
    return lax.optimization_barrier(values.astype(jnp.bfloat16)).astype(jnp.float32)


def local(
    tokens,
    norm_gain,
    gate_proj,
    inner_proj,
    shared_proj,
    step_proj,
    conv_inner,
    conv_inner_bias,
    conv_shared,
    conv_shared_bias,
    step_bias,
    decay_log,
    skip_gain,
    out_gain,
    out_proj,
    cotangent,
):
    token_rows = tokens.astype(jnp.float32)
    normed, norm_pull = jax.vjp(pre_norm, token_rows, norm_gain)
    normed_low = normed.astype(jnp.bfloat16)
    group_rows = lax.all_gather(normed_low, "tensor", axis=0, tiled=True)
    inward_full = fetch_inputs(gate_proj, inner_proj, shared_proj, step_proj)
    outward_full = fetch_output(out_proj)
    gate_full, inner_full, shared_full, step_full = inward_full
    gate_values = jnp.dot(group_rows, gate_full, preferred_element_type=jnp.float32)
    inner_values = jnp.dot(group_rows, inner_full, preferred_element_type=jnp.float32)
    shared_values = jnp.dot(group_rows, shared_full, preferred_element_type=jnp.float32)
    step_values = jnp.dot(group_rows, step_full, preferred_element_type=jnp.float32)
    inner_conv, inner_pull = jax.vjp(conv_silu, inner_values, conv_inner, conv_inner_bias)
    shared_conv, shared_pull = jax.vjp(conv_silu, shared_values, conv_shared, conv_shared_bias)
    gated_rows, scan_pull = jax.vjp(
        gated_scan,
        rounded_copy(inner_conv),
        rounded_copy(shared_conv),
        gate_values,
        step_values,
        step_bias,
        decay_log,
        skip_gain,
    )
    squares = lax.psum(jnp.sum(gated_rows * gated_rows, axis=-1), "tensor")
    out_normed, out_pull = jax.vjp(out_norm, gated_rows, squares, out_gain)
    out_low = out_normed.astype(jnp.bfloat16)
    branch = lax.psum_scatter(
        jnp.dot(out_low, outward_full, preferred_element_type=jnp.float32),
        "tensor",
        scatter_dimension=0,
        tiled=True,
    )
    mixed_out = (token_rows + branch).astype(jnp.bfloat16)
    inward_full = fetch_inputs(gate_proj, inner_proj, shared_proj, step_proj)
    outward_full = fetch_output(out_proj)
    gate_full, inner_full, shared_full, step_full = inward_full
    cot_rows = lax.all_gather(cotangent, "tensor", axis=0, tiled=True)
    grad_out_proj = lax.psum_scatter(
        leading(out_low, cot_rows), "dp", scatter_dimension=1, tiled=True
    )
    grad_out_normed = transposed(cot_rows, outward_full)
    grad_gated, grad_squares, grad_out_gain = out_pull(grad_out_normed)
    grad_squares = lax.psum(grad_squares, "tensor")
    grad_gated = grad_gated + 2.0 * gated_rows * grad_squares[:, None]
    (
        grad_inner_conv,
        grad_shared_conv,
        grad_gate_values,
        grad_step_values,
        grad_step_bias,
        grad_decay_log,
        grad_skip_gain,
    ) = scan_pull(grad_gated)
    grad_inner_values, grad_conv_inner, grad_conv_inner_bias = inner_pull(grad_inner_conv)
    grad_shared_part, grad_conv_shared, grad_conv_shared_bias = shared_pull(grad_shared_conv)
    shared_back = lax.psum_scatter(
        grad_shared_part, "tensor", scatter_dimension=0, tiled=True
    ).astype(jnp.bfloat16)
    gate_back = grad_gate_values.astype(jnp.bfloat16)
    inner_back = grad_inner_values.astype(jnp.bfloat16)
    step_back = grad_step_values.astype(jnp.bfloat16)
    grad_normed = lax.psum_scatter(
        transposed(gate_back, gate_full)
        + transposed(inner_back, inner_full)
        + transposed(step_back, step_full),
        "tensor",
        scatter_dimension=0,
        tiled=True,
    ) + transposed(shared_back, shared_full)
    grad_gate_proj, grad_inner_proj, grad_shared_proj, grad_step_proj = (
        lax.psum_scatter(leading(group_rows, gate_back), "dp", scatter_dimension=0, tiled=True),
        lax.psum_scatter(leading(group_rows, inner_back), "dp", scatter_dimension=0, tiled=True),
        lax.psum_scatter(leading(normed_low, shared_back), "dp", scatter_dimension=0, tiled=True),
        lax.psum_scatter(leading(group_rows, step_back), "dp", scatter_dimension=0, tiled=True),
    )
    grad_token_rows, grad_norm_gain = norm_pull(grad_normed)
    grad_tokens = grad_token_rows + cotangent.astype(jnp.float32)
    (
        grad_conv_inner,
        grad_conv_inner_bias,
        grad_step_bias,
        grad_decay_log,
        grad_skip_gain,
        grad_out_gain,
        grad_conv_shared,
        grad_conv_shared_bias,
        grad_norm_gain,
    ) = lax.psum(
        (
            grad_conv_inner,
            grad_conv_inner_bias,
            grad_step_bias,
            grad_decay_log,
            grad_skip_gain,
            grad_out_gain,
            grad_conv_shared,
            grad_conv_shared_bias,
            grad_norm_gain,
        ),
        "dp",
    )
    grad_conv_shared, grad_conv_shared_bias, grad_norm_gain, grad_shared_proj = lax.psum(
        (grad_conv_shared, grad_conv_shared_bias, grad_norm_gain, grad_shared_proj), "tensor"
    )
    return (
        mixed_out,
        grad_tokens,
        grad_norm_gain,
        grad_gate_proj,
        grad_inner_proj,
        grad_shared_proj,
        grad_step_proj,
        grad_conv_inner,
        grad_conv_inner_bias,
        grad_conv_shared,
        grad_conv_shared_bias,
        grad_step_bias,
        grad_decay_log,
        grad_skip_gain,
        grad_out_gain,
        grad_out_proj,
    )


def solution(mesh):
    return jax.shard_map(
        local,
        mesh=mesh,
        in_specs=(
            P(("dp", "tensor"), None),
            P(),
            P("dp", "tensor"),
            P("dp", "tensor"),
            P("dp", None),
            P("dp", "tensor"),
            P(None, "tensor"),
            P("tensor"),
            P(),
            P(),
            P("tensor"),
            P("tensor"),
            P("tensor"),
            P("tensor"),
            P("tensor", "dp"),
            P(("dp", "tensor"), None),
        ),
        out_specs=(
            P(("dp", "tensor"), None),
            P(("dp", "tensor"), None),
            P(),
            P("dp", "tensor"),
            P("dp", "tensor"),
            P("dp", None),
            P("dp", "tensor"),
            P(None, "tensor"),
            P("tensor"),
            P(),
            P(),
            P("tensor"),
            P("tensor"),
            P("tensor"),
            P("tensor"),
            P("tensor", "dp"),
        ),
        check_vma=False,
    )
```

profile of v0, /device:TPU:0, one launch (start us, length us, event | category | flops | bytes accessed | tf_op | source)
XLA Modules:
  0.0 760.2 jit_solution(1551230992207926940)
XLA Ops:
  15.1 15.7 %all-gather = bf16[8,192,12]{1,2,0:T(8,128)(2,1)S(1)} all-gather(bf16[1,192,12]{1,2,0:T(8,128)(2,1)S(1)} %bitcast.338), channel_id=1, replica_groups=mesh['dp'=8,'tensor'=4] {'dp'}, dimensions={0}, use_global_device_ids=true | all-gather | bytes 41472 | tf_op jit(solution)/shard_map/all_gather | solution.py:93
  30.9 16.6 %all_gather.29 = bf16[1536,256]{1,0:T(8,128)(2,1)} all-gather(bf16[192,256]{1,0:T(8,128)(2,1)S(1)} %copy-done.37), channel_id=1, replica_groups=mesh['dp'=8,'tensor'=4] {'dp'}, dimensions={0}, use_global_device_ids=true | all-gather | bytes 884736 | tf_op jit(solution)/shard_map/all_gather | solution.py:92
  48.0 10.4 %all-gather.7.cloned.1.call-done = bf16[1024,1536]{1,0:T(8,128)(2,1)} async-done(((bf16[256,1536]{1,0:T(8,128)(2,1)}), bf16[1024,1536]{1,0:T(8,128)(2,1)}) %all-gather.7.cloned.1.call-update) | async-done | bytes 3145744 | tf_op jit(solution)/shard_map/all_gather | solution.py:138
  65.4 26.3 %all-gather.9.cloned.1.call-done = bf16[1536,768]{1,0:T(8,128)(2,1)} async-done(((bf16[192,768]{1,0:T(8,128)(2,1)}), bf16[1536,768]{1,0:T(8,128)(2,1)}) %all-gather.9.cloned.1.call-update) | async-done | bytes 2359312 | tf_op jit(solution)/shard_map/all_gather | solution.py:91
  127.0 14.3 %fusion.23 = f32[1,4,256,12,64]{2,4,3,1,0:T(8,128)S(1)} fusion(f32[4,256,12,64]{1,3,2,0:T(8,128)S(1)} %fusion.75, f32[1,4,256,12,64]{2,1,4,3,0:T(4,128)S(1)} %copy-done.15, f32[12]{0:T(128)S(1)} %copy-done.89, f32[4,256,12]{1,2,0:T(8,128)S(1)} %copy-done.35, f32[4,256,12]{1,2,0:T(8,128)S(1)} %copy-done.39, f32[4,256,256]{2,1,0:T(8,128)S(1)} %fusion.134, ...), kind=kOutput, calls=%fused_computation.35 | convolution fusion | flops 2429288448 | bytes 13844528 | tf_op jit(solution)/shard_map/jvp(sctuh,scuhp->scthp)/dot_general | solution.py:42
  149.3 9.1 %multiply_reduce_fusion.9 = (f32[1024]{0:T(1024)S(1)}, f32[1024,768]{1,0:T(8,128)}, f32[1024,768]{1,0:T(8,128)}) fusion(f32[1024,768]{1,0:T(8,128)} %copy.333, bf16[1024,1536]{1,0:T(8,128)(2,1)} %all-gather.7.cloned.1.call-done, bf16[1536,768]{1,0:T(8,128)(2,1)} %all-gather.11.cloned.1.call-done), kind=kOutput, calls=%fused_computation.54 | convolution fusion | flops 2421423104 | bytes 14946304 | tf_op jit(solution)/shard_map/dot_general | solution.py:142
  158.4 10.2 %psum.105 = f32[1024]{0:T(1024)S(1)} all-reduce(f32[1024]{0:T(1024)S(1)} %get-tuple-element.62), channel_id=1, replica_groups=mesh['dp'=8,'tensor'=4] {'tensor'}, use_global_device_ids=true, to_apply=%region_4.5 | all-reduce | flops 1024 | bytes 8192 | tf_op jit(solution)/shard_map/psum | solution.py:158
  168.6 32.6 %all-gather.15.cloned.1.call-done = bf16[1024,1536]{1,0:T(8,128)(2,1)} async-done(((bf16[256,1536]{1,0:T(8,128)(2,1)}), bf16[1024,1536]{1,0:T(8,128)(2,1)}) %all-gather.15.cloned.1.call-update) | async-done | bytes 3145744 | tf_op jit(solution)/shard_map/all_gather | solution.py:171
  201.2 8.5 %multiply_reduce_fusion = (f32[768]{0:T(1024)}, f32[1024]{0:T(1024)S(1)}, f32[1024,768]{1,0:T(8,128)}) fusion(f32[1024,768]{1,0:T(8,128)} %get-tuple-element.63, f32[1024]{0:T(1024)S(1)} %fusion.110, f32[768]{0:T(1024)} %param.29, bf16[1024,1536]{1,0:T(8,128)(2,1)} %all-gather.15.cloned.1.call-done, bf16[768,1536]{0,1:T(8,128)(2,1)} %all-gather.13.cloned.1.call-done), kind=kOutput, calls=%fused_computation.43 | convolution fusion | flops 2420635904 | bytes 11810816 | tf_op jit(solution)/shard_map/dot_general | solution.py:102
  209.7 8.9 %psum.106 = f32[1024]{0:T(1024)S(1)} all-reduce(f32[1024]{0:T(1024)S(1)} %multiply_multiply_fusion), channel_id=1, replica_groups=mesh['dp'=8,'tensor'=4] {'tensor'}, use_global_device_ids=true, to_apply=%region_7.8 | all-reduce | flops 1024 | bytes 8192 | tf_op jit(solution)/shard_map/psum | solution.py:177
  218.6 8.2 %multiply_reduce_fusion.1 = (f32[768]{0:T(1024)}, f32[1024,768]{1,0:T(8,128)}, bf16[1024,768]{1,0:T(8,128)(2,1)}) fusion(bf16[1024,768]{1,0:T(8,128)(2,1)} %get-tuple-element.69, f32[1024,768]{1,0:T(8,128)} %get-tuple-element.102, f32[1024,768]{1,0:T(8,128)} %get-tuple-element.63, f32[1024]{0:T(1024)S(1)} %broadcast_multiply_fusion.8, f32[1024]{0:T(1024)S(1)} %fusion.110, ...), kind=kLoop, calls=%fused_computation.44 | loop fusion | flops 15727872 | bytes 18888704 | tf_op jit(solution)/shard_map/transpose(jvp())/reduce_sum | solution.py:62
  235.5 8.4 %fusion.64 = f32[4,256,128]{2,1,0:T(8,128)} fusion(f32[4,256,12,64]{1,0,3,2:T(4,128)} %reshape.724, f32[4,256,12]{1,2,0:T(8,128)} %copy.329, f32[1,1,12,64,128]{4,3,2,1,0:T(8,128)} %copy-done.19, f32[1,1,12,64,128]{4,3,2,1,0:T(8,128)} %copy-done.20, f32[1,1,12,64,128]{4,3,2,1,0:T(8,128)} %copy-done.21, f32[4]{0:T(128)S(1)} %copy-done.86), kind=kOutput, calls=%fused_computation.109 | convolution fusion | flops 1209925632 | bytes 4898832 | tf_op jit(solution)/shard_map/transpose(jvp(sctn,schpn->scthp))/dot_general | solution.py:59
  253.6 21.6 %fusion.6 = (f32[4,256,12]{1,2,0:T(8,128)}, f32[4,256,12]{1,2,0:T(8,128)}, f32[4,256,256]{2,1,0:T(8,128)S(1)}) fusion(f32[4,256,12]{1,2,0:T(8,128)} %copy.323, f32[4,256,256]{2,1,0:T(8,128)} %copy-done.24, pred[256,256]{1,0:T(8,128)(4,1)} %iota_compare_fusion, f32[4,256,12,64]{1,0,3,2:T(4,128)} %reshape.710, f32[4,256,12]{1,2,0:T(8,128)S(1)} %copy.315, ...), kind=kOutput, calls=%fused_computation.10 | convolution fusion | flops 2444730368 | bytes 8650752 | tf_op jit(solution)/shard_map/transpose(jvp(sctuh,scuhp->scthp))/dot_general | solution.py:42
  292.0 15.7 %fusion.24 = (f32[4,256,12]{1,2,0:T(8,128)S(1)}, f32[4,256,12]{1,2,0:T(8,128)}, f32[1,4,256,12,64]{2,4,3,1,0:T(8,128)}) fusion(f32[4,12,64,256]{3,2,1,0:T(8,128)S(1)} %fusion.48, f32[1,4,256,12,64]{2,1,4,3,0:T(4,128)S(1)} %copy-done.16, f32[4,256,12]{1,2,0:T(8,128)S(1)} %copy.315, f32[1,4,256,12,64]{2,1,4,3,0:T(4,128)} %reshape.723, f32[12]{0:T(128)S(1)} %copy-done.90, ...), kind=kOutput, calls=%fused_computation.38 | convolution fusion | flops 2433196032 | bytes 17088560 | tf_op jit(solution)/shard_map/transpose(jvp(sctuh,scuhp->scthp))/dot_general | solution.py:42
  321.0 10.2 %reduce-window.16 = f32[1,4,12,2,128]{4,2,3,1,0:T(8,128)S(1)} reduce-window(f32[1,4,12,2,128]{4,2,3,1,0:T(8,128)S(1)} %copy.358, f32[]{:T(128)} %constant.22.clone.1), window={size=1x1x1x1x128 pad=0_0x0_0x0_0x0_0x0_127}, to_apply=%region_17.18 | reduce-window | flops 1560576 | bytes 98308 | tf_op jit(solution)/shard_map/reduce-window.2
  383.1 6.8 fusion.121
  407.0 55.8 %reduce-scatter.13.cloned.1.call-done = f32[256,1536]{1,0:T(8,128)} async-done(((f32[1024,1536]{1,0:T(8,128)}), f32[256,1536]{1,0:T(8,128)}) %reduce-scatter.13.cloned.1.call-update) | async-done | bytes 1572880 | tf_op jit(solution)/shard_map/reduce_scatter | solution.py:196
  465.2 29.6 %all-reduce.27 = (f32[1536]{0:T(1024)S(1)}, f32[4,768]{1,0:T(4,128)}, f32[768]{0:T(1024)}, f32[4,256]{1,0:T(4,128)S(1)}, f32[256]{0:T(256)S(1)}, /*index=5*/f32[...) all-reduce(f32[1536]{0:T(1024)S(1)} %get-tuple-element.30, ...), channel_id=1, replica_groups=mesh['dp'=8,'tensor'=4] {'dp'}, use_global_device_ids=true, to_apply=%region_24.25 | all-reduce | flops 7460 | bytes 59680 | tf_op jit(solution)/shard_map/psum | solution.py:222
  494.8 16.0 %all-reduce.28 = (f32[1536]{0:T(1024)}, f32[4,256]{1,0:T(4,128)}, f32[256]{0:T(256)}) all-reduce(f32[1536]{0:T(1024)S(1)} %get-tuple-element.42, f32[4,256]{1,0:T(4,128)S(1)} %get-tuple-element.45, f32[256]{0:T(256)S(1)} %get-tuple-element.46), channel_id=1, replica_groups=mesh['dp'=8,'tensor'=4] {'tensor'}, use_global_device_ids=true, to_apply=%region_25.26 | all-reduce | flops 2816 | bytes 22528 | tf_op jit(solution)/shard_map/psum | solution.py:236
  510.8 25.4 %reduce-scatter.11.cloned.1.call-done = f32[256,1536]{1,0:T(8,128)} async-done(((f32[1024,1536]{1,0:T(8,128)}), f32[256,1536]{1,0:T(8,128)}) %reduce-scatter.11.cloned.1.call-update) | async-done | bytes 1572880 | tf_op jit(solution)/shard_map/reduce_scatter | solution.py:161
  539.6 42.0 %all-reduce.31.cloned.1.call-done = f32[192,256]{1,0:T(8,128)} async-done(((f32[192,256]{1,0:T(8,128)}), f32[192,256]{1,0:T(8,128)}) %all-reduce.31.cloned.1.call-update) | async-done | bytes 196624 | tf_op jit(solution)/shard_map/psum | solution.py:236
  581.6 57.8 %reduce-scatter.23.cloned.1.call-done = f32[768,192]{0,1:T(8,128)} async-done(((f32[768,1536]{0,1:T(8,128)}), f32[768,192]{0,1:T(8,128)}) %reduce-scatter.23.cloned.1.call-update) | async-done | bytes 589840 | tf_op jit(solution)/shard_map/reduce_scatter | solution.py:172
  639.4 56.3 %reduce-scatter.17.cloned.1.call-done = f32[192,768]{1,0:T(8,128)} async-done(((f32[1536,768]{1,0:T(8,128)}), f32[192,768]{1,0:T(8,128)}) %reduce-scatter.17.cloned.1.call-update) | async-done | bytes 589840 | tf_op jit(solution)/shard_map/reduce_scatter | solution.py:205
  695.8 56.2 %reduce-scatter.19.cloned.1.call-done = f32[192,768]{1,0:T(8,128)} async-done(((f32[1536,768]{1,0:T(8,128)}), f32[192,768]{1,0:T(8,128)}) %reduce-scatter.19.cloned.1.call-update) | async-done | bytes 589840 | tf_op jit(solution)/shard_map/reduce_scatter | solution.py:206
  (336 shorter events, 182.3 us)
Async XLA Ops:
  7.2 51.1 %all-gather.7.cloned.1.call-start = ((), (), s32[]{:S(2)}) async-start(), calls=%async_computation.8 | async-start | bytes 3932160 | tf_op jit(solution)/shard_map/all_gather | solution.py:138
  11.6 80.1 %all-gather.9.cloned.1.call-start = ((), (), s32[]{:S(2)}) async-start(), calls=%async_computation.9 | async-start | bytes 2654208 | tf_op jit(solution)/shard_map/all_gather | solution.py:91
  12.3 137.0 %all-gather.11.cloned.1.call-start = ((), (), s32[]{:S(2)}) async-start(), calls=%async_computation.10 | async-start | bytes 2654208 | tf_op jit(solution)/shard_map/all_gather | solution.py:90
  13.0 155.6 %all-gather.13.cloned.1.call-start = ((), (), s32[]{:S(2)}) async-start(), calls=%async_computation.11 | async-start | bytes 2654208 | tf_op jit(solution)/shard_map/all_gather | solution.py:98
  13.6 187.6 %all-gather.15.cloned.1.call-start = ((), (), s32[]{:S(2)}) async-start(), calls=%async_computation.13 | async-start | bytes 3932160 | tf_op jit(solution)/shard_map/all_gather | solution.py:171
  14.2 302.7 %reduce-scatter.15.cloned.1.call-start = ((), (), s32[]{:S(2)}) async-start(), calls=%async_computation.15 | async-start | bytes 1310720 | tf_op jit(solution)/shard_map/reduce_scatter | solution.py:190
  14.9 104.4 %copy-start.58 = (f32[1,256]{1,0:T(1,128)}, f32[1,256]{1,0:T(1,128)S(1)}, u32[]{:S(2)}) copy-start(f32[1,256]{1,0:T(1,128)S(1)} %get-tuple-element.92) | copy-start | bytes 3076
  15.0 104.4 %copy-start.60 = (f32[1,256]{1,0:T(1,128)}, f32[1,256]{1,0:T(1,128)S(1)}, u32[]{:S(2)}) copy-start(f32[1,256]{1,0:T(1,128)S(1)} %get-tuple-element.93) | copy-start | bytes 3076
  15.0 81.9 %copy-start.44 = (f32[768]{0:T(1024)}, f32[768]{0:T(1024)S(1)}, u32[]{:S(2)}) copy-start(f32[768]{0:T(1024)S(1)} %get-tuple-element.38) | copy-start | bytes 9220
  15.0 81.9 %copy-start.46 = (f32[768]{0:T(1024)}, f32[768]{0:T(1024)S(1)}, u32[]{:S(2)}) copy-start(f32[768]{0:T(1024)S(1)} %get-tuple-element.39) | copy-start | bytes 9220
  15.0 81.9 %copy-start.48 = (f32[768]{0:T(1024)}, f32[768]{0:T(1024)S(1)}, u32[]{:S(2)}) copy-start(f32[768]{0:T(1024)S(1)} %get-tuple-element.40) | copy-start | bytes 9220
  15.0 81.9 %copy-start.50 = (f32[768]{0:T(1024)}, f32[768]{0:T(1024)S(1)}, u32[]{:S(2)}) copy-start(f32[768]{0:T(1024)S(1)} %get-tuple-element.41) | copy-start | bytes 9220
  289.0 93.3 %reduce-scatter.21.cloned.1.call-start = ((), (), s32[]{:S(2)}) async-start(), calls=%async_computation.18 | async-start | bytes 1769472 | tf_op jit(solution)/shard_map/reduce_scatter | solution.py:207
  319.7 85.7 %reduce-scatter.25.cloned.1.call-start = ((), (), s32[]{:S(2)}) async-start(), calls=%async_computation.21 | async-start | bytes 884736
  359.8 103.0 %reduce-scatter.13.cloned.1.call-start = ((), (), s32[]{:S(2)}) async-start(), calls=%async_computation.14 | async-start | bytes 7864320 | tf_op jit(solution)/shard_map/reduce_scatter | solution.py:196
  374.0 162.2 %reduce-scatter.11.cloned.1.call-start = ((), (), s32[]{:S(2)}) async-start(), calls=%async_computation.12 | async-start | bytes 7864320 | tf_op jit(solution)/shard_map/reduce_scatter | solution.py:161
  382.3 199.3 %all-reduce.31.cloned.1.call-start = ((), (), s32[]{:S(2)}) async-start(), calls=%async_computation.19 | async-start | bytes 393216 | tf_op jit(solution)/shard_map/psum | solution.py:236
  383.0 256.4 %reduce-scatter.23.cloned.1.call-start = ((), (), s32[]{:S(2)}) async-start(), calls=%async_computation.20 | async-start | bytes 5308416 | tf_op jit(solution)/shard_map/reduce_scatter | solution.py:172
  389.9 305.9 %reduce-scatter.17.cloned.1.call-start = ((), (), s32[]{:S(2)}) async-start(), calls=%async_computation.16 | async-start | bytes 5308416 | tf_op jit(solution)/shard_map/reduce_scatter | solution.py:205
  397.6 354.4 %reduce-scatter.19.cloned.1.call-start = ((), (), s32[]{:S(2)}) async-start(), calls=%async_computation.17 | async-start | bytes 5308416 | tf_op jit(solution)/shard_map/reduce_scatter | solution.py:206
  404.5 60.7 %copy-start.73 = (f32[256]{0:T(256)S(1)}, f32[256]{0:T(256)}, u32[]{:S(2)}) copy-start(f32[256]{0:T(256)} %get-tuple-element.36) | copy-start | bytes 3076
  404.5 60.7 %copy-start.78 = (f32[768]{0:T(1024)S(1)}, f32[768]{0:T(1024)}, u32[]{:S(2)}) copy-start(f32[768]{0:T(1024)} %get-tuple-element.19) | copy-start | bytes 9220
  404.5 106.3 %copy-start.63 = (f32[256]{0:T(256)S(1)}, f32[256]{0:T(256)}, u32[]{:S(2)}) copy-start(f32[256]{0:T(256)} %copy-done.62) | copy-start | bytes 3076
  404.5 131.7 %copy-start.14 = (bf16[256,1536]{1,0:T(8,128)(2,1)S(1)}, bf16[256,1536]{1,0:T(8,128)(2,1)}, u32[]{:S(2)}) copy-start(bf16[256,1536]{1,0:T(8,128)(2,1)} %param.31) | copy-start | bytes 2359300
  (83 other events, 907.3 us)
Sparse Core Ops, SparseCore 0:
  11.7 46.6 all-gather.6
  60.0 31.6 all-gather.8
  93.3 30.7 all-gather.10
  125.6 30.6 all-gather.12
  158.1 43.0 all-gather.14
  289.2 27.7 reduce-scatter.14
  319.8 34.0 reduce-scatter.20
  359.9 31.4 reduce-scatter.24
  394.3 68.3 reduce-scatter.12
  465.6 70.5 reduce-scatter.10
  539.1 42.4 all-reduce.30
  584.4 54.9 reduce-scatter.22
  642.4 53.3 reduce-scatter.16
  698.6 53.2 reduce-scatter.18
where the time goes:
time: 767 us; the launch traced here: 760 us
  waiting for transfers between devices  369 us (48%)
  matrix products  147 us (19%)
  blocking collectives  97 us (13%)
  local copies, waits for them, and re-layouts  66.7 us (9%)
  other arithmetic  63.2 us (8%)
  between operations  15.5 us (2%)
    reduce_scatter x1, waiting for transfers between devices, local(): lax.psum_scatter(leading(out_low, cot_rows), 'dp', scatter_dimension=1, t...  57.8 us
    reduce_scatter x1, waiting for transfers between devices, local(): lax.psum_scatter(leading(group_rows, gate_back), 'dp', scatter_dimension=...  56.3 us
    reduce_scatter x1, waiting for transfers between devices, local(): lax.psum_scatter(leading(group_rows, inner_back), 'dp', scatter_dimension...  56.2 us
    reduce_scatter x1, waiting for transfers between devices, local(): lax.psum_scatter(transposed(gate_back, gate_full) + transposed(inner_back...  55.8 us
    dot_general x3, matrix products, scan_heads(): jnp.einsum('sctuh,scuhp->scthp', scores[..., None] * kernel, weighted, pr...  51.5 us
    psum x1, waiting for transfers between devices, local(): lax.psum((grad_conv_shared, grad_conv_shared_bias, grad_norm_gain, grad_s...  42 us
    all_gather x1, waiting for transfers between devices, local(): cot_rows = lax.all_gather(cotangent, 'tensor', axis=0, tiled=True)  32.6 us
    psum x1, blocking collectives, local(): lax.psum((grad_conv_inner, grad_conv_inner_bias, grad_step_bias, grad_dec...  29.6 us
  transfers between devices with their start and end apart: 14, of which 10 were waited for; matrix products, arithmetic and copies ran while one was open for 24% of the time, Pallas kernels for 0%

commit v1 on v0

v1 whole, which is shorter than its diff:
```python
import jax
import jax.numpy as jnp
from jax import lax
from jax.sharding import PartitionSpec as P

HEAD_DIM = 64
STATE = 128
CONV = 4
SPAN = 256
SEQ = 1024
DI = 3072


epsilon = 1e-05
highest = lax.Precision.HIGHEST
f32 = jnp.float32
bf16 = jnp.bfloat16


def conv_silu(values, weight, conv_bias):
    channels = values.shape[-1]
    blocks = values.reshape(-1, SEQ, channels)
    padded = jnp.pad(blocks, ((0, 0), (CONV - 1, 0), (0, 0)))
    summed = conv_bias + weight[0] * padded[:, 0:SEQ]
    for offset in range(1, CONV):
        summed = summed + weight[offset] * padded[:, offset : offset + SEQ]
    return jax.nn.silu(summed).reshape(-1, channels)


def scan_heads(values, step_sizes, decay_rates, write_state, read_state, skip_gain):
    head_count = step_sizes.shape[-1]
    spans = SEQ // SPAN
    shaped = values.reshape(-1, spans, SPAN, head_count, HEAD_DIM)
    step_blocks = step_sizes.reshape(-1, spans, SPAN, head_count)
    write_blocks = write_state.reshape(-1, spans, SPAN, STATE)
    read_blocks = read_state.reshape(-1, spans, SPAN, STATE)
    cumulated = jnp.cumsum(step_blocks * decay_rates, axis=2)
    places = jnp.arange(SPAN)
    causal = (places[:, None] >= places[None, :])[None, None, :, :, None]
    log_gaps = cumulated[:, :, :, None, :] - cumulated[:, :, None, :, :]
    kernel = jnp.exp(jnp.where(causal, log_gaps, -1e30))
    scores = jnp.einsum("sctn,scun->sctu", read_blocks, write_blocks, precision=highest)
    weighted = shaped * step_blocks[..., None]
    within = jnp.einsum(
        "sctuh,scuhp->scthp", scores[..., None] * kernel, weighted, precision=highest
    )
    final_log = cumulated[:, :, -1, :]
    tail_decay = jnp.exp(final_log[:, :, None, :] - cumulated)
    states = jnp.einsum(
        "scuhp,scun->schpn", tail_decay[..., None] * weighted, write_blocks, precision=highest
    )
    carried = jnp.zeros_like(states[:, 0])
    entering = []
    for span_index in range(spans):
        entering.append(carried)
        carried = (
            jnp.exp(final_log[:, span_index])[:, :, None, None] * carried + states[:, span_index]
        )
    entering = jnp.stack(entering, axis=1)
    across = (
        jnp.einsum("sctn,schpn->scthp", read_blocks, entering, precision=highest)
        * jnp.exp(cumulated)[..., None]
    )
    result = within + across + skip_gain[:, None] * shaped
    return result.reshape(values.shape)


def gated_scan(inner_conv, shared_conv, gate_values, step_values, step_bias, decay_log, skip_gain):
    step_sizes = jax.nn.softplus(step_values + step_bias)
    scanned = scan_heads(
        inner_conv,
        step_sizes,
        -jnp.exp(decay_log),
        shared_conv[:, :STATE],
        shared_conv[:, STATE:],
        skip_gain,
    )
    return scanned * jax.nn.silu(gate_values)


def transposed(first_operand, second_operand):
    return lax.dot_general(
        first_operand, second_operand, (((1,), (1,)), ((), ())), preferred_element_type=f32
    )


def leading(first_operand, second_operand):
    return lax.dot_general(
        first_operand, second_operand, (((0,), (0,)), ((), ())), preferred_element_type=f32
    )


def plain(first_operand, second_operand):
    return jnp.dot(first_operand, second_operand, preferred_element_type=f32)


def rounded_copy(values):
    return lax.optimization_barrier(values.astype(bf16)).astype(f32)


def flip(values, count, axis, me):
    shape = values.shape
    width = shape[axis] // count
    bit = 1
    while bit < count:
        split = shape[:axis] + (count // (2 * bit), 2, bit * width) + shape[axis + 1 :]
        parts = values.reshape(split)
        first = lax.index_in_dim(parts, 0, axis + 1, keepdims=True)
        second = lax.index_in_dim(parts, 1, axis + 1, keepdims=True)
        swapped = lax.concatenate([second, first], axis + 1).reshape(shape)
        values = jnp.where((me & bit) != 0, swapped, values)
        bit *= 2
    return values


class Net:
    def __init__(self, dp, tensor):
        self.dp, self.tensor = dp, tensor
        self.chips = dp // 2
        self.place = lax.axis_index("dp")
        self.chip, self.core = self.place // 2, self.place % 2
        self.rank = lax.axis_index("tensor")

    def over_chips(self, values, k):
        return lax.ppermute(values, "dp", [(i, i ^ (2 * k)) for i in range(self.dp)])

    def over_core(self, values):
        return lax.ppermute(values, "dp", [(i, i ^ 1) for i in range(self.dp)])

    def over_tensor(self, values, k):
        return lax.ppermute(values, "tensor", [(i, i ^ k) for i in range(self.tensor)])

    def gather_dp(self, shard):
        mine = jnp.stack([shard] + [self.over_chips(shard, k) for k in range(1, self.chips)])
        other = self.over_core(mine)
        first = jnp.where(self.core == 0, mine, other)
        second = jnp.where(self.core == 0, other, mine)
        return jnp.stack([first, second], axis=1).reshape((-1,) + shard.shape[1:])

    def scatter_dp(self, values):
        split = values.reshape((self.chips, 2, -1) + values.shape[1:])
        keep = jnp.where(self.core == 0, split[:, 0], split[:, 1])
        give = jnp.where(self.core == 0, split[:, 1], split[:, 0]).astype(bf16)
        pair = keep + self.over_core(give).astype(f32)
        total = pair[0]
        for k in range(1, self.chips):
            total = total + self.over_chips(pair[k].astype(bf16), k).astype(f32)
        return total

    def gather_tensor(self, shard):
        if self.tensor != 4:
            return lax.all_gather(shard, "tensor", axis=0, tiled=True)
        half = shard.shape[0] // 2
        one, two = self.over_tensor(shard, 1), self.over_tensor(shard, 2)
        last = [self.over_tensor(one[:half], 2), self.over_tensor(two[half:], 1)]
        stacked = jnp.concatenate([shard, one, two] + last)
        return flip(stacked, 4, 0, self.rank)

    def scatter_tensor(self, values):
        if self.tensor != 4:
            low = values.astype(bf16)
            return lax.psum_scatter(low, "tensor", scatter_dimension=0, tiled=True).astype(f32)
        own, one, two, last = jnp.split(flip(values, 4, 0, self.rank), 4)
        half = own.shape[0] // 2
        low = last.astype(bf16)
        to_one = self.over_tensor(low[:half], 2).astype(f32)
        to_two = self.over_tensor(low[half:], 1).astype(f32)
        one = jnp.concatenate([one[:half] + to_one, one[half:]]).astype(bf16)
        two = jnp.concatenate([two[:half], two[half:] + to_two]).astype(bf16)
        return own + self.over_tensor(one, 1).astype(f32) + self.over_tensor(two, 2).astype(f32)

    def sum_tensor(self, values):
        total = values
        for k in range(1, self.tensor):
            total = total + self.over_tensor(values, k)
        return total

    def sum_dp(self, values):
        pair = values + self.over_core(values)
        total = pair
        for k in range(1, self.chips):
            total = total + self.over_chips(pair, k)
        return total


def local(
    net_of,
    tokens,
    norm_gain,
    gate_proj,
    inner_proj,
    shared_proj,
    step_proj,
    conv_inner,
    conv_inner_bias,
    conv_shared,
    conv_shared_bias,
    step_bias,
    decay_log,
    skip_gain,
    out_gain,
    out_proj,
    cotangent,
):
    net = net_of()
    channels = gate_proj.shape[1]
    heads = step_proj.shape[1]
    tokens_here = flip(tokens, net.chips, 1, net.chip)
    cot_here = flip(cotangent, net.chips, 1, net.chip)
    gain_here = flip(norm_gain, net.chips, 0, net.chip)
    token_rows = tokens_here.astype(f32)
    inverse = lax.rsqrt(jnp.mean(token_rows * token_rows, axis=-1, keepdims=True) + epsilon)
    unit = token_rows * inverse
    normed_low = (unit * gain_here).astype(bf16)
    padding = jnp.zeros((step_proj.shape[0], 128 - heads), bf16)
    scan_shard = jnp.concatenate([inner_proj, shared_proj, step_proj, padding], axis=1)
    rows = net.gather_tensor(normed_low)
    scan_full = net.gather_dp(scan_shard)
    gate_full = net.gather_dp(gate_proj)
    outward_full = net.gather_dp(out_proj.T)
    cot_rows = net.gather_tensor(cot_here)

    scan_values = plain(rows, scan_full)
    inner_values = scan_values[:, :channels]
    shared_values = scan_values[:, channels : channels + 2 * STATE]
    step_values = scan_values[:, channels + 2 * STATE : channels + 2 * STATE + heads]
    gate_values = plain(rows, gate_full)
    inner_conv, inner_pull = jax.vjp(conv_silu, inner_values, conv_inner, conv_inner_bias)
    shared_conv, shared_pull = jax.vjp(conv_silu, shared_values, conv_shared, conv_shared_bias)
    gated_rows, scan_pull = jax.vjp(
        gated_scan,
        rounded_copy(inner_conv),
        rounded_copy(shared_conv),
        gate_values,
        step_values,
        step_bias,
        decay_log,
        skip_gain,
    )
    grad_out = plain(cot_rows, outward_full)
    scaled = out_gain * grad_out
    sums = jnp.stack([jnp.sum(gated_rows * gated_rows, -1), jnp.sum(scaled * gated_rows, -1)])
    squares, dots = net.sum_tensor(sums)
    ratio = lax.rsqrt(squares / DI + epsilon)
    out_low = (out_gain * (gated_rows * ratio[:, None])).astype(bf16)
    branch = net.scatter_tensor(transposed(out_low, outward_full))
    mixed = flip((token_rows + branch).astype(bf16), net.chips, 1, net.chip)
    grad_out_proj = net.scatter_dp(leading(cot_rows, out_low)).T
    grad_out_gain = jnp.sum(grad_out * gated_rows * ratio[:, None], axis=0)
    grad_gated = scaled * ratio[:, None] - gated_rows * (ratio**3 / DI * dots)[:, None]
    (
        grad_inner_conv,
        grad_shared_conv,
        grad_gate_values,
        grad_step_values,
        grad_step_bias,
        grad_decay_log,
        grad_skip_gain,
    ) = scan_pull(grad_gated)
    grad_inner_values, grad_conv_inner, grad_conv_inner_bias = inner_pull(grad_inner_conv)
    grad_shared_values, grad_conv_shared, grad_conv_shared_bias = shared_pull(grad_shared_conv)
    gate_back = grad_gate_values.astype(bf16)
    scan_back = jnp.concatenate(
        [
            grad_inner_values.astype(bf16),
            grad_shared_values.astype(bf16),
            grad_step_values.astype(bf16),
            jnp.zeros((grad_step_values.shape[0], 128 - heads), bf16),
        ],
        axis=1,
    )
    grad_normed = net.scatter_tensor(
        transposed(gate_back, gate_full) + transposed(scan_back, scan_full)
    )
    gate_partial = leading(rows, gate_back)
    scan_partial = leading(rows, scan_back)
    grad_gate_proj = net.scatter_dp(gate_partial)
    grad_scan_proj = net.scatter_dp(scan_partial)
    grad_inner_proj = grad_scan_proj[:, :channels]
    grad_shared_proj = net.sum_tensor(grad_scan_proj[:, channels : channels + 2 * STATE])
    grad_step_proj = grad_scan_proj[:, channels + 2 * STATE : channels + 2 * STATE + heads]
    grad_gain_here = (
        jnp.sum(gate_full.astype(f32) * gate_partial, axis=1)
        + jnp.sum(scan_full.astype(f32) * scan_partial, axis=1)
    ) / gain_here
    grad_norm_gain = flip(grad_gain_here, net.chips, 0, net.chip)
    spread = grad_normed * gain_here
    grad_token_rows = (
        cot_here.astype(f32)
        + inverse * spread
        - unit * (inverse * jnp.mean(spread * unit, axis=-1, keepdims=True))
    )
    grad_tokens = flip(grad_token_rows, net.chips, 1, net.chip)
    own = (
        grad_conv_inner,
        grad_conv_inner_bias,
        grad_out_gain,
        grad_step_bias,
        grad_decay_log,
        grad_skip_gain,
    )
    common = (grad_conv_shared, grad_conv_shared_bias, grad_norm_gain)
    common_flat = net.sum_tensor(jnp.concatenate([v.reshape(-1) for v in common]))
    flat = net.sum_dp(jnp.concatenate([v.reshape(-1) for v in own] + [common_flat]))
    small = []
    start = 0
    for v in own + common:
        small.append(flat[start : start + v.size].reshape(v.shape))
        start += v.size
    (
        grad_conv_inner,
        grad_conv_inner_bias,
        grad_out_gain,
        grad_step_bias,
        grad_decay_log,
        grad_skip_gain,
        grad_conv_shared,
        grad_conv_shared_bias,
        grad_norm_gain,
    ) = small
    return (
        mixed,
        grad_tokens,
        grad_norm_gain,
        grad_gate_proj,
        grad_inner_proj,
        grad_shared_proj,
        grad_step_proj,
        grad_conv_inner,
        grad_conv_inner_bias,
        grad_conv_shared,
        grad_conv_shared_bias,
        grad_step_bias,
        grad_decay_log,
        grad_skip_gain,
        grad_out_gain,
        grad_out_proj,
    )


def solution(mesh):
    dp, tensor = mesh.shape["dp"], mesh.shape["tensor"]

    def on_device(*args):
        return local(lambda: Net(dp, tensor), *args)

    return jax.shard_map(
        on_device,
        mesh=mesh,
        in_specs=(
            P(("dp", "tensor"), None),
            P(),
            P("dp", "tensor"),
            P("dp", "tensor"),
            P("dp", None),
            P("dp", "tensor"),
            P(None, "tensor"),
            P("tensor"),
            P(),
            P(),
            P("tensor"),
            P("tensor"),
            P("tensor"),
            P("tensor"),
            P("tensor", "dp"),
            P(("dp", "tensor"), None),
        ),
        out_specs=(
            P(("dp", "tensor"), None),
            P(("dp", "tensor"), None),
            P(),
            P("dp", "tensor"),
            P("dp", "tensor"),
            P("dp", None),
            P("dp", "tensor"),
            P(None, "tensor"),
            P("tensor"),
            P(),
            P(),
            P("tensor"),
            P("tensor"),
            P("tensor"),
            P("tensor"),
            P("tensor", "dp"),
        ),
        check_vma=False,
    )
```

time: 767 us -> 603 us (0.79)
  waiting for transfers between devices: 369 us -> 142 us
  blocking collectives: 97 us -> 0 us
  other arithmetic: 63.2 us -> 137 us
  starting transfers between devices: 1.38 us -> 66 us
  local copies, waits for them, and re-layouts: 66.7 us -> 121 us
  matrix products: 147 us -> 131 us
  between operations: 15.5 us -> 3.36 us
    reduce_scatter x7 -> x0, waiting for transfers between devices: 255 us -> none  [the longest x1 57.8 us: local(): lax.psum_scatter(leading(out_low, cot_rows), 'dp', scatter_dimension=1, t...]
    ppermute x0 -> x53, waiting for transfers between devices: none -> 142 us  [the longest x21 95 us: over_chips(): return lax.ppermute(values, 'dp', [(i, i ^ 2 * k) for i in range(self.dp)])]
    all_gather x5 -> x0, waiting for transfers between devices: 69.3 us -> none  [the longest x1 32.6 us: local(): cot_rows = lax.all_gather(cotangent, 'tensor', axis=0, tiled=True)]
    ppermute x0 -> x53, starting transfers between devices: none -> 66 us  [the longest x21 32.5 us: over_chips(): return lax.ppermute(values, 'dp', [(i, i ^ 2 * k) for i in range(self.dp)])]
    psum x4 -> x0, blocking collectives: 64.7 us -> none  [the longest x1 29.6 us: local(): lax.psum((grad_conv_inner, grad_conv_inner_bias, grad_step_bias, grad_dec...]
    psum x1 -> x0, waiting for transfers between devices: 42 us -> none  [local(): lax.psum((grad_conv_shared, grad_conv_shared_bias, grad_norm_gain, grad_s...]
    all_gather x2 -> x0, blocking collectives: 32.3 us -> none  [the longest x1 16.6 us: fetch_inputs(): lax.all_gather(shared_proj, 'dp', axis=0, tiled=True)]
    another operation x5 -> x23, other arithmetic: 13.5 us -> 45.7 us
  transfers between devices with their start and end apart: 14 -> 53, of which waited for: 10 -> 16; matrix products, arithmetic and copies ran while one was open for 24% -> 27% of each run, Pallas kernels for 0% -> 0%
where the time goes in v1:
time: 603 us; the launch traced here: 599 us
  waiting for transfers between devices  142 us (24%)
  other arithmetic  137 us (23%)
  matrix products  131 us (22%)
  local copies, waits for them, and re-layouts  121 us (20%)
  starting transfers between devices  66 us (11%)
    ppermute x21, waiting for transfers between devices, over_chips(): return lax.ppermute(values, 'dp', [(i, i ^ 2 * k) for i in range(self.dp)])  95 us
    dot_general x3, matrix products, scan_heads(): jnp.einsum('sctuh,scuhp->scthp', scores[..., None] * kernel, weighted, pr...  51.4 us
    ppermute x25, waiting for transfers between devices, over_tensor(): lax.ppermute(values, 'tensor', [(i, i ^ k) for i in range(self.tensor)])  46.7 us
    another operation x12, other arithmetic  34.2 us
    ppermute x21, starting transfers between devices, over_chips(): return lax.ppermute(values, 'dp', [(i, i ^ 2 * k) for i in range(self.dp)])  32.5 us
    ppermute x25, starting transfers between devices, over_tensor(): lax.ppermute(values, 'tensor', [(i, i ^ k) for i in range(self.tensor)])  32.3 us
    dot_general x3, matrix products, leading(): lax.dot_general(first_operand, second_operand, (((0,), (0,)), ((), ())),...  20.4 us
    concatenate x20, other arithmetic, flip(): swapped = lax.concatenate([second, first], axis + 1).reshape(shape)  20.1 us
  transfers between devices with their start and end apart: 53, of which 16 were waited for; matrix products, arithmetic and copies ran while one was open for 27% of the time, Pallas kernels for 0%

profile of v1, /device:TPU:0, one launch (start us, length us, event | category | flops | bytes accessed | tf_op | source)
XLA Modules:
  0.0 599.3 jit_solution(10038452411887198337)
XLA Ops:
  45.4 30.7 %collective-permute-done.9 = bf16[192,768]{1,0:T(8,128)(2,1)S(1)} collective-permute-done((bf16[192,768]{1,0:T(8,128)(2,1)S(1)}, bf16[192,768]{1,0:T(8,128)(2,1)S(1)}, u32[]{:S(2)}, u32[]{:S(2)}) %collective-permute-start.9) | collective-permute-done | bytes 294944 | tf_op jit(solution)/shard_map/ppermute | solution.py:125
  84.1 10.2 %collective-permute-done.5 = bf16[192,1152]{1,0:T(8,128)(2,1)} collective-permute-done((bf16[192,1152]{1,0:T(8,128)(2,1)}, bf16[192,1152]{1,0:T(8,128)(2,1)}, u32[]{:S(2)}, u32[]{:S(2)}) %collective-permute-start.5) | collective-permute-done | bytes 442400 | tf_op jit(solution)/shard_map/ppermute | solution.py:125
  104.1 10.9 %collective-permute-done = bf16[256,1536]{1,0:T(8,128)(2,1)S(1)} collective-permute-done((bf16[256,1536]{1,0:T(8,128)(2,1)}, bf16[256,1536]{1,0:T(8,128)(2,1)S(1)}, u32[]{:S(2)}, u32[]{:S(2)}) %collective-permute-start) | collective-permute-done | bytes 786464 | tf_op jit(solution)/shard_map/ppermute | solution.py:131
  117.8 5.0 collective-permute-done.14
  174.6 5.1 reshape.1034
  179.7 5.3 reshape.1045
  198.7 14.5 %fusion.23 = f32[1,4,256,12,64]{2,4,3,1,0:T(8,128)S(1)} fusion(f32[4,256,12,64]{1,3,2,0:T(8,128)S(1)} %fusion.85, f32[1,4,256,12,64]{2,1,4,3,0:T(4,128)S(1)} %copy-done.36, f32[12]{0:T(128)S(1)} %copy-done.119, f32[4,256,12]{1,2,0:T(8,128)S(1)} %copy-done.69, f32[4,256,12]{1,2,0:T(8,128)S(1)} %copy-done.76, f32[4,256,256]{2,1,0:T(8,128)S(1)} %fusion.186, ...), kind=kOutput, calls=%fused_computation.54 | convolution fusion | flops 2429288448 | bytes 13844528 | tf_op jit(solution)/shard_map/jvp(sctuh,scuhp->scthp)/dot_general | solution.py:44
  221.2 10.0 %multiply_reduce_fusion.11 = (f32[1024]{0:T(1024)S(1)}, f32[1024]{0:T(1024)S(1)}, f32[1024,768]{1,0:T(8,128)}, f32[1024,768]{1,0:T(8,128)}) fusion(f32[768]{0:T(1024)} %param.29, f32[1024,768]{1,0:T(8,128)} %copy.433, f32[1024,768]{1,0:T(8,128)} %fusion.187, bf16[1024,1536]{1,0:T(8,128)(2,1)} %bitcast.551, bf16[1536,768]{1,0:T(8,128)(2,1)} %bitcast.557), kind=kOutput, calls=%fused_computation.77 | convolution fusion | flops 2423781376 | bytes 18099200 | tf_op jit(solution)/shard_map/dot_general | solution.py:94
  237.8 5.0 copy.473
  243.7 6.5 %fusion.143 = f32[1024,1536]{1,0:T(8,128)} fusion(bf16[1536,768]{1,0:T(8,128)(2,1)} %bitcast.558, f32[1024,768]{1,0:T(8,128)S(1)} %copy-done.40, f32[1024]{0:T(1024)S(1)} %bitcast.576, f32[768]{0:T(1024)} %param.29), kind=kOutput, calls=%fused_computation.348 | convolution fusion | flops 2418278400 | bytes 11803648 | tf_op jit(solution)/shard_map/dot_general | solution.py:82
  250.2 4.8 multiply_reduce_fusion.2
  264.9 6.1 %fusion.74 = f32[4,256,128]{2,1,0:T(8,128)} fusion(f32[4,256,12,64]{1,0,3,2:T(4,128)S(1)} %copy-done.5, f32[4,256,12]{1,2,0:T(8,128)S(1)} %copy-done.70, f32[1,1,12,64,128]{4,3,2,1,0:T(8,128)S(1)} %copy-done.48, f32[1,1,12,64,128]{4,3,2,1,0:T(8,128)S(1)} %copy-done.50, f32[1,1,12,64,128]{4,3,2,1,0:T(8,128)S(1)} %copy-done.52, f32[4]{0:T(128)S(1)} %copy-done.118), kind=kOutput, calls=%fused_computation.159 | convolution fusion | flops 1209925632 | bytes 4898832 | tf_op jit(solution)/shard_map/transpose(jvp(sctn,schpn->scthp))/dot_general | solution.py:61
  277.9 21.6 %fusion.6 = (f32[4,256,12]{1,2,0:T(8,128)S(1)}, f32[4,256,12]{1,2,0:T(8,128)}, f32[4,256,256]{2,1,0:T(8,128)S(1)}) fusion(f32[4,256,256]{2,1,0:T(8,128)} %copy-done.60, f32[4,256,12]{1,2,0:T(8,128)} %copy.422, pred[256,256]{1,0:T(8,128)(4,1)} %iota_compare_fusion, f32[4,256,12,64]{1,0,3,2:T(4,128)} %reshape.1034, f32[4,256,12]{1,2,0:T(8,128)} %copy.413, ...), kind=kOutput, calls=%fused_computation.10 | convolution fusion | flops 2444730368 | bytes 8650752 | tf_op jit(solution)/shard_map/transpose(jvp(sctuh,scuhp->scthp))/dot_general | solution.py:44
  314.2 15.3 %fusion.26 = (f32[4,256,12]{1,2,0:T(8,128)S(1)}, f32[4,256,12]{1,2,0:T(8,128)S(1)}, f32[1,4,256,12,64]{2,4,3,1,0:T(8,128)}) fusion(f32[4,12,64,256]{3,2,1,0:T(8,128)} %fusion.58, f32[1,4,256,12,64]{2,1,4,3,0:T(4,128)S(1)} %copy-done.37, f32[4,256,12]{1,2,0:T(8,128)S(1)} %copy-done.64, f32[1,4,256,12,64]{2,1,4,3,0:T(4,128)} %reshape.1063, ...), kind=kOutput, calls=%fused_computation.61 | convolution fusion | flops 2433196032 | bytes 17088560 | tf_op jit(solution)/shard_map/transpose(jvp(sctuh,scuhp->scthp))/dot_general | solution.py:44
  330.2 10.1 %reduce-window.16 = f32[1,4,12,2,128]{4,2,3,1,0:T(8,128)S(1)} reduce-window(f32[1,4,12,2,128]{4,2,3,1,0:T(8,128)S(1)} %copy.462, f32[]{:T(128)} %constant.72.clone.1), window={size=1x1x1x1x128 pad=0_0x0_0x0_0x0_0x0_127}, to_apply=%region_15.16 | reduce-window | flops 1560576 | bytes 98308 | tf_op jit(solution)/shard_map/reduce-window.2
  372.3 11.1 %multiply_reduce_fusion = (f32[1536]{0:T(1024)S(1)}, f32[1536,1152]{1,0:T(8,128)}) fusion(bf16[4,2,192,1152]{3,2,1,0:T(8,128)(2,1)} %copy-done.28, bf16[1024,1536]{1,0:T(8,128)(2,1)} %fusion.25, bf16[1024,1152]{1,0:T(8,128)(2,1)} %concatenate.131), kind=kOutput, calls=%fused_computation.11 | convolution fusion | flops 3629185536 | bytes 16128000 | tf_op jit(solution)/shard_map/dot_general | solution.py:88
  387.1 4.8 fusion.55
  400.8 5.4 fusion.154
  406.2 8.8 %convolution_add_fusion = f32[1024,1536]{1,0:T(8,128)S(1)} fusion(f32[1024,1536]{1,0:T(8,128)} %fusion.188, bf16[1024,1152]{1,0:T(8,128)(2,1)} %concatenate.131, bf16[1536,1152]{1,0:T(8,128)(2,1)} %bitcast.542), kind=kOutput, calls=%fused_computation.33 | convolution fusion | flops 3625451520 | bytes 18481152 | tf_op jit(solution)/shard_map/dot_general | solution.py:82
  423.0 5.1 fusion.153
  470.4 21.5 %collective-permute-done.30 = bf16[256,1536]{1,0:T(8,128)(2,1)S(1)} collective-permute-done((bf16[256,1536]{1,0:T(8,128)(2,1)S(1)}, bf16[256,1536]{1,0:T(8,128)(2,1)S(1)}, u32[]{:S(2)}, u32[]{:S(2)}) %collective-permute-start.30) | collective-permute-done | bytes 786464 | tf_op jit(solution)/shard_map/ppermute | solution.py:131
  539.4 14.9 %collective-permute-done.43 = bf16[192,1152]{1,0:T(8,128)(2,1)S(1)} collective-permute-done((bf16[192,1152]{1,0:T(8,128)(2,1)S(1)}, bf16[192,1152]{1,0:T(8,128)(2,1)S(1)}, u32[]{:S(2)}, u32[]{:S(2)}) %collective-permute-start.43) | collective-permute-done | bytes 442400 | tf_op jit(solution)/shard_map/ppermute | solution.py:125
  554.3 31.6 %collective-permute-done.44 = bf16[192,1152]{1,0:T(8,128)(2,1)S(1)} collective-permute-done((bf16[192,1152]{1,0:T(8,128)(2,1)S(1)}, bf16[192,1152]{1,0:T(8,128)(2,1)S(1)}, u32[]{:S(2)}, u32[]{:S(2)}) %collective-permute-start.44) | collective-permute-done | bytes 442400 | tf_op jit(solution)/shard_map/ppermute | solution.py:125
  589.6 6.2 %collective-permute-done.40 = bf16[192,768]{1,0:T(8,128)(2,1)S(1)} collective-permute-done((bf16[192,768]{1,0:T(8,128)(2,1)S(1)}, bf16[192,768]{1,0:T(8,128)(2,1)S(1)}, u32[]{:S(2)}, u32[]{:S(2)}) %collective-permute-start.40) | collective-permute-done | bytes 294944 | tf_op jit(solution)/shard_map/ppermute | solution.py:125
  (629 shorter events, 325.5 us)
Async XLA Ops:
  0.6 37.6 %collective-permute-start.17 = (bf16[192,768]{1,0:T(8,128)(2,1)}, bf16[192,768]{1,0:T(8,128)(2,1)}, u32[]{:S(2)}, u32[]{:S(2)}) collective-permute-start(bf16[192,768]{1,0:T(8,128)(2,1)} %bitcast.563), channel_id=1, source_target_pairs={{0,16},{4,20},{8,24},{12,28},{16,0},{20,4},{24,8},{28,12},{1,17},{... | collective-permute-start | bytes 884744 | tf_op jit(solution)/shard_map/ppermute | solution.py:125
  6.3 36.7 %collective-permute-start.18 = (bf16[192,768]{1,0:T(8,128)(2,1)}, bf16[192,768]{1,0:T(8,128)(2,1)}, u32[]{:S(2)}, u32[]{:S(2)}) collective-permute-start(bf16[192,768]{1,0:T(8,128)(2,1)} %bitcast.565), channel_id=1, source_target_pairs={{0,24},{4,28},{8,16},{12,20},{16,8},{20,12},{24,0},{28,4},{1,25},{... | collective-permute-start | bytes 884744 | tf_op jit(solution)/shard_map/ppermute | solution.py:125
  6.3 36.8 %collective-permute-start.8 = (bf16[192,768]{1,0:T(8,128)(2,1)}, bf16[192,768]{1,0:T(8,128)(2,1)}, u32[]{:S(2)}, u32[]{:S(2)}) collective-permute-start(bf16[192,768]{1,0:T(8,128)(2,1)} %param.18), channel_id=1, source_target_pairs={{0,8},{4,12},{8,0},{12,4},{16,24},{20,28},{24,16},{28,20},{1,9},{5... | collective-permute-start | bytes 884744 | tf_op jit(solution)/shard_map/ppermute | solution.py:125
  38.2 37.8 %collective-permute-start.9 = (bf16[192,768]{1,0:T(8,128)(2,1)S(1)}, bf16[192,768]{1,0:T(8,128)(2,1)S(1)}, u32[]{:S(2)}, u32[]{:S(2)}) collective-permute-start(bf16[192,768]{1,0:T(8,128)(2,1)S(1)} %copy-done.56), channel_id=1, source_target_pairs={{0,16},{4,20},{8,24},{12,28},{16,0},{20,4},{24,8},{28,12},{1,17},{... | collective-permute-start | bytes 884744 | tf_op jit(solution)/shard_map/ppermute | solution.py:125
  38.8 39.8 %collective-permute-start.6 = (bf16[192,1152]{1,0:T(8,128)(2,1)}, bf16[192,1152]{1,0:T(8,128)(2,1)}, u32[]{:S(2)}, u32[]{:S(2)}) collective-permute-start(bf16[192,1152]{1,0:T(8,128)(2,1)} %concatenate.118), channel_id=1, source_target_pairs={{0,24},{4,28},{8,16},{12,20},{16,8},{20,12},{24,0},{28,4},{1,25},{... | collective-permute-start | bytes 1327112 | tf_op jit(solution)/shard_map/ppermute | solution.py:125
  43.0 51.3 %collective-permute-start.5 = (bf16[192,1152]{1,0:T(8,128)(2,1)}, bf16[192,1152]{1,0:T(8,128)(2,1)}, u32[]{:S(2)}, u32[]{:S(2)}) collective-permute-start(bf16[192,1152]{1,0:T(8,128)(2,1)} %concatenate.118), channel_id=1, source_target_pairs={{0,16},{4,20},{8,24},{12,28},{16,0},{20,4},{24,8},{28,12},{1,17},{... | collective-permute-start | bytes 1327112 | tf_op jit(solution)/shard_map/ppermute | solution.py:125
  43.1 52.7 %collective-permute-start.4 = (bf16[192,1152]{1,0:T(8,128)(2,1)}, bf16[192,1152]{1,0:T(8,128)(2,1)}, u32[]{:S(2)}, u32[]{:S(2)}) collective-permute-start(bf16[192,1152]{1,0:T(8,128)(2,1)} %concatenate.118), channel_id=1, source_target_pairs={{0,8},{4,12},{8,0},{12,4},{16,24},{20,28},{24,16},{28,20},{1,9},{5... | collective-permute-start | bytes 1327112 | tf_op jit(solution)/shard_map/ppermute | solution.py:125
  43.8 53.5 %collective-permute-start.13 = (bf16[256,1536]{1,0:T(8,128)(2,1)}, bf16[256,1536]{1,0:T(8,128)(2,1)}, u32[]{:S(2)}, u32[]{:S(2)}) collective-permute-start(bf16[256,1536]{1,0:T(8,128)(2,1)} %get-tuple-element.175), channel_id=1, source_target_pairs={{0,2},{1,3},{2,0},{3,1},{4,6},{5,7},{6,4},{7,5},{8,10},{9,11},{10,... | collective-permute-start | bytes 2359304 | tf_op jit(solution)/shard_map/ppermute | solution.py:131
  95.8 43.5 %collective-permute-start.19 = (bf16[4,192,768]{2,1,0:T(8,128)(2,1)S(1)}, bf16[4,192,768]{2,1,0:T(8,128)(2,1)S(1)}, u32[]{:S(2)}, u32[]{:S(2)}) collective-permute-start(bf16[4,192,768]{2,1,0:T(8,128)(2,1)S(1)} %pad_maximum_fusion.15), channel_id=1, source_target_pairs={{0,4},{4,0},{8,12},{12,8},{16,20},{20,16},{24,28},{28,24},{1,5},{5... | collective-permute-start | bytes 3538952 | tf_op jit(solution)/shard_map/ppermute | solution.py:128
  97.4 40.2 %collective-permute-start.11 = (bf16[4,192,768]{2,1,0:T(8,128)(2,1)S(1)}, bf16[4,192,768]{2,1,0:T(8,128)(2,1)S(1)}, u32[]{:S(2)}, u32[]{:S(2)}) collective-permute-start(bf16[4,192,768]{2,1,0:T(8,128)(2,1)S(1)} %pad_maximum_fusion.14), channel_id=1, source_target_pairs={{0,4},{4,0},{8,12},{12,8},{16,20},{20,16},{24,28},{28,24},{1,5},{5... | collective-permute-start | bytes 3538952 | tf_op jit(solution)/shard_map/ppermute | solution.py:128
  99.0 48.4 %collective-permute-start.7 = (bf16[4,192,1152]{2,1,0:T(8,128)(2,1)S(1)}, bf16[4,192,1152]{2,1,0:T(8,128)(2,1)S(1)}, u32[]{:S(2)}, u32[]{:S(2)}) collective-permute-start(bf16[4,192,1152]{2,1,0:T(8,128)(2,1)S(1)} %pad_maximum_fusion.11), channel_id=1, source_target_pairs={{0,4},{4,0},{8,12},{12,8},{16,20},{20,16},{24,28},{28,24},{1,5},{5... | collective-permute-start | bytes 5308424 | tf_op jit(solution)/shard_map/ppermute | solution.py:128
  383.5 44.9 %collective-permute-start.32 = (f32[2816]{0:T(1024)S(1)}, f32[2816]{0:T(1024)S(1)}, u32[]{:S(2)}, u32[]{:S(2)}) collective-permute-start(f32[2816]{0:T(1024)S(1)} %pad_maximum_fusion.26), channel_id=1, source_target_pairs={{0,2},{1,3},{2,0},{3,1},{4,6},{5,7},{6,4},{7,5},{8,10},{9,11},{10,... | collective-permute-start | bytes 33800 | tf_op jit(solution)/shard_map/ppermute | solution.py:131
  385.1 43.3 %collective-permute-start.33 = (f32[2816]{0:T(1024)S(1)}, f32[2816]{0:T(1024)S(1)}, u32[]{:S(2)}, u32[]{:S(2)}) collective-permute-start(f32[2816]{0:T(1024)S(1)} %pad_maximum_fusion.26), channel_id=1, source_target_pairs={{0,3},{1,2},{2,1},{3,0},{4,7},{5,6},{6,5},{7,4},{8,11},{9,10},{10,... | collective-permute-start | bytes 33800 | tf_op jit(solution)/shard_map/ppermute | solution.py:131
  385.1 43.2 %collective-permute-start.31 = (f32[2816]{0:T(1024)S(1)}, f32[2816]{0:T(1024)S(1)}, u32[]{:S(2)}, u32[]{:S(2)}) collective-permute-start(f32[2816]{0:T(1024)S(1)} %pad_maximum_fusion.26), channel_id=1, source_target_pairs={{0,1},{1,0},{2,3},{3,2},{4,5},{5,4},{6,7},{7,6},{8,9},{9,8},{10,11... | collective-permute-start | bytes 33800 | tf_op jit(solution)/shard_map/ppermute | solution.py:131
  393.3 71.1 %collective-permute-start.49 = (bf16[4,192,768]{2,1,0:T(8,128)(2,1)}, bf16[4,192,768]{2,1,0:T(8,128)(2,1)}, u32[]{:S(2)}, u32[]{:S(2)}) collective-permute-start(bf16[4,192,768]{2,1,0:T(8,128)(2,1)} %fusion.87), channel_id=1, source_target_pairs={{0,4},{4,0},{8,12},{12,8},{16,20},{20,16},{24,28},{28,24},{1,5},{5... | collective-permute-start | bytes 3538952 | tf_op jit(solution)/shard_map/ppermute | solution.py:128
  397.5 126.1 %collective-permute-start.38 = (bf16[4,192,768]{2,1,0:T(8,128)(2,1)}, bf16[4,192,768]{2,1,0:T(8,128)(2,1)}, u32[]{:S(2)}, u32[]{:S(2)}) collective-permute-start(bf16[4,192,768]{2,1,0:T(8,128)(2,1)} %fusion.86), channel_id=1, source_target_pairs={{0,4},{4,0},{8,12},{12,8},{16,20},{20,16},{24,28},{28,24},{1,5},{5... | collective-permute-start | bytes 3538952 | tf_op jit(solution)/shard_map/ppermute | solution.py:128
  454.5 39.4 %collective-permute-start.26 = (bf16[256,1536]{1,0:T(8,128)(2,1)S(1)}, bf16[256,1536]{1,0:T(8,128)(2,1)S(1)}, u32[]{:S(2)}, u32[]{:S(2)}) collective-permute-start(bf16[256,1536]{1,0:T(8,128)(2,1)S(1)} %pad_maximum_fusion.21), channel_id=1, source_target_pairs={{0,2},{1,3},{2,0},{3,1},{4,6},{5,7},{6,4},{7,5},{8,10},{9,11},{10,... | collective-permute-start | bytes 2359304 | tf_op jit(solution)/shard_map/ppermute | solution.py:131
  491.9 40.7 %collective-permute-start.50 = (bf16[192,768]{1,0:T(8,128)(2,1)}, bf16[192,768]{1,0:T(8,128)(2,1)}, u32[]{:S(2)}, u32[]{:S(2)}) collective-permute-start(bf16[192,768]{1,0:T(8,128)(2,1)} %get-tuple-element.242), channel_id=1, source_target_pairs={{0,8},{4,12},{8,0},{12,4},{16,24},{20,28},{24,16},{28,20},{1,9},{5... | collective-permute-start | bytes 884744 | tf_op jit(solution)/shard_map/ppermute | solution.py:125
  493.9 39.8 %collective-permute-start.52 = (bf16[192,768]{1,0:T(8,128)(2,1)}, bf16[192,768]{1,0:T(8,128)(2,1)}, u32[]{:S(2)}, u32[]{:S(2)}) collective-permute-start(bf16[192,768]{1,0:T(8,128)(2,1)} %get-tuple-element.243), channel_id=1, source_target_pairs={{0,24},{4,28},{8,16},{12,20},{16,8},{20,12},{24,0},{28,4},{1,25},{... | collective-permute-start | bytes 884744 | tf_op jit(solution)/shard_map/ppermute | solution.py:125
  496.5 40.0 %collective-permute-start.51 = (bf16[192,768]{1,0:T(8,128)(2,1)S(1)}, bf16[192,768]{1,0:T(8,128)(2,1)}, u32[]{:S(2)}, u32[]{:S(2)}) collective-permute-start(bf16[192,768]{1,0:T(8,128)(2,1)S(1)} %get-tuple-element.244), channel_id=1, source_target_pairs={{0,16},{4,20},{8,24},{12,28},{16,0},{20,4},{24,8},{28,12},{1,17},{... | collective-permute-start | bytes 884744 | tf_op jit(solution)/shard_map/ppermute | solution.py:125
  532.6 53.3 %collective-permute-start.44 = (bf16[192,1152]{1,0:T(8,128)(2,1)S(1)}, bf16[192,1152]{1,0:T(8,128)(2,1)S(1)}, u32[]{:S(2)}, u32[]{:S(2)}) collective-permute-start(bf16[192,1152]{1,0:T(8,128)(2,1)S(1)} %get-tuple-element.236), channel_id=1, source_target_pairs={{0,16},{4,20},{8,24},{12,28},{16,0},{20,4},{24,8},{28,12},{1,17},{... | collective-permute-start | bytes 1327112 | tf_op jit(solution)/shard_map/ppermute | solution.py:125
  533.8 54.4 %collective-permute-start.39 = (bf16[192,768]{1,0:T(8,128)(2,1)S(1)}, bf16[192,768]{1,0:T(8,128)(2,1)S(1)}, u32[]{:S(2)}, u32[]{:S(2)}) collective-permute-start(bf16[192,768]{1,0:T(8,128)(2,1)S(1)} %get-tuple-element.245), channel_id=1, source_target_pairs={{0,8},{4,12},{8,0},{12,4},{16,24},{20,28},{24,16},{28,20},{1,9},{5... | collective-permute-start | bytes 884744 | tf_op jit(solution)/shard_map/ppermute | solution.py:125
  536.4 53.2 %collective-permute-start.41 = (bf16[192,768]{1,0:T(8,128)(2,1)S(1)}, bf16[192,768]{1,0:T(8,128)(2,1)S(1)}, u32[]{:S(2)}, u32[]{:S(2)}) collective-permute-start(bf16[192,768]{1,0:T(8,128)(2,1)S(1)} %get-tuple-element.246), channel_id=1, source_target_pairs={{0,24},{4,28},{8,16},{12,20},{16,8},{20,12},{24,0},{28,4},{1,25},{... | collective-permute-start | bytes 884744 | tf_op jit(solution)/shard_map/ppermute | solution.py:125
  554.3 41.5 %collective-permute-start.40 = (bf16[192,768]{1,0:T(8,128)(2,1)S(1)}, bf16[192,768]{1,0:T(8,128)(2,1)S(1)}, u32[]{:S(2)}, u32[]{:S(2)}) collective-permute-start(bf16[192,768]{1,0:T(8,128)(2,1)S(1)} %get-tuple-element.247), channel_id=1, source_target_pairs={{0,16},{4,20},{8,24},{12,28},{16,0},{20,4},{24,8},{28,12},{1,17},{... | collective-permute-start | bytes 884744 | tf_op jit(solution)/shard_map/ppermute | solution.py:125
  (164 other events, 1939.3 us)

commit v2 on v1

v2 whole, which is shorter than its diff:
```python
import functools

import jax
import jax.numpy as jnp
from jax import lax
from jax.experimental import pallas as pl
from jax.experimental.pallas import tpu as pltpu
from jax.sharding import PartitionSpec as P

DI = 3072
epsilon = 1e-05
HEAD_DIM = 64
STATE = 128
CONV = 4
SEQ = 1024
SPAN = 256
CHUNK = 128
LANES = 128
NEVER = -1e30
f32 = jnp.float32
bf16 = jnp.bfloat16
highest = lax.Precision.HIGHEST


def dot(first, second, first_dim=1, second_dim=0, precision=None):
    return lax.dot_general(
        first,
        second,
        (((first_dim,), (second_dim,)), ((), ())),
        precision=precision,
        preferred_element_type=f32,
    )


def sigmoid(values):
    return 0.5 * jnp.tanh(0.5 * values) + 0.5


def places(dim):
    return lax.broadcasted_iota(jnp.int32, (CHUNK, LANES), dim)


def decays(step_raw, heads_ref):
    raw = step_raw + heads_ref[0:1]
    small = jnp.exp(-jnp.abs(raw))
    log_one = jnp.where(small < 1e-3, small - 0.5 * small * small, jnp.log(1.0 + small))
    steps = jnp.maximum(raw, 0.0) + log_one
    upto = (places(0) >= places(1)).astype(f32)
    summed = dot(upto, steps * heads_ref[1:2], precision=highest)
    return steps, sigmoid(raw), summed, summed - jnp.log(steps)


def pair_of(first, second):
    return jnp.concatenate([first, second], axis=0)


def forward_kernel(raw_ref, taps_ref, heads_ref, skip_ref, scanned_ref, pre_ref, states_ref, state, before):
    chunk = pl.program_id(0)
    channels = skip_ref.shape[1]
    width = channels + 2 * STATE

    @pl.when(chunk % (SEQ // CHUNK) == 0)
    def _():
        state[...] = jnp.zeros_like(state)
        before[...] = jnp.zeros_like(before)

    raw = raw_ref[:, :width]
    extended = jnp.concatenate([before[...], raw], axis=0)
    pre = taps_ref[CONV : CONV + 1] + taps_ref[CONV - 1 : CONV] * raw
    for tap in range(CONV - 1):
        start = 8 - (CONV - 1) + tap
        pre = pre + taps_ref[tap : tap + 1] * extended[start : start + CHUNK]
    before[...] = raw[CHUNK - 8 :]
    pre_ref[...] = pre
    act = (pre * sigmoid(pre)).astype(bf16)
    writes = act[:, channels : channels + STATE]
    reads = act[:, channels + STATE :]
    _, _, summed, shifted = decays(raw_ref[:, width:], heads_ref)
    summed_t, shifted_t = summed.T, shifted.T
    tail_t = jnp.exp(summed_t[:, CHUNK - 1 :] - shifted_t)
    scores = dot(reads, writes, 1, 1)
    writes_t = writes.astype(f32).T
    causal = places(0) >= places(1)
    left = places(1) < HEAD_DIM
    states_ref[...] = state[...].astype(bf16)
    for pair in range(channels // LANES):
        cols = slice(pair * LANES, (pair + 1) * LANES)
        values = act[:, cols].astype(f32)
        both = pair_of(jnp.where(left, values, 0.0), jnp.where(left, 0.0, values)).astype(bf16)
        mixes, tails, grown = [], [], []
        for head in (2 * pair, 2 * pair + 1):
            here = jnp.broadcast_to(summed[:, head : head + 1], (CHUNK, LANES))
            decay = jnp.exp(jnp.where(causal, here - shifted_t[head : head + 1], NEVER))
            mixes.append((scores * decay).astype(bf16))
            tails.append((writes_t * tail_t[head : head + 1]).astype(bf16))
            grown.append(here)
        stacked = pair_of(jnp.concatenate(mixes, axis=1), jnp.concatenate(tails, axis=1))
        out = dot(stacked, both)
        entering = state[:, cols]
        factor = jnp.exp(jnp.where(left, grown[0], grown[1]))
        across = dot(reads, entering.astype(bf16)) * factor
        scanned_ref[:, cols] = out[:CHUNK] + across + values * skip_ref[:, cols]
        state[:, cols] = entering * factor[CHUNK - 1 :] + out[CHUNK:]


def backward_kernel(part, n_deps, *refs):
    raw_ref, pre_ref, grad_ref, states_ref, taps_ref, heads_ref, skip_ref = refs[:7]
    held, refs = refs[7 : 7 + (5 if part else 0)], refs[7 + (5 if part else 0) + n_deps :]
    low_ref, sums_ref, head_sums_ref, carry, after, wide = refs
    step = pl.program_id(0)
    channels = skip_ref.shape[1]
    width = channels + 2 * STATE

    @pl.when(step == 0)
    def _():
        if part:
            for ref, source in zip((sums_ref, head_sums_ref, carry, after), held[1:], strict=True):
                ref[...] = source[...]
        else:
            sums_ref[...] = jnp.zeros_like(sums_ref)
            head_sums_ref[...] = jnp.zeros_like(head_sums_ref)

    @pl.when((step + part * pl.num_programs(0)) % (SEQ // CHUNK) == 0)
    def _():
        carry[...] = jnp.zeros_like(carry)
        after[...] = jnp.zeros_like(after)

    pre = pre_ref[...]
    gate = sigmoid(pre)
    act = (pre * gate).astype(bf16)
    writes = act[:, channels : channels + STATE]
    reads = act[:, channels + STATE :]
    steps, slopes, summed, shifted = decays(raw_ref[:, width:], heads_ref)
    summed_t = summed.T
    scores_t = dot(writes, reads, 1, 1)
    causal = places(0) <= places(1)
    earlier = places(0) < places(1)
    suffix = (places(0) >= places(1)).astype(bf16)
    left = places(1) < HEAD_DIM
    score_grads = jnp.zeros((CHUNK, LANES), f32)
    spans, inner_grads = [], []
    for pair in range(channels // LANES):
        cols = slice(pair * LANES, (pair + 1) * LANES)
        values = act[:, cols].astype(f32)
        both = pair_of(jnp.where(left, values, 0.0), jnp.where(left, 0.0, values)).astype(bf16)
        grad_low = grad_ref[:, cols]
        grad = grad_low.astype(f32)
        grad_both = pair_of(jnp.where(left, grad, 0.0), jnp.where(left, 0.0, grad)).astype(bf16)
        products = dot(both, grad_low, 1, 1)
        mixes, crossing, grown, tails = [], [], [], []
        for place, head in enumerate((2 * pair, 2 * pair + 1)):
            here = jnp.broadcast_to(shifted[:, head : head + 1], (CHUNK, LANES))
            decay = jnp.exp(jnp.where(causal, summed_t[head : head + 1] - here, NEVER))
            product = products[place * CHUNK : (place + 1) * CHUNK]
            score_grads = score_grads + decay * product
            mix = scores_t * decay
            mixes.append(mix.astype(bf16))
            crossing.append((mix * product).astype(bf16))
            level = jnp.broadcast_to(summed[:, head : head + 1], (CHUNK, LANES))
            grown.append(level)
            tails.append(level[CHUNK - 1 :] - here)
        sums = dot(pair_of(*crossing), suffix)
        for place in range(2):
            part = jnp.where(earlier, sums[place * CHUNK : (place + 1) * CHUNK], 0.0)
            spans.append(jnp.sum(part, axis=0, keepdims=True))
        within = dot(jnp.concatenate(mixes, axis=1), grad_both)
        factor = jnp.exp(jnp.where(left, grown[0], grown[1]))
        tail = jnp.exp(jnp.where(left, tails[0], tails[1]))
        leaving = carry[:, cols]
        entering = states_ref[:, cols]
        later = tail * dot(writes, leaving.astype(bf16))
        both_grads = within + later
        inner_grads.append(both_grads + skip_ref[:, cols] * grad)
        spread = factor * grad
        spread_low = spread.astype(bf16)
        wide[0:CHUNK, cols] = spread_low
        wide[CHUNK : 2 * CHUNK, cols] = (tail * values).astype(bf16)
        wide[2 * CHUNK : 3 * CHUNK, cols] = (spread * dot(reads, entering)).astype(bf16)
        wide[3 * CHUNK : 4 * CHUNK, cols] = (values * later).astype(bf16)
        wide[4 * CHUNK : 5 * CHUNK, cols] = (values * both_grads).astype(bf16)
        held = jnp.sum(entering.astype(f32) * leaving, axis=0, keepdims=True) * factor[CHUNK - 1 :]
        sums_ref[CONV + 1 : CONV + 2, cols] += jnp.sum(grad * values, axis=0, keepdims=True)
        sums_ref[CONV + 2 : CONV + 3, cols] = held
    reads_t = reads.astype(f32).T.astype(bf16)
    score_low = score_grads.astype(bf16)
    spread_all = wide[0:CHUNK, :]
    read_grads = dot(score_low, writes, 0, 0) + dot(spread_all, states_ref[...], 1, 1)
    write_grads = dot(score_low, reads) + dot(wide[CHUNK : 2 * CHUNK, :], carry[...].astype(bf16), 1, 1)
    last = jnp.exp(summed[CHUNK - 1 :])
    of_head = (
        lax.broadcasted_iota(jnp.int32, (channels, LANES), 0) // HEAD_DIM
        == lax.broadcasted_iota(jnp.int32, (channels, LANES), 1)
    )
    reduced = dot(wide[2 * CHUNK : 5 * CHUNK, :], of_head.astype(bf16))
    held_rows = jnp.broadcast_to(sums_ref[CONV + 2 : CONV + 3, :channels], (8, channels))
    held_heads = dot(held_rows, of_head.astype(f32), precision=highest)[0:1]
    lasts = dot(jnp.broadcast_to(last, (8, LANES)), of_head.astype(f32), 1, 1, precision=highest)[0:1]
    carry[...] = carry[...] * lasts + dot(reads_t, spread_all)
    across_sums, later_sums, both_sums = reduced[:CHUNK], reduced[CHUNK : 2 * CHUNK], reduced[2 * CHUNK :]
    span_rows = jnp.concatenate(spans + [jnp.zeros((LANES - len(spans), LANES), f32)], axis=0)
    log_grads = (
        dot((places(0) <= places(1)).astype(f32), across_sums, precision=highest)
        + dot((places(0) > places(1)).astype(f32), later_sums, precision=highest)
        + span_rows.T
        + held_heads
    )
    ratio = jnp.where(steps > 1e-30, slopes / steps, 1.0)
    step_grads = both_sums * ratio + heads_ref[1:2] * log_grads * slopes
    head_sums_ref[0:1] += jnp.sum(step_grads, axis=0, keepdims=True)
    head_sums_ref[1:2] += jnp.sum(log_grads * steps, axis=0, keepdims=True)

    raw = raw_ref[:, :width]
    act_grads = jnp.concatenate(inner_grads + [write_grads, read_grads], axis=1)
    pre_grads = act_grads * (gate * (1.0 + pre * (1.0 - gate)))
    extended = jnp.concatenate([pre_grads, after[...]], axis=0)
    after[...] = pre_grads[:8]
    sums_ref[CONV : CONV + 1] += jnp.sum(pre_grads, axis=0, keepdims=True)
    raw_grads = taps_ref[CONV - 1 : CONV] * pre_grads
    sums_ref[CONV - 1 : CONV] += jnp.sum(raw * pre_grads, axis=0, keepdims=True)
    for tap in range(CONV - 1):
        moved = extended[CONV - 1 - tap : CONV - 1 - tap + CHUNK]
        raw_grads = raw_grads + taps_ref[tap : tap + 1] * moved
        sums_ref[tap : tap + 1] += jnp.sum(raw * moved, axis=0, keepdims=True)
    low_ref[:, :width] = raw_grads.astype(bf16)
    low_ref[:, width:] = step_grads.astype(bf16)


def stay(values):
    return pltpu.with_memory_space_constraint(values, pltpu.HBM)


def scan_forward(raw, taps, heads, skip):
    tokens, full = raw.shape
    channels = skip.shape[1]
    width = channels + 2 * STATE
    count = tokens // CHUNK
    by_chunk = lambda shape: pl.BlockSpec(shape, lambda s: (s, 0))
    whole = lambda v: pl.BlockSpec(v.shape, lambda s: (0, 0))
    return pl.pallas_call(
        forward_kernel,
        grid=(count,),
        in_specs=[by_chunk((CHUNK, full)), whole(taps), whole(heads), whole(skip)],
        out_specs=[
            by_chunk((CHUNK, channels)),
            by_chunk((CHUNK, width)),
            by_chunk((STATE, channels)),
        ],
        scratch_shapes=[pltpu.VMEM((STATE, channels), f32), pltpu.VMEM((8, width), f32)],
        out_shape=[
            jax.ShapeDtypeStruct((tokens, channels), f32),
            pltpu.HBM((tokens, width), f32),
            pltpu.HBM((count * STATE, channels), bf16),
        ],
        compiler_params=pltpu.CompilerParams(vmem_limit_bytes=20 << 20),
        cost_estimate=cost(9),
        name="scan_forward",
    )(raw, taps, heads, skip)


def scan_backward(part, raw, pre, grad, states, taps, heads, skip, held, earlier):
    tokens, full = raw.shape
    channels = skip.shape[1]
    width = channels + 2 * STATE
    count = tokens // CHUNK
    half = count // 2
    last = count - 1 - part * half
    by_chunk = lambda shape: pl.BlockSpec(shape, lambda s: (last - s, 0))
    whole = lambda shape: pl.BlockSpec(shape, lambda s: (0, 0))
    anywhere = pl.BlockSpec(memory_space=pl.ANY)
    kept = [(8, width), (8, LANES), (STATE, channels), (8, width)]
    held = list(held) if part else []
    return pl.pallas_call(
        functools.partial(backward_kernel, part, len(earlier)),
        grid=(half,),
        in_specs=[
            by_chunk((CHUNK, full)),
            by_chunk((CHUNK, width)),
            by_chunk((CHUNK, channels)),
            by_chunk((STATE, channels)),
            whole(taps.shape),
            whole(heads.shape),
            whole(skip.shape),
        ]
        + ([anywhere] + [whole(shape) for shape in kept] if part else [])
        + [anywhere] * len(earlier),
        out_specs=[by_chunk((CHUNK, full))] + [whole(shape) for shape in kept],
        scratch_shapes=[pltpu.VMEM((5 * CHUNK, channels), bf16)],
        out_shape=[jax.ShapeDtypeStruct((tokens, full), bf16)]
        + [jax.ShapeDtypeStruct(shape, f32) for shape in kept],
        input_output_aliases={7: 0} if part else {},
        compiler_params=pltpu.CompilerParams(vmem_limit_bytes=20 << 20),
        cost_estimate=cost(12),
        name=f"scan_backward_{part}",
    )(stay(raw), stay(pre), grad, stay(states), taps, heads, skip, *held, *earlier)


BLOCK = 256


def cost(microseconds):
    return pl.CostEstimate(flops=0, bytes_accessed=int(microseconds * 3.5e6), transcendentals=0)


LIMIT = 24 << 20


def column_sums(values, count):
    rows = [
        jnp.sum(values[i * LANES : (i + 1) * LANES].T, axis=0, keepdims=True)
        for i in range(count // LANES)
    ]
    return jnp.concatenate(rows, axis=0)


def fold(values):
    total = values[:, :LANES]
    for start in range(LANES, values.shape[1], LANES):
        total = total + values[:, start : start + LANES]
    return total


def shard_rows(place, index, chips, height):
    core, chip = index // chips, index % chips
    return pl.multiple_of(((place[0] ^ chip) * 2 + (place[1] ^ core)) * height, height)


def row_start(place, start):
    if isinstance(start, int):
        return pl.multiple_of((start // BLOCK ^ place[2]) * BLOCK + start % BLOCK, LANES)
    return pl.multiple_of((start // BLOCK ^ place[2]) * BLOCK, BLOCK)


def product_kernel(layout, chips, epilogue, place, *refs):
    heights, keep_rows, n_extra, n_out = layout
    n_rows, n_full = len(heights), 2 * chips
    row_refs, refs = refs[:n_rows], refs[n_rows:]
    full_refs, refs = refs[:n_full], refs[n_full:]
    extra, refs = refs[:n_extra], refs[n_extra:]
    outs, refs = refs[:n_out], refs[n_out:]
    full_out, refs = refs[0], refs[1:]
    if keep_rows:
        rows_out, refs = refs[0], refs[1:]
    rows, full, sems, back = refs
    step = pl.program_id(0)
    starts = [sum(heights[:i]) for i in range(n_rows)]
    shard = full.shape[0] // n_full
    row_copies = [
        pltpu.make_async_copy(
            row_refs[i], rows.at[pl.ds(row_start(place, starts[i]), heights[i])], sems.at[i]
        )
        for i in range(n_rows)
    ]
    full_copies = [
        pltpu.make_async_copy(
            full_refs[i], full.at[pl.ds(shard_rows(place, i, chips, shard), shard)], sems.at[n_rows + i]
        )
        for i in range(n_full)
    ]
    backs = [pltpu.make_async_copy(full, full_out, back.at[0])]

    @pl.when(step == 0)
    def _():
        for copy in full_copies + row_copies:
            copy.start()
        for copy in full_copies:
            copy.wait()
        backs[0].start()

    for i in range(n_rows):

        @pl.when(step == starts[i] // BLOCK)
        def _(i=i):
            row_copies[i].wait()

    if keep_rows:
        backs.append(pltpu.make_async_copy(rows, rows_out, back.at[1]))

        @pl.when(step == starts[-1] // BLOCK)
        def _():
            backs[1].start()

    block = rows[pl.ds(row_start(place, step * BLOCK), BLOCK), :]
    epilogue(step, lambda cols: dot(block, full[:, cols]), extra, outs)

    @pl.when(step == pl.num_programs(0) - 1)
    def _():
        for copy in backs:
            copy.wait()


def product(place, row_pieces, full_pieces, epilogue, extra, outs, keep_rows, name):
    chips = len(full_pieces) // 2
    heights = tuple(piece.shape[0] for piece in row_pieces)
    tokens, depth = sum(heights), row_pieces[0].shape[1]
    columns = full_pieces[0].shape[1]
    anywhere = pl.BlockSpec(memory_space=pl.ANY)
    by_block = lambda cols: pl.BlockSpec((BLOCK, cols), lambda s, p: (s ^ p[2], 0))
    whole = lambda shape: pl.BlockSpec(shape, lambda s, p: (0, 0))
    out_specs, out_shape = [], []
    for cols, dtype in outs:
        shape = (tokens // LANES, LANES) if cols is None else (tokens, cols)
        out_specs.append(whole(shape) if cols is None else by_block(cols))
        out_shape.append(jax.ShapeDtypeStruct(shape, dtype))
    out_specs.append(anywhere)
    out_shape.append(jax.ShapeDtypeStruct((depth, columns), bf16))
    if keep_rows:
        out_specs.append(anywhere)
        out_shape.append(jax.ShapeDtypeStruct((tokens, depth), bf16))
    layout = (heights, keep_rows, len(extra), len(outs))
    return pl.pallas_call(
        functools.partial(product_kernel, layout, chips, epilogue),
        grid_spec=pltpu.PrefetchScalarGridSpec(
            num_scalar_prefetch=1,
            grid=(tokens // BLOCK,),
            in_specs=[anywhere] * (len(row_pieces) + len(full_pieces))
            + [by_block(v.shape[1]) if by else whole(v.shape) for v, by in extra],
            out_specs=out_specs,
            scratch_shapes=[
                pltpu.VMEM((tokens, depth), bf16),
                pltpu.VMEM((depth, columns), bf16),
                pltpu.SemaphoreType.DMA((len(row_pieces) + len(full_pieces),)),
                pltpu.SemaphoreType.DMA((2,)),
            ],
        ),
        out_shape=out_shape,
        compiler_params=pltpu.CompilerParams(vmem_limit_bytes=(56 << 20) if keep_rows else LIMIT),
        cost_estimate=cost(8),
        name=name,
    )(place, *row_pieces, *full_pieces, *[v for v, _ in extra])


def slices(columns):
    return [slice(start, min(start + 256, columns)) for start in range(0, columns, 256)]


def raw_epilogue(step, multiply, extra, outs):
    (raw,) = outs
    for cols in slices(raw.shape[1]):
        raw[:, cols] = multiply(cols)


def gate_epilogue(step, multiply, extra, outs):
    (scanned,) = extra
    gate, gated, sums = outs
    total = jnp.zeros((BLOCK, LANES), f32)
    for cols in slices(gate.shape[1]):
        value = multiply(cols)
        gate[:, cols] = value
        product = scanned[:, cols] * (value * sigmoid(value))
        gated[:, cols] = product
        total = total + fold(product * product)
    sums[pl.ds(step * (BLOCK // LANES), BLOCK // LANES), :] = column_sums(total, BLOCK)


def out_epilogue(step, multiply, extra, outs):
    gated, gain = extra
    grad, sums = outs
    total = jnp.zeros((BLOCK, LANES), f32)
    for cols in slices(grad.shape[1]):
        value = multiply(cols)
        grad[:, cols] = value
        total = total + fold(value * gain[:, cols] * gated[:, cols])
    sums[pl.ds(step * (BLOCK // LANES), BLOCK // LANES), :] = column_sums(total, BLOCK)


def grads_kernel(place, rows, low, *refs):
    keep, give, acc = refs[-3:]
    shard = keep.shape[1]
    for cols in slices(low.shape[1]):
        acc[:, cols] = dot(rows[...], low[:, cols], 0, 0)
    keep[0] = acc[pl.ds(pl.multiple_of(place[1] * shard, shard), shard), :]
    give[0] = acc[pl.ds(pl.multiple_of((1 - place[1]) * shard, shard), shard), :].astype(bf16)


def weight_grads(place, chips, rows, low, name, earlier=()):
    tokens, depth = rows.shape
    columns = low.shape[1]
    shard = depth // (2 * chips)
    if depth // chips % LANES:
        whole = dot(rows, low, 0, 0).reshape(chips, 2, shard, columns)
        whole = jnp.take(whole, jnp.arange(chips) ^ place[0], axis=0)
        return jnp.take(whole, place[1], axis=1), jnp.take(whole, 1 - place[1], axis=1).astype(bf16)
    out = pl.BlockSpec((1, shard, columns), lambda k, p: (k, 0, 0))
    return pl.pallas_call(
        grads_kernel,
        grid_spec=pltpu.PrefetchScalarGridSpec(
            num_scalar_prefetch=1,
            grid=(chips,),
            in_specs=[
                pl.BlockSpec((tokens, depth // chips), lambda k, p: (0, k ^ p[0])),
                pl.BlockSpec((tokens, columns), lambda k, p: (0, 0)),
            ]
            + [pl.BlockSpec(memory_space=pl.ANY)] * len(earlier),
            out_specs=[out, out],
            scratch_shapes=[pltpu.VMEM((depth // chips, columns), f32)],
        ),
        out_shape=[
            jax.ShapeDtypeStruct((chips, shard, columns), f32),
            jax.ShapeDtypeStruct((chips, shard, columns), bf16),
        ],
        compiler_params=pltpu.CompilerParams(vmem_limit_bytes=LIMIT),
        cost_estimate=cost(6),
        name=name,
    )(place, rows, low, *earlier)


def back_kernel(count, with_rows, place, *refs):
    lows, fulls, refs = refs[:count], refs[count : 2 * count], refs[2 * count :]
    rows, out, sums = (refs[0], refs[-2], refs[-1]) if with_rows else (None, refs[-1], None)
    if with_rows:

        @pl.when(pl.program_id(0) == 0)
        def _():
            sums[...] = jnp.zeros_like(sums)

    for cols in slices(out.shape[1]):
        value = dot(lows[0][...], fulls[0][cols, :], 1, 1)
        for low, full in zip(lows[1:], fulls[1:], strict=True):
            value = value + dot(low[...], full[cols, :], 1, 1)
        out[:, cols] = value.astype(out.dtype)
        if with_rows:
            sums[0:1, cols] += jnp.sum(value * rows[:, cols].astype(f32), axis=0, keepdims=True)


def back(place, lows, fulls, rows, first, count, dtype, name, earlier):
    depth = fulls[0].shape[0]
    by_block = lambda cols: pl.BlockSpec((BLOCK, cols), lambda s, p: ((s + first) ^ p[2], 0))
    whole = lambda shape: pl.BlockSpec(shape, lambda s, p: (0, 0))
    extra = [] if rows is None else [rows]
    out = pl.pallas_call(
        functools.partial(back_kernel, len(lows), rows is not None),
        grid_spec=pltpu.PrefetchScalarGridSpec(
            num_scalar_prefetch=1,
            grid=(count,),
            in_specs=[by_block(v.shape[1]) for v in lows]
            + [whole(v.shape) for v in fulls]
            + [by_block(depth) for _ in extra]
            + [pl.BlockSpec(memory_space=pl.ANY)] * len(earlier),
            out_specs=[pl.BlockSpec((BLOCK, depth), lambda s, p: (s, 0))] + [whole((8, depth)) for _ in extra],
        ),
        out_shape=[jax.ShapeDtypeStruct((count * BLOCK, depth), dtype)]
        + [jax.ShapeDtypeStruct((8, depth), f32) for _ in extra],
        compiler_params=pltpu.CompilerParams(vmem_limit_bytes=LIMIT),
        cost_estimate=cost(2 * count),
        name=name,
    )(place, *lows, *fulls, *extra, *earlier)
    return out[0], out[1] if extra else None


def columns_of(row):
    return jnp.broadcast_to(row, (LANES, LANES)).T


def low_kernel(gated, squares, gain, out):
    for part in range(BLOCK // LANES):
        rows = slice(part * LANES, (part + 1) * LANES)
        row = squares[pl.ds(pl.program_id(0) * (BLOCK // LANES) + part, 1), :]
        ratio = columns_of(lax.rsqrt(row / DI + epsilon))
        for start in range(0, out.shape[1], LANES):
            cols = slice(start, start + LANES)
            out[rows, cols] = (gain[:, cols] * (gated[rows, cols] * ratio)).astype(bf16)


def low_rows(gated, squares, gain):
    tokens, columns = gated.shape
    return pl.pallas_call(
        low_kernel,
        grid=(tokens // BLOCK,),
        in_specs=[
            pl.BlockSpec((BLOCK, columns), lambda s: (s, 0)),
            pl.BlockSpec(squares.shape, lambda s: (0, 0)),
            pl.BlockSpec(gain.shape, lambda s: (0, 0)),
        ],
        out_specs=pl.BlockSpec((BLOCK, columns), lambda s: (s, 0)),
        out_shape=jax.ShapeDtypeStruct((tokens, columns), bf16),
        cost_estimate=cost(4),
        name="out_normed",
    )(gated, squares, gain)


def gating_kernel(grad_out, gated, scanned, gate, squares, dots, gain, gate_back, scan_grad, gain_grad):
    step = pl.program_id(0)

    @pl.when(step == 0)
    def _():
        gain_grad[...] = jnp.zeros_like(gain_grad)

    for part in range(BLOCK // LANES):
        rows = slice(part * LANES, (part + 1) * LANES)
        place = pl.ds(step * (BLOCK // LANES) + part, 1)
        ratio_row = lax.rsqrt(squares[place, :] / DI + epsilon)
        ratio = columns_of(ratio_row)
        pull = columns_of(ratio_row * ratio_row * ratio_row / DI * dots[place, :])
        for start in range(0, gate.shape[1], LANES):
            cols = slice(start, start + LANES)
            out, held, value = grad_out[rows, cols], gated[rows, cols], gate[rows, cols]
            scaled = out * ratio
            gain_grad[0:1, cols] += jnp.sum(scaled * held, axis=0, keepdims=True)
            grad = gain[:, cols] * scaled - held * pull
            slope = sigmoid(value)
            scan_grad[rows, cols] = (grad * (value * slope)).astype(bf16)
            gate_grad = grad * scanned[rows, cols] * (slope * (1.0 + value * (1.0 - slope)))
            gate_back[rows, cols] = gate_grad.astype(bf16)


def gating(grad_out, gated, scanned, gate, squares, dots, gain):
    tokens, columns = gated.shape
    block = pl.BlockSpec((BLOCK, columns), lambda s: (s, 0))
    whole = lambda v: pl.BlockSpec(v.shape, lambda s: (0, 0))
    return pl.pallas_call(
        gating_kernel,
        grid=(tokens // BLOCK,),
        in_specs=[block] * 4 + [whole(squares), whole(dots), whole(gain)],
        out_specs=[block, block, pl.BlockSpec((8, columns), lambda s: (0, 0))],
        out_shape=[
            jax.ShapeDtypeStruct((tokens, columns), bf16),
            jax.ShapeDtypeStruct((tokens, columns), bf16),
            jax.ShapeDtypeStruct((8, columns), f32),
        ],
        compiler_params=pltpu.CompilerParams(vmem_limit_bytes=LIMIT),
        cost_estimate=cost(3),
        name="gating",
    )(grad_out, gated, scanned, gate, squares, dots, gain)


def nothing(*refs):
    pass


def pinned(values, earlier):
    anywhere = pl.BlockSpec(memory_space=pl.ANY)
    held = pl.pallas_call(
        nothing,
        in_specs=[anywhere] * (len(values) + len(earlier)),
        out_specs=[anywhere] * len(values),
        out_shape=[jax.ShapeDtypeStruct(v.shape, v.dtype) for v in values],
        input_output_aliases={i: i for i in range(len(values))},
        name="pinned",
    )(*values, *earlier)
    return list(held)


def copy_kernel(source, *refs):
    refs[-1][...] = source[...]


def copied(value, earlier):
    whole = pl.BlockSpec(memory_space=pltpu.VMEM)
    return pl.pallas_call(
        copy_kernel,
        in_specs=[whole] + [pl.BlockSpec(memory_space=pl.ANY)] * len(earlier),
        out_specs=whole,
        out_shape=jax.ShapeDtypeStruct(value.shape, value.dtype),
        name="copied",
    )(value, *earlier)


def total_of(own, arrived):
    for value in arrived:
        own = own + value.astype(f32)
    return own


class Net:
    def __init__(self, dp, tensor):
        self.dp, self.tensor = dp, tensor
        self.chips = dp // 2
        self.rank = lax.axis_index("tensor")
        at = lax.axis_index("dp")
        self.place = jnp.stack([at // 2, at % 2, self.row_shift()]).astype(jnp.int32)

    def over_chips(self, values, k):
        return lax.ppermute(values, "dp", [(i, i ^ (2 * k)) for i in range(self.dp)])

    def over_core(self, values):
        return lax.ppermute(values, "dp", [(i, i ^ 1) for i in range(self.dp)])

    def over_tensor(self, values, k):
        return lax.ppermute(values, "tensor", [(i, i ^ k) for i in range(self.tensor)])

    def gather_chips(self, shard):
        return [shard] + [self.over_chips(shard, k) for k in range(1, self.chips)]

    def gather_cores(self, mine):
        return mine + [self.over_core(piece) for piece in mine]

    def gather_whole(self, shard, axis):
        return lax.all_gather(shard, axis, axis=0, tiled=True)

    def scatter_whole(self, values, axis):
        return lax.psum_scatter(values, axis, scatter_dimension=0, tiled=True).astype(f32)

    def scatter_pairs(self, keep, give):
        pairs = keep + self.over_core(give).astype(f32)
        return pairs[0], [pairs[k].astype(bf16) for k in range(1, self.chips)]

    def over_all_chips(self, others):
        return [self.over_chips(value, k + 1) for k, value in enumerate(others)]

    def row_shift(self):
        return self.rank if self.tensor == 4 else jnp.zeros_like(self.rank)

    def gather_tensor(self, shard):
        if self.tensor != 4:
            return [lax.all_gather(shard, "tensor", axis=0, tiled=True)]
        half = shard.shape[0] // 2
        one, two = self.over_tensor(shard, 1), self.over_tensor(shard, 2)
        return [shard, one, two, self.over_tensor(one[:half], 2), self.over_tensor(two[half:], 1)]

    def scatter_tensor(self, lows, fulls, rows, name, earlier):
        tokens = lows[0].shape[0]
        if self.tensor != 4:
            low, sums = back(self.place, lows, fulls, rows, 0, tokens // BLOCK, bf16, name, earlier)
            return lax.psum_scatter(low, "tensor", scatter_dimension=0, tiled=True).astype(f32), sums
        last, last_sums = back(self.place, lows, fulls, rows, 3, 1, bf16, name + "_last", earlier)
        half = BLOCK // 2
        to_one = self.over_tensor(last[:half], 2)
        to_two = self.over_tensor(last[half:], 1)
        rest, rest_sums = back(self.place, lows, fulls, rows, 0, 3, f32, name, [last])
        own, one, two = jnp.split(rest, 3)
        one = jnp.concatenate([one[:half] + to_one.astype(f32), one[half:]]).astype(bf16)
        two = jnp.concatenate([two[:half], two[half:] + to_two.astype(f32)]).astype(bf16)
        total = own + self.over_tensor(one, 1).astype(f32) + self.over_tensor(two, 2).astype(f32)
        return total, None if rows is None else last_sums + rest_sums

    def branch(self, low, full):
        place = self.place * jnp.array([1, 1, 0], jnp.int32)
        partial, _ = back(place, [low], [full], None, 0, low.shape[0] // BLOCK, bf16, "branch", [])
        return lax.psum_scatter(partial, "tensor", scatter_dimension=0, tiled=True).astype(f32)

    def sum_tensor(self, values):
        total = values
        for k in range(1, self.tensor):
            total = total + self.over_tensor(values, k)
        return total

    def sum_dp(self, values):
        pair = values + self.over_core(values)
        total = pair
        for k in range(1, self.chips):
            total = total + self.over_chips(pair, k)
        return total


def local(
    net_of,
    tokens,
    norm_gain,
    gate_proj,
    inner_proj,
    shared_proj,
    step_proj,
    conv_inner,
    conv_inner_bias,
    conv_shared,
    conv_shared_bias,
    step_bias,
    decay_log,
    skip_gain,
    out_gain,
    out_proj,
    cotangent,
):
    net = net_of()
    place, chips = net.place, net.chips
    straight = place * jnp.array([1, 1, 0], jnp.int32)
    channels = gate_proj.shape[1]
    heads = step_proj.shape[1]
    width = channels + 2 * STATE
    token_rows = tokens.astype(f32)
    inverse = lax.rsqrt(jnp.mean(token_rows * token_rows, axis=-1, keepdims=True) + epsilon)
    unit = token_rows * inverse
    normed_low = (unit * norm_gain).astype(bf16)
    padding = jnp.zeros((step_proj.shape[0], LANES - heads), bf16)
    scan_shard = jnp.concatenate([inner_proj, shared_proj, step_proj, padding], axis=1)
    scan_mine = net.gather_chips(scan_shard)
    row_pieces = net.gather_tensor(normed_low)
    scan_pieces = net.gather_cores(scan_mine)
    reached = scan_mine[1:]
    gate_mine = net.gather_chips(copied(gate_proj, reached + row_pieces[1:3]))
    cot_rows = net.gather_whole(copied(cotangent, reached + row_pieces), "tensor")

    taps = jnp.concatenate(
        [
            jnp.concatenate([conv_inner, conv_inner_bias[None]]),
            jnp.concatenate([conv_shared, conv_shared_bias[None]]),
        ],
        axis=1,
    )
    taps = jnp.pad(taps, ((0, 8 - CONV - 1), (0, 0)))
    rates = -jnp.exp(decay_log)
    head_rows = jnp.pad(jnp.stack([step_bias, rates]), ((0, 6), (0, LANES - heads)))
    skip_row = jnp.repeat(skip_gain, HEAD_DIM)[None]
    gain = out_gain[None]

    raw, scan_full, rows = product(
        place, row_pieces, scan_pieces, raw_epilogue, [], [(width + LANES, f32)], True, "project"
    )
    scanned, pre, states = scan_forward(raw, taps, head_rows, skip_row)
    gate_mine = pinned(gate_mine, [scanned])
    gate_pieces = net.gather_cores(gate_mine)
    outward_mine = net.gather_chips(copied(out_proj.T, gate_mine))
    gate, gated, squares, gate_full = product(
        straight,
        [rows],
        gate_pieces,
        gate_epilogue,
        [(scanned, True)],
        [(channels, f32), (channels, f32), (None, f32)],
        False,
        "gate",
    )
    squares = net.sum_tensor(squares)
    out_low = low_rows(gated, squares, gain)
    out_keep, out_give = weight_grads(place, chips, cot_rows, out_low, "grad_out_proj")
    outward_mine = pinned(outward_mine, [out_give])
    outward_pieces = net.gather_cores(outward_mine)
    grad_out, dots, outward_full = product(
        straight,
        [cot_rows],
        outward_pieces,
        out_epilogue,
        [(gated, True), (gain, False)],
        [(channels, f32), (None, f32)],
        False,
        "grad_out",
    )
    out_own, out_others = net.scatter_pairs(out_keep, out_give)
    out_others = pinned(out_others, outward_mine)
    out_arrived = net.over_all_chips(out_others)
    dots = net.sum_tensor(dots)
    branch = net.branch(out_low, outward_full)
    mixed = (token_rows + branch).astype(bf16)
    gate_back, scan_grad, gain_grad = gating(grad_out, gated, scanned, gate, squares, dots, gain)
    gate_keep, gate_give = weight_grads(place, chips, rows, gate_back, "grad_gate_proj")
    gate_own, gate_others = net.scatter_pairs(gate_keep, gate_give)
    carried = scan_backward(
        0, raw, pre, scan_grad, states, taps, head_rows, skip_row, None, gate_others
    )
    out_arrived = pinned(out_arrived, [carried[1]])
    grad_out_proj = total_of(out_own, out_arrived)
    gate_arrived = net.over_all_chips(pinned(gate_others, out_arrived))
    scan_back, sums, head_sums, _, _ = scan_backward(
        1, raw, pre, scan_grad, states, taps, head_rows, skip_row, carried, out_arrived
    )
    scan_keep, scan_give = weight_grads(
        place, chips, rows, scan_back, "grad_scan_proj", gate_arrived
    )
    scan_own, scan_others = net.scatter_pairs(scan_keep, scan_give)
    grad_gate_proj = total_of(gate_own, gate_arrived)
    scan_arrived = net.over_all_chips(scan_others)
    grad_scan_proj = total_of(scan_own, scan_arrived)
    grad_normed, norm_sums = net.scatter_tensor(
        [gate_back, scan_back], [gate_full, scan_full], rows, "grad_normed", [scan_give]
    )
    grad_out_proj = grad_out_proj.T
    grad_inner_proj = grad_scan_proj[:, :channels]
    grad_shared_proj = net.sum_tensor(grad_scan_proj[:, channels:width])
    grad_step_proj = grad_scan_proj[:, width : width + heads]
    grad_norm_gain = jnp.sum(norm_sums, axis=0) / norm_gain
    spread = grad_normed * norm_gain
    grad_tokens = (
        cotangent.astype(f32)
        + inverse * spread
        - unit * (inverse * jnp.mean(spread * unit, axis=-1, keepdims=True))
    )
    own = (
        sums[:CONV, :channels],
        sums[CONV, :channels],
        gain_grad[0],
        head_sums[0, :heads],
        head_sums[1, :heads] * rates,
        jnp.sum(sums[CONV + 1, :channels].reshape(heads, HEAD_DIM), axis=1),
    )
    common = (sums[:CONV, channels:], sums[CONV, channels:], grad_norm_gain)
    common_flat = net.sum_tensor(jnp.concatenate([v.reshape(-1) for v in common]))
    flat = net.sum_dp(jnp.concatenate([v.reshape(-1) for v in own] + [common_flat]))
    small = []
    start = 0
    for v in own + common:
        small.append(flat[start : start + v.size].reshape(v.shape))
        start += v.size
    (
        grad_conv_inner,
        grad_conv_inner_bias,
        grad_out_gain,
        grad_step_bias,
        grad_decay_log,
        grad_skip_gain,
        grad_conv_shared,
        grad_conv_shared_bias,
        grad_norm_gain,
    ) = small
    return (
        mixed,
        grad_tokens,
        grad_norm_gain,
        grad_gate_proj,
        grad_inner_proj,
        grad_shared_proj,
        grad_step_proj,
        grad_conv_inner,
        grad_conv_inner_bias,
        grad_conv_shared,
        grad_conv_shared_bias,
        grad_step_bias,
        grad_decay_log,
        grad_skip_gain,
        grad_out_gain,
        grad_out_proj,
    )


def solution(mesh):
    dp, tensor = mesh.shape["dp"], mesh.shape["tensor"]

    def on_device(*args):
        return local(lambda: Net(dp, tensor), *args)

    return jax.shard_map(
        on_device,
        mesh=mesh,
        in_specs=(
            P(("dp", "tensor"), None),
            P(),
            P("dp", "tensor"),
            P("dp", "tensor"),
            P("dp", None),
            P("dp", "tensor"),
            P(None, "tensor"),
            P("tensor"),
            P(),
            P(),
            P("tensor"),
            P("tensor"),
            P("tensor"),
            P("tensor"),
            P("tensor", "dp"),
            P(("dp", "tensor"), None),
        ),
        out_specs=(
            P(("dp", "tensor"), None),
            P(("dp", "tensor"), None),
            P(),
            P("dp", "tensor"),
            P("dp", "tensor"),
            P("dp", None),
            P("dp", "tensor"),
            P(None, "tensor"),
            P("tensor"),
            P(),
            P(),
            P("tensor"),
            P("tensor"),
            P("tensor"),
            P("tensor"),
            P("tensor", "dp"),
        ),
        check_vma=False,
    )
```

time: 603 us -> 365 us (0.61)
  matrix products: 131 us -> 0 us
  other arithmetic: 137 us -> 28.4 us
  Pallas kernels: 0 us -> 98.8 us
  local copies, waits for them, and re-layouts: 121 us -> 57.8 us
  waiting for transfers between devices: 142 us -> 91.1 us
  between operations: 3.36 us -> 14.9 us
    dot_general x21 -> x0, matrix products: 131 us -> none  [the longest x3 51.4 us: scan_heads(): jnp.einsum('sctuh,scuhp->scthp', scores[..., None] * kernel, weighted, pr...]
    pallas_call x0 -> x22, Pallas kernels: none -> 98.8 us  [the longest x2 25.9 us: scan_backward(): pl.pallas_call(functools.partial(backward_kernel, part, len(earlier)), gr...]
    reshape x31 -> x0, local copies, waits for them, and re-layouts: 47.1 us -> none  [the longest x2 10.4 us: scan_heads(): shaped = values.reshape(-1, spans, SPAN, head_count, HEAD_DIM)]
    ppermute x21, waiting for transfers between devices: 95 us -> 51.4 us  [over_chips(): return lax.ppermute(values, 'dp', [(i, i ^ 2 * k) for i in range(self.dp)])]
    another operation x23 -> x7, other arithmetic: 45.7 us -> 11.4 us
    unnamed x284 -> x170, local copies, waits for them, and re-layouts: 18.3 us -> 47.7 us
    concatenate x24 -> x3, other arithmetic: 20.3 us -> 0.12 us  [the longest x1 0.05 us: scatter_tensor(): jnp.concatenate([two[:half], two[half:] + to_two.astype(f32)]).astype(bf16)]
    slice x35 -> x10, local copies, waits for them, and re-layouts: 21.8 us -> 1.69 us  [the longest x1 0.93 us: scatter_tensor(): to_one = self.over_tensor(last[:half], 2)]
  transfers between devices with their start and end apart: 53 -> 59, of which waited for: 16 -> 28; matrix products, arithmetic and copies ran while one was open for 27% -> 9% of each run, Pallas kernels for 0% -> 27%
where the time goes in v2:
time: 365 us; the launch traced here: 360 us
  Pallas kernels  98.8 us (27%)
  waiting for transfers between devices  91.1 us (25%)
  starting transfers between devices  68.9 us (19%)
  local copies, waits for them, and re-layouts  57.8 us (16%)
  other arithmetic  28.4 us (8%)
  between operations  14.9 us (4%)
    ppermute x21, waiting for transfers between devices, over_chips(): return lax.ppermute(values, 'dp', [(i, i ^ 2 * k) for i in range(self.dp)])  51.4 us
    unnamed x170, local copies, waits for them, and re-layouts  47.7 us
    ppermute x21, starting transfers between devices, over_chips(): return lax.ppermute(values, 'dp', [(i, i ^ 2 * k) for i in range(self.dp)])  40.6 us
    ppermute x20, waiting for transfers between devices, over_tensor(): lax.ppermute(values, 'tensor', [(i, i ^ k) for i in range(self.tensor)])  35.1 us
    pallas_call x2, Pallas kernels, scan_backward(): pl.pallas_call(functools.partial(backward_kernel, part, len(earlier)), gr...  25.9 us
    ppermute x20, starting transfers between devices, over_tensor(): lax.ppermute(values, 'tensor', [(i, i ^ k) for i in range(self.tensor)])  25 us
    pallas_call x3, Pallas kernels, product(): pl.pallas_call(functools.partial(product_kernel, layout, chips, epilogue)...  21 us
    pallas_call x3, Pallas kernels, weight_grads(): pl.pallas_call(grads_kernel, grid_spec=pltpu.PrefetchScalarGridSpec(num_s...  17.5 us
  transfers between devices with their start and end apart: 59, of which 28 were waited for; matrix products, arithmetic and copies ran while one was open for 9% of the time, Pallas kernels for 27%

profile of v2, /device:TPU:0, one launch (start us, length us, event | category | flops | bytes accessed | tf_op | source)
XLA Modules:
  0.0 359.9 jit_solution(2388326517773242082)
XLA Ops:
  20.1 10.6 %collective-permute-done.refs_1_.refs_3_.refs_4_ = bf16[256,1536]{1,0:T(8,128)(2,1)S(1)} collective-permute-done((bf16[256,1536]{1,0:T(8,128)(2,1)S(1)}, bf16[256,1536]{1,0:T(8,128)(2,1)S(1)}, u32[]{:S(2)}, u32[]{:S(2)}) %collective-permute-start) | collective-permute-done | bytes 786464 | tf_op jit(solution)/shard_map/ppermute | solution.py:679
  34.2 5.5 %collective-permute-done.4.refs_6_.refs_0_ = bf16[192,1152]{1,0:T(8,128)(2,1)S(1)} collective-permute-done((bf16[192,1152]{1,0:T(8,128)(2,1)}, bf16[192,1152]{1,0:T(8,128)(2,1)S(1)}, u32[]{:S(2)}, u32[]{:S(2)}) %collective-permute-start.4) | collective-permute-done | bytes 442400 | tf_op jit(solution)/shard_map/ppermute | solution.py:673
  39.7 17.1 %collective-permute-done.5.refs_7_.refs_1_ = bf16[192,1152]{1,0:T(8,128)(2,1)} collective-permute-done((bf16[192,1152]{1,0:T(8,128)(2,1)}, bf16[192,1152]{1,0:T(8,128)(2,1)}, u32[]{:S(2)}, u32[]{:S(2)}) %collective-permute-start.5) | collective-permute-done | bytes 442400 | tf_op jit(solution)/shard_map/ppermute | solution.py:673
  68.0 9.8 %project.1 = (f32[1024,1152]{1,0:T(8,128)}, bf16[1536,1152]{1,0:T(8,128)(2,1)}, bf16[1024,1536]{1,0:T(8,128)(2,1)}) custom-call(s32[3]{0:T(128)} %get-tuple-element.143.place, bf16[256,1536]{1,0:T(8,128)(2,1)} %copy-done.57, bf16[256,1536]{1,0:T(8,128)(2,1)} %copy-done.55, bf16[256,1536]{1,0:T(8,128)(2,1)} %copy-done.56, ...), custom_call_target="tpu_custom_call" | custom-call | bytes 28000000 | tf_op jit(solution)/shard_map/project/pallas_call | solution.py:410
  80.2 9.8 %scan_forward.1 = (f32[1024,768]{1,0:T(8,128)S(1)}, f32[1024,1024]{1,0:T(8,128)}, bf16[1024,768]{1,0:T(8,128)(2,1)}) custom-call(f32[1024,1152]{1,0:T(8,128)S(1)} %copy-done.1, f32[8,1024]{1,0:T(8,128)S(1)} %fusion.18.taps_ref.refs_4_, f32[8,128]{1,0:T(8,128)S(1)} %select_maximum_fusion.2.heads_ref.refs_5_, f32[1,768]{1,0:T(1,128)S(1)} %broadcast_in_dim_reshape.3.skip_ref.refs_6_), custom_call_target="tpu_custom_call" | custom-call | bytes 31500000 | tf_op jit(solution)/shard_map/scan_forward/pallas_call | solution.py:239
  101.9 5.4 %gate.1 = (f32[1024,768]{1,0:T(8,128)S(1)}, f32[1024,768]{1,0:T(8,128)S(1)}, f32[8,128]{1,0:T(8,128)S(1)}, bf16[1536,768]{1,0:T(8,128)(2,1)S(1)}) custom-call(s32[3]{0:T(128)S(1)} %get-tuple-element.142.place, bf16[1024,1536]{1,0:T(8,128)(2,1)S(1)} %copy-done, bf16[192,768]{1,0:T(8,128)(2,1)S(1)} %copy-done.29, bf16[192,768]{1,0:T(8,128)(2,1)S(1)} %copy-done.38, ...), custom_call_target="tpu_custom_call" | custom-call | bytes 28000000 | tf_op jit(solution)/shard_map/gate/pallas_call | solution.py:410
  122.9 4.2 %out_normed.1.low.refs_0_ = bf16[1024,768]{1,0:T(8,128)(2,1)} custom-call(f32[1024,768]{1,0:T(8,128)} %copy-done.10, f32[8,128]{1,0:T(8,128)} %add_add_fusion.4.squares, f32[1,768]{1,0:T(1,128)} %broadcast_in_dim.23.gain.refs_10_), custom_call_target="tpu_custom_call" | custom-call | bytes 14000000 | tf_op jit(solution)/shard_map/out_normed/pallas_call | solution.py:566
  130.4 5.2 %grad_out_proj.1 = (f32[4,192,768]{2,1,0:T(8,128)S(1)}, bf16[4,192,768]{2,1,0:T(8,128)(2,1)}) custom-call(s32[3]{0:T(128)S(1)} %copy-done.53, bf16[1024,1536]{1,0:T(8,128)(2,1)S(1)} %copy-done.21, bf16[1024,768]{1,0:T(8,128)(2,1)S(1)} %copy-done.14), custom_call_target="tpu_custom_call" | custom-call | bytes 21000000 | tf_op jit(solution)/shard_map/grad_out_proj/pallas_call | solution.py:484
  137.0 4.8 %collective-permute-done.22.refs_2_ = bf16[192,768]{1,0:T(8,128)(2,1)} collective-permute-done((bf16[192,768]{1,0:T(8,128)(2,1)}, bf16[192,768]{1,0:T(8,128)(2,1)}, u32[]{:S(2)}, u32[]{:S(2)}) %collective-permute-start.22) | collective-permute-done | bytes 294944 | tf_op jit(solution)/shard_map/ppermute | solution.py:673
  150.6 5.8 %grad_out.1 = (f32[1024,768]{1,0:T(8,128)S(1)}, f32[8,128]{1,0:T(8,128)S(1)}, bf16[1536,768]{1,0:T(8,128)(2,1)S(1)}) custom-call(s32[3]{0:T(128)S(1)} %get-tuple-element.142.place, bf16[1024,1536]{1,0:T(8,128)(2,1)S(1)} %copy-done.22, bf16[192,768]{1,0:T(8,128)(2,1)S(1)} %copy-done.30, bf16[192,768]{1,0:T(8,128)(2,1)S(1)} %copy-done.44, ...), custom_call_target="tpu_custom_call" | custom-call | bytes 28000000 | tf_op jit(solution)/shard_map/grad_out/pallas_call | solution.py:410
  166.6 5.2 %grad_gate_proj.1 = (f32[4,192,768]{2,1,0:T(8,128)S(1)}, bf16[4,192,768]{2,1,0:T(8,128)(2,1)}) custom-call(s32[3]{0:T(128)S(1)} %copy-done.53, bf16[1024,1536]{1,0:T(8,128)(2,1)S(1)} %copy-done, bf16[1024,768]{1,0:T(8,128)(2,1)S(1)} %get-tuple-element.85.low.refs_0_), custom_call_target="tpu_custom_call" | custom-call | bytes 21000000 | tf_op jit(solution)/shard_map/grad_gate_proj/pallas_call | solution.py:484
  173.3 3.8 %branch.1 = bf16[1024,1536]{1,0:T(8,128)(2,1)S(1)} custom-call(s32[3]{0:T(128)S(1)} %get-tuple-element.142.place, bf16[1024,768]{1,0:T(8,128)(2,1)S(1)} %copy-done.15, bf16[1536,768]{1,0:T(8,128)(2,1)S(1)} %get-tuple-element.81.refs_1_), custom_call_target="tpu_custom_call" | custom-call | bytes 28000000 | tf_op jit(solution)/shard_map/branch/pallas_call | solution.py:530
  184.1 5.2 %collective-permute-start.33 = (bf16[192,768]{1,0:T(8,128)(2,1)}, bf16[192,768]{1,0:T(8,128)(2,1)S(1)}, u32[]{:S(2)}, u32[]{:S(2)}) collective-permute-start(bf16[192,768]{1,0:T(8,128)(2,1)} %get-tuple-element.97), channel_id=1, source_target_pairs={{0,8},{4,12},{8,0},{12,4},{16,24},{20,28},{24,16},{28,20},{1,9},{5... | collective-permute-start | bytes 884744 | tf_op jit(solution)/shard_map/ppermute | solution.py:673
  197.0 12.8 %scan_backward_0.1 = (bf16[1024,1152]{1,0:T(8,128)(2,1)S(1)}, f32[8,1024]{1,0:T(8,128)S(1)}, f32[8,128]{1,0:T(8,128)S(1)}, f32[128,768]{1,0:T(8,128)S(1)}, f32[8,1024]{1,0:T(8,128)S(1)}) custom-call(f32[1024,1152]{1,0:T(8,128)} %get-tuple-element.68.raw_ref.refs_0_, f32[1024,1024]{1,0:T(8,128)} %get-tuple-element.86.refs_1_, ...), custom_call_target="tpu_custom_call" | custom-call | bytes 42000000 | tf_op jit(solution)/shard_map/scan_backward_0/pallas_call | solution.py:272
  216.7 5.6 %collective-permute-start.36 = (bf16[192,768]{1,0:T(8,128)(2,1)}, bf16[192,768]{1,0:T(8,128)(2,1)}, u32[]{:S(2)}, u32[]{:S(2)}) collective-permute-start(bf16[192,768]{1,0:T(8,128)(2,1)} %get-tuple-element.106), channel_id=1, source_target_pairs={{0,8},{4,12},{8,0},{12,4},{16,24},{20,28},{24,16},{28,20},{1,9},{5... | collective-permute-start | bytes 884744 | tf_op jit(solution)/shard_map/ppermute | solution.py:673
  226.3 13.1 %scan_backward_1.1 = (bf16[1024,1152]{1,0:T(8,128)(2,1)S(1)}, f32[8,1024]{1,0:T(8,128)S(1)}, f32[8,128]{1,0:T(8,128)S(1)}, f32[128,768]{1,0:T(8,128)}, f32[8,1024]{1,0:T(8,128)}) custom-call(f32[1024,1152]{1,0:T(8,128)} %get-tuple-element.68.raw_ref.refs_0_, f32[1024,1024]{1,0:T(8,128)} %get-tuple-element.86.refs_1_, ...), custom_call_target="tpu_custom_call", output_to_operand_aliasing={{0}: (7, {})} | custom-call | bytes 42000000 | tf_op jit(solution)/shard_map/scan_backward_1/pallas_call | solution.py:272
  241.2 4.9 %collective-permute-done.37.refs_1_ = bf16[192,768]{1,0:T(8,128)(2,1)} collective-permute-done((bf16[192,768]{1,0:T(8,128)(2,1)}, bf16[192,768]{1,0:T(8,128)(2,1)}, u32[]{:S(2)}, u32[]{:S(2)}) %collective-permute-start.37) | collective-permute-done | bytes 294944 | tf_op jit(solution)/shard_map/ppermute | solution.py:673
  247.8 7.0 %grad_scan_proj.1 = (f32[4,192,1152]{2,1,0:T(8,128)S(1)}, bf16[4,192,1152]{2,1,0:T(8,128)(2,1)}) custom-call(s32[3]{0:T(128)S(1)} %copy-done.53, bf16[1024,1536]{1,0:T(8,128)(2,1)S(1)} %copy-done, bf16[1024,1152]{1,0:T(8,128)(2,1)S(1)} %copy-done.5, bf16[192,768]{1,0:T(8,128)(2,1)} %collective-permute-done.36.refs_0_, ...), custom_call_target="tpu_custom_call" | custom-call | bytes 21000000 | tf_op jit(solution)/shard_map/grad_scan_proj/pallas_call | solution.py:484
  262.2 6.3 %grad_normed.1 = (f32[768,1536]{1,0:T(8,128)S(1)}, f32[8,1536]{1,0:T(8,128)S(1)}) custom-call(s32[3]{0:T(128)S(1)} %copy-done.53, bf16[1024,768]{1,0:T(8,128)(2,1)S(1)} %copy-done.19, bf16[1024,1152]{1,0:T(8,128)(2,1)S(1)} %copy-done.6, bf16[1536,768]{1,0:T(8,128)(2,1)S(1)} %copy-done.25, bf16[1536,1152]{1,0:T(8,128)(2,1)S(1)} %copy-done.16, ...), custom_call_target="tpu_custom_call" | custom-call | bytes 21000000 | tf_op jit(solution)/shard_map/grad_normed/pallas_call | solution.py:530
  277.4 5.0 %collective-permute-start.47 = (f32[7460]{0:T(1024)S(1)}, f32[7460]{0:T(1024)S(1)}, u32[]{:S(2)}, u32[]{:S(2)}) collective-permute-start(f32[7460]{0:T(1024)S(1)} %add.151), channel_id=1, source_target_pairs={{0,8},{4,12},{8,0},{12,4},{16,24},{20,28},{24,16},{28,20},{1,9},{5... | collective-permute-start | bytes 89528 | tf_op jit(solution)/shard_map/ppermute | solution.py:673
  292.3 5.6 %collective-permute-done.41 = bf16[128,1536]{1,0:T(8,128)(2,1)S(1)} collective-permute-done((bf16[128,1536]{1,0:T(8,128)(2,1)}, bf16[128,1536]{1,0:T(8,128)(2,1)S(1)}, u32[]{:S(2)}, u32[]{:S(2)}) %collective-permute-start.41) | collective-permute-done | bytes 393248 | tf_op jit(solution)/shard_map/ppermute | solution.py:679
  308.8 9.2 %collective-permute-done.40 = bf16[256,1536]{1,0:T(8,128)(2,1)S(1)} collective-permute-done((bf16[256,1536]{1,0:T(8,128)(2,1)S(1)}, bf16[256,1536]{1,0:T(8,128)(2,1)S(1)}, u32[]{:S(2)}, u32[]{:S(2)}) %collective-permute-start.40) | collective-permute-done | bytes 786464 | tf_op jit(solution)/shard_map/ppermute | solution.py:679
  322.1 15.4 %collective-permute-done.52 = bf16[192,1152]{1,0:T(8,128)(2,1)S(1)} collective-permute-done((bf16[192,1152]{1,0:T(8,128)(2,1)S(1)}, bf16[192,1152]{1,0:T(8,128)(2,1)S(1)}, u32[]{:S(2)}, u32[]{:S(2)}) %collective-permute-start.52) | collective-permute-done | bytes 442400 | tf_op jit(solution)/shard_map/ppermute | solution.py:673
  349.0 4.1 %fusion.5 = (f32[256,1536]{1,0:T(8,128)}, bf16[256,1536]{1,0:T(8,128)(2,1)}) fusion(bf16[256,1536]{1,0:T(8,128)(2,1)S(1)} %copy-done.54, bf16[256,1536]{1,0:T(8,128)(2,1)} %source.3, f32[256]{0:T(256)S(1)} %multiply_multiply_fusion, f32[256]{0:T(256)S(1)} %copy-done.69, f32[1536]{0:T(1024)S(1)} %copy-done.65, ...), kind=kLoop, calls=%fused_computation.11 | loop fusion | flops 5898240 | bytes 7872512 | tf_op jit(solution)/shard_map/sub | solution.py:863
  (351 shorter events, 163.5 us)
Async XLA Ops:
  7.2 119.9 %all-gather.2.cloned.1.call-start = ((), (), s32[]{:S(2)}) async-start(), calls=%async_computation.1 | async-start | bytes 3932160 | tf_op jit(solution)/shard_map/all_gather | solution.py:688
  10.1 20.5 %collective-permute-start = (bf16[256,1536]{1,0:T(8,128)(2,1)S(1)}, bf16[256,1536]{1,0:T(8,128)(2,1)S(1)}, u32[]{:S(2)}, u32[]{:S(2)}) collective-permute-start(bf16[256,1536]{1,0:T(8,128)(2,1)S(1)} %fusion.3.refs_0_.refs_3_), channel_id=1, source_target_pairs={{0,1},{1,0},{2,3},{3,2},{4,5},{5,4},{6,7},{7,6},{8,9},{9,8},{10,11... | collective-permute-start | bytes 2359304 | tf_op jit(solution)/shard_map/ppermute | solution.py:679
  13.1 19.4 %collective-permute-start.1 = (bf16[256,1536]{1,0:T(8,128)(2,1)S(1)}, bf16[256,1536]{1,0:T(8,128)(2,1)S(1)}, u32[]{:S(2)}, u32[]{:S(2)}) collective-permute-start(bf16[256,1536]{1,0:T(8,128)(2,1)S(1)} %fusion.3.refs_0_.refs_3_), channel_id=1, source_target_pairs={{0,2},{1,3},{2,0},{3,1},{4,6},{5,7},{6,4},{7,5},{8,10},{9,11},{10,... | collective-permute-start | bytes 2359304 | tf_op jit(solution)/shard_map/ppermute | solution.py:679
  19.3 20.4 %collective-permute-start.4 = (bf16[192,1152]{1,0:T(8,128)(2,1)}, bf16[192,1152]{1,0:T(8,128)(2,1)S(1)}, u32[]{:S(2)}, u32[]{:S(2)}) collective-permute-start(bf16[192,1152]{1,0:T(8,128)(2,1)} %concatenate.26.refs_5_), channel_id=1, source_target_pairs={{0,8},{4,12},{8,0},{12,4},{16,24},{20,28},{24,16},{28,20},{1,9},{5... | collective-permute-start | bytes 1327112 | tf_op jit(solution)/shard_map/ppermute | solution.py:673
  19.3 37.5 %collective-permute-start.5 = (bf16[192,1152]{1,0:T(8,128)(2,1)}, bf16[192,1152]{1,0:T(8,128)(2,1)}, u32[]{:S(2)}, u32[]{:S(2)}) collective-permute-start(bf16[192,1152]{1,0:T(8,128)(2,1)} %concatenate.26.refs_5_), channel_id=1, source_target_pairs={{0,16},{4,20},{8,24},{12,28},{16,0},{20,4},{24,8},{28,12},{1,17},{... | collective-permute-start | bytes 1327112 | tf_op jit(solution)/shard_map/ppermute | solution.py:673
  30.7 26.1 %collective-permute-start.2 = (bf16[128,1536]{1,0:T(8,128)(2,1)S(1)}, bf16[128,1536]{1,0:T(8,128)(2,1)}, u32[]{:S(2)}, u32[]{:S(2)}) collective-permute-start(bf16[128,1536]{1,0:T(8,128)(2,1)S(1)} %slice.175), channel_id=1, source_target_pairs={{0,2},{1,3},{2,0},{3,1},{4,6},{5,7},{6,4},{7,5},{8,10},{9,11},{10,... | collective-permute-start | bytes 1179656 | tf_op jit(solution)/shard_map/ppermute | solution.py:679
  32.6 24.2 %collective-permute-start.3 = (bf16[128,1536]{1,0:T(8,128)(2,1)S(1)}, bf16[128,1536]{1,0:T(8,128)(2,1)}, u32[]{:S(2)}, u32[]{:S(2)}) collective-permute-start(bf16[128,1536]{1,0:T(8,128)(2,1)S(1)} %slice.176), channel_id=1, source_target_pairs={{0,1},{1,0},{2,3},{3,2},{4,5},{5,4},{6,7},{7,6},{8,9},{9,8},{10,11... | collective-permute-start | bytes 1179656 | tf_op jit(solution)/shard_map/ppermute | solution.py:679
  59.0 290.0 %reduce-scatter.2.cloned.1.call-start = ((), (), s32[]{:S(2)}) async-start(), calls=%async_computation.2 | async-start | bytes 3932160 | tf_op jit(solution)/shard_map/reduce_scatter | solution.py:729
  62.1 29.5 %collective-permute-start.11 = (bf16[192,768]{1,0:T(8,128)(2,1)}, bf16[192,768]{1,0:T(8,128)(2,1)S(1)}, u32[]{:S(2)}, u32[]{:S(2)}) collective-permute-start(bf16[192,768]{1,0:T(8,128)(2,1)} %copied.3.refs_0_), channel_id=1, source_target_pairs={{0,8},{4,12},{8,0},{12,4},{16,24},{20,28},{24,16},{28,20},{1,9},{5... | collective-permute-start | bytes 884744 | tf_op jit(solution)/shard_map/ppermute | solution.py:673
  62.1 29.5 %collective-permute-start.12 = (bf16[192,768]{1,0:T(8,128)(2,1)}, bf16[192,768]{1,0:T(8,128)(2,1)S(1)}, u32[]{:S(2)}, u32[]{:S(2)}) collective-permute-start(bf16[192,768]{1,0:T(8,128)(2,1)} %copied.3.refs_0_), channel_id=1, source_target_pairs={{0,16},{4,20},{8,24},{12,28},{16,0},{20,4},{24,8},{28,12},{1,17},{... | collective-permute-start | bytes 884744 | tf_op jit(solution)/shard_map/ppermute | solution.py:673
  65.1 26.5 %collective-permute-start.13 = (bf16[192,768]{1,0:T(8,128)(2,1)}, bf16[192,768]{1,0:T(8,128)(2,1)S(1)}, u32[]{:S(2)}, u32[]{:S(2)}) collective-permute-start(bf16[192,768]{1,0:T(8,128)(2,1)} %copied.3.refs_0_), channel_id=1, source_target_pairs={{0,24},{4,28},{8,16},{12,20},{16,8},{20,12},{24,0},{28,4},{1,25},{... | collective-permute-start | bytes 884744 | tf_op jit(solution)/shard_map/ppermute | solution.py:673
  117.9 19.1 %collective-permute-start.21 = (bf16[192,768]{1,0:T(8,128)(2,1)}, bf16[192,768]{1,0:T(8,128)(2,1)S(1)}, u32[]{:S(2)}, u32[]{:S(2)}) collective-permute-start(bf16[192,768]{1,0:T(8,128)(2,1)} %copied.5.refs_0_), channel_id=1, source_target_pairs={{0,8},{4,12},{8,0},{12,4},{16,24},{20,28},{24,16},{28,20},{1,9},{5... | collective-permute-start | bytes 884744 | tf_op jit(solution)/shard_map/ppermute | solution.py:673
  117.9 23.9 %collective-permute-start.22 = (bf16[192,768]{1,0:T(8,128)(2,1)}, bf16[192,768]{1,0:T(8,128)(2,1)}, u32[]{:S(2)}, u32[]{:S(2)}) collective-permute-start(bf16[192,768]{1,0:T(8,128)(2,1)} %copied.5.refs_0_), channel_id=1, source_target_pairs={{0,16},{4,20},{8,24},{12,28},{16,0},{20,4},{24,8},{28,12},{1,17},{... | collective-permute-start | bytes 884744 | tf_op jit(solution)/shard_map/ppermute | solution.py:673
  120.9 20.9 %collective-permute-start.23 = (bf16[192,768]{1,0:T(8,128)(2,1)}, bf16[192,768]{1,0:T(8,128)(2,1)}, u32[]{:S(2)}, u32[]{:S(2)}) collective-permute-start(bf16[192,768]{1,0:T(8,128)(2,1)} %copied.5.refs_0_), channel_id=1, source_target_pairs={{0,24},{4,28},{8,16},{12,20},{16,8},{20,12},{24,0},{28,4},{1,25},{... | collective-permute-start | bytes 884744 | tf_op jit(solution)/shard_map/ppermute | solution.py:673
  137.0 42.4 %collective-permute-start.32 = (bf16[4,192,768]{2,1,0:T(8,128)(2,1)}, bf16[4,192,768]{2,1,0:T(8,128)(2,1)}, u32[]{:S(2)}, u32[]{:S(2)}) collective-permute-start(bf16[4,192,768]{2,1,0:T(8,128)(2,1)} %get-tuple-element.76.refs_4_), channel_id=1, source_target_pairs={{0,4},{4,0},{8,12},{12,8},{16,20},{20,16},{24,28},{28,24},{1,5},{5... | collective-permute-start | bytes 3538952 | tf_op jit(solution)/shard_map/ppermute | solution.py:676
  184.1 28.6 %collective-permute-start.33 = (bf16[192,768]{1,0:T(8,128)(2,1)}, bf16[192,768]{1,0:T(8,128)(2,1)S(1)}, u32[]{:S(2)}, u32[]{:S(2)}) collective-permute-start(bf16[192,768]{1,0:T(8,128)(2,1)} %get-tuple-element.97), channel_id=1, source_target_pairs={{0,8},{4,12},{8,0},{12,4},{16,24},{20,28},{24,16},{28,20},{1,9},{5... | collective-permute-start | bytes 884744 | tf_op jit(solution)/shard_map/ppermute | solution.py:673
  189.2 23.7 %collective-permute-start.34 = (bf16[192,768]{1,0:T(8,128)(2,1)}, bf16[192,768]{1,0:T(8,128)(2,1)}, u32[]{:S(2)}, u32[]{:S(2)}) collective-permute-start(bf16[192,768]{1,0:T(8,128)(2,1)} %get-tuple-element.98), channel_id=1, source_target_pairs={{0,16},{4,20},{8,24},{12,28},{16,0},{20,4},{24,8},{28,12},{1,17},{... | collective-permute-start | bytes 884744 | tf_op jit(solution)/shard_map/ppermute | solution.py:673
  190.1 22.9 %collective-permute-start.35 = (bf16[192,768]{1,0:T(8,128)(2,1)}, bf16[192,768]{1,0:T(8,128)(2,1)}, u32[]{:S(2)}, u32[]{:S(2)}) collective-permute-start(bf16[192,768]{1,0:T(8,128)(2,1)} %get-tuple-element.99), channel_id=1, source_target_pairs={{0,24},{4,28},{8,16},{12,20},{16,8},{20,12},{24,0},{28,4},{1,25},{... | collective-permute-start | bytes 884744 | tf_op jit(solution)/shard_map/ppermute | solution.py:673
  216.7 24.5 %collective-permute-start.36 = (bf16[192,768]{1,0:T(8,128)(2,1)}, bf16[192,768]{1,0:T(8,128)(2,1)}, u32[]{:S(2)}, u32[]{:S(2)}) collective-permute-start(bf16[192,768]{1,0:T(8,128)(2,1)} %get-tuple-element.106), channel_id=1, source_target_pairs={{0,8},{4,12},{8,0},{12,4},{16,24},{20,28},{24,16},{28,20},{1,9},{5... | collective-permute-start | bytes 884744 | tf_op jit(solution)/shard_map/ppermute | solution.py:673
  222.3 23.8 %collective-permute-start.37 = (bf16[192,768]{1,0:T(8,128)(2,1)}, bf16[192,768]{1,0:T(8,128)(2,1)}, u32[]{:S(2)}, u32[]{:S(2)}) collective-permute-start(bf16[192,768]{1,0:T(8,128)(2,1)} %get-tuple-element.107), channel_id=1, source_target_pairs={{0,16},{4,20},{8,24},{12,28},{16,0},{20,4},{24,8},{28,12},{1,17},{... | collective-permute-start | bytes 884744 | tf_op jit(solution)/shard_map/ppermute | solution.py:673
  223.2 22.9 %collective-permute-start.38 = (bf16[192,768]{1,0:T(8,128)(2,1)}, bf16[192,768]{1,0:T(8,128)(2,1)}, u32[]{:S(2)}, u32[]{:S(2)}) collective-permute-start(bf16[192,768]{1,0:T(8,128)(2,1)} %get-tuple-element.108), channel_id=1, source_target_pairs={{0,24},{4,28},{8,16},{12,20},{16,8},{20,12},{24,0},{28,4},{1,25},{... | collective-permute-start | bytes 884744 | tf_op jit(solution)/shard_map/ppermute | solution.py:673
  256.6 44.9 %collective-permute-start.50 = (bf16[4,192,1152]{2,1,0:T(8,128)(2,1)}, bf16[4,192,1152]{2,1,0:T(8,128)(2,1)}, u32[]{:S(2)}, u32[]{:S(2)}) collective-permute-start(bf16[4,192,1152]{2,1,0:T(8,128)(2,1)} %get-tuple-element.109.refs_5_), channel_id=1, source_target_pairs={{0,4},{4,0},{8,12},{12,8},{16,20},{20,16},{24,28},{28,24},{1,5},{5... | collective-permute-start | bytes 5308424 | tf_op jit(solution)/shard_map/ppermute | solution.py:676
  304.5 33.0 %collective-permute-start.52 = (bf16[192,1152]{1,0:T(8,128)(2,1)S(1)}, bf16[192,1152]{1,0:T(8,128)(2,1)S(1)}, u32[]{:S(2)}, u32[]{:S(2)}) collective-permute-start(bf16[192,1152]{1,0:T(8,128)(2,1)S(1)} %get-tuple-element.150), channel_id=1, source_target_pairs={{0,16},{4,20},{8,24},{12,28},{16,0},{20,4},{24,8},{28,12},{1,17},{... | collective-permute-start | bytes 1327112 | tf_op jit(solution)/shard_map/ppermute | solution.py:673
  306.7 30.8 %collective-permute-start.53 = (bf16[192,1152]{1,0:T(8,128)(2,1)S(1)}, bf16[192,1152]{1,0:T(8,128)(2,1)S(1)}, u32[]{:S(2)}, u32[]{:S(2)}) collective-permute-start(bf16[192,1152]{1,0:T(8,128)(2,1)S(1)} %get-tuple-element.149), channel_id=1, source_target_pairs={{0,24},{4,28},{8,16},{12,20},{16,8},{20,12},{24,0},{28,4},{1,25},{... | collective-permute-start | bytes 1327112 | tf_op jit(solution)/shard_map/ppermute | solution.py:673
  (118 other events, 864.8 us)
Sparse Core Ops, SparseCore 0:
  59.1 42.2 all-gather.1
  178.9 47.6 reduce-scatter.1

commit v3 on v2

v3 whole, which is shorter than its diff:
```python
import functools

import jax
import jax.numpy as jnp
from jax import lax
from jax.experimental import pallas as pl
from jax.experimental.pallas import tpu as pltpu
from jax.sharding import PartitionSpec as P

DI = 3072
epsilon = 1e-05
HEAD_DIM = 64
STATE = 128
CONV = 4
SEQ = 1024
SPAN = 256
CHUNK = 128
LANES = 128
NEVER = -1e30
NEAR = jax.ShapeDtypeStruct
f32 = jnp.float32
bf16 = jnp.bfloat16
highest = lax.Precision.HIGHEST


def dot(first, second, first_dim=1, second_dim=0, precision=None):
    return lax.dot_general(
        first,
        second,
        (((first_dim,), (second_dim,)), ((), ())),
        precision=precision,
        preferred_element_type=f32,
    )


def sigmoid(values):
    return 0.5 * jnp.tanh(0.5 * values) + 0.5


def places(dim):
    return lax.broadcasted_iota(jnp.int32, (CHUNK, LANES), dim)


def decays(step_raw, heads_ref):
    raw = step_raw + heads_ref[0:1]
    small = jnp.exp(-jnp.abs(raw))
    log_one = jnp.where(small < 1e-3, small - 0.5 * small * small, jnp.log(1.0 + small))
    steps = jnp.maximum(raw, 0.0) + log_one
    upto = (places(0) >= places(1)).astype(f32)
    summed = dot(upto, steps * heads_ref[1:2], precision=highest)
    return steps, sigmoid(raw), summed, summed - jnp.log(steps)


def pair_of(first, second):
    return jnp.concatenate([first, second], axis=0)


def forward_kernel(raw_ref, taps_ref, heads_ref, skip_ref, *refs):
    scanned_ref, pre_ref, states_ref, state, before = refs[-5:]
    chunk = pl.program_id(0)
    channels = skip_ref.shape[1]
    width = channels + 2 * STATE

    @pl.when(chunk % (SEQ // CHUNK) == 0)
    def _():
        state[...] = jnp.zeros_like(state)
        before[...] = jnp.zeros_like(before)

    raw = raw_ref[:, :width]
    extended = jnp.concatenate([before[...], raw], axis=0)
    pre = taps_ref[CONV : CONV + 1] + taps_ref[CONV - 1 : CONV] * raw
    for tap in range(CONV - 1):
        start = 8 - (CONV - 1) + tap
        pre = pre + taps_ref[tap : tap + 1] * extended[start : start + CHUNK]
    before[...] = raw[CHUNK - 8 :]
    pre_ref[...] = pre
    act = (pre * sigmoid(pre)).astype(bf16)
    writes = act[:, channels : channels + STATE]
    reads = act[:, channels + STATE :]
    _, _, summed, shifted = decays(raw_ref[:, width:], heads_ref)
    summed_t, shifted_t = summed.T, shifted.T
    tail_t = jnp.exp(summed_t[:, CHUNK - 1 :] - shifted_t)
    scores = dot(reads, writes, 1, 1)
    writes_t = writes.astype(f32).T
    causal = places(0) >= places(1)
    left = places(1) < HEAD_DIM
    states_ref[...] = state[...].astype(bf16)
    for pair in range(channels // LANES):
        cols = slice(pair * LANES, (pair + 1) * LANES)
        values = act[:, cols].astype(f32)
        both = pair_of(jnp.where(left, values, 0.0), jnp.where(left, 0.0, values)).astype(bf16)
        mixes, tails, grown = [], [], []
        for head in (2 * pair, 2 * pair + 1):
            here = jnp.broadcast_to(summed[:, head : head + 1], (CHUNK, LANES))
            decay = jnp.exp(jnp.where(causal, here - shifted_t[head : head + 1], NEVER))
            mixes.append((scores * decay).astype(bf16))
            tails.append((writes_t * tail_t[head : head + 1]).astype(bf16))
            grown.append(here)
        stacked = pair_of(jnp.concatenate(mixes, axis=1), jnp.concatenate(tails, axis=1))
        out = dot(stacked, both)
        entering = state[:, cols]
        factor = jnp.exp(jnp.where(left, grown[0], grown[1]))
        across = dot(reads, entering.astype(bf16)) * factor
        scanned_ref[:, cols] = out[:CHUNK] + across + values * skip_ref[:, cols]
        state[:, cols] = entering * factor[CHUNK - 1 :] + out[CHUNK:]


def backward_kernel(part, n_deps, *refs):
    raw_ref, pre_ref, grad_ref, states_ref, taps_ref, heads_ref, skip_ref = refs[:7]
    n_held = 5 if part else 0
    held, refs = refs[7 : 7 + n_held], refs[7 + n_held + n_deps :]
    low_ref, sums_ref, head_sums_ref, carry, after, wide = refs
    step = pl.program_id(0)
    channels = skip_ref.shape[1]
    width = channels + 2 * STATE

    @pl.when(step == 0)
    def _():
        if part:
            for ref, source in zip((sums_ref, head_sums_ref, carry, after), held[1:], strict=True):
                ref[...] = source[...]
        else:
            sums_ref[...] = jnp.zeros_like(sums_ref)
            head_sums_ref[...] = jnp.zeros_like(head_sums_ref)

    @pl.when((step + part * pl.num_programs(0)) % (SEQ // CHUNK) == 0)
    def _():
        carry[...] = jnp.zeros_like(carry)
        after[...] = jnp.zeros_like(after)

    pre = pre_ref[...]
    gate = sigmoid(pre)
    act = (pre * gate).astype(bf16)
    writes = act[:, channels : channels + STATE]
    reads = act[:, channels + STATE :]
    steps, slopes, summed, shifted = decays(raw_ref[:, width:], heads_ref)
    summed_t = summed.T
    scores_t = dot(writes, reads, 1, 1)
    causal = places(0) <= places(1)
    earlier = places(0) < places(1)
    suffix = (places(0) >= places(1)).astype(bf16)
    left = places(1) < HEAD_DIM
    score_grads = jnp.zeros((CHUNK, LANES), f32)
    spans, inner_grads = [], []
    for pair in range(channels // LANES):
        cols = slice(pair * LANES, (pair + 1) * LANES)
        values = act[:, cols].astype(f32)
        both = pair_of(jnp.where(left, values, 0.0), jnp.where(left, 0.0, values)).astype(bf16)
        grad_low = grad_ref[:, cols]
        grad = grad_low.astype(f32)
        grad_both = pair_of(jnp.where(left, grad, 0.0), jnp.where(left, 0.0, grad)).astype(bf16)
        products = dot(both, grad_low, 1, 1)
        mixes, crossing, grown, tails = [], [], [], []
        for place, head in enumerate((2 * pair, 2 * pair + 1)):
            here = jnp.broadcast_to(shifted[:, head : head + 1], (CHUNK, LANES))
            decay = jnp.exp(jnp.where(causal, summed_t[head : head + 1] - here, NEVER))
            product = products[place * CHUNK : (place + 1) * CHUNK]
            score_grads = score_grads + decay * product
            mix = scores_t * decay
            mixes.append(mix.astype(bf16))
            crossing.append((mix * product).astype(bf16))
            level = jnp.broadcast_to(summed[:, head : head + 1], (CHUNK, LANES))
            grown.append(level)
            tails.append(level[CHUNK - 1 :] - here)
        sums = dot(pair_of(*crossing), suffix)
        for place in range(2):
            piece = jnp.where(earlier, sums[place * CHUNK : (place + 1) * CHUNK], 0.0)
            spans.append(jnp.sum(piece, axis=0, keepdims=True))
        within = dot(jnp.concatenate(mixes, axis=1), grad_both)
        factor = jnp.exp(jnp.where(left, grown[0], grown[1]))
        tail = jnp.exp(jnp.where(left, tails[0], tails[1]))
        leaving = carry[:, cols]
        entering = states_ref[:, cols]
        later = tail * dot(writes, leaving.astype(bf16))
        both_grads = within + later
        inner_grads.append(both_grads + skip_ref[:, cols] * grad)
        spread = factor * grad
        spread_low = spread.astype(bf16)
        wide[0:CHUNK, cols] = spread_low
        wide[CHUNK : 2 * CHUNK, cols] = (tail * values).astype(bf16)
        wide[2 * CHUNK : 3 * CHUNK, cols] = (spread * dot(reads, entering)).astype(bf16)
        wide[3 * CHUNK : 4 * CHUNK, cols] = (values * later).astype(bf16)
        wide[4 * CHUNK : 5 * CHUNK, cols] = (values * both_grads).astype(bf16)
        held = jnp.sum(entering.astype(f32) * leaving, axis=0, keepdims=True) * factor[CHUNK - 1 :]
        sums_ref[CONV + 1 : CONV + 2, cols] += jnp.sum(grad * values, axis=0, keepdims=True)
        sums_ref[CONV + 2 : CONV + 3, cols] = held
    reads_t = reads.astype(f32).T.astype(bf16)
    score_low = score_grads.astype(bf16)
    spread_all = wide[0:CHUNK, :]
    read_grads = dot(score_low, writes, 0, 0) + dot(spread_all, states_ref[...], 1, 1)
    write_grads = dot(score_low, reads) + dot(wide[CHUNK : 2 * CHUNK, :], carry[...].astype(bf16), 1, 1)
    last = jnp.exp(summed[CHUNK - 1 :])
    of_head = (
        lax.broadcasted_iota(jnp.int32, (channels, LANES), 0) // HEAD_DIM
        == lax.broadcasted_iota(jnp.int32, (channels, LANES), 1)
    )
    reduced = dot(wide[2 * CHUNK : 5 * CHUNK, :], of_head.astype(bf16))
    held_rows = jnp.broadcast_to(sums_ref[CONV + 2 : CONV + 3, :channels], (8, channels))
    held_heads = dot(held_rows, of_head.astype(f32), precision=highest)[0:1]
    lasts = dot(jnp.broadcast_to(last, (8, LANES)), of_head.astype(f32), 1, 1, precision=highest)[0:1]
    carry[...] = carry[...] * lasts + dot(reads_t, spread_all)
    across_sums, later_sums, both_sums = reduced[:CHUNK], reduced[CHUNK : 2 * CHUNK], reduced[2 * CHUNK :]
    span_rows = jnp.concatenate(spans + [jnp.zeros((LANES - len(spans), LANES), f32)], axis=0)
    log_grads = (
        dot((places(0) <= places(1)).astype(f32), across_sums, precision=highest)
        + dot((places(0) > places(1)).astype(f32), later_sums, precision=highest)
        + span_rows.T
        + held_heads
    )
    ratio = jnp.where(steps > 1e-30, slopes / steps, 1.0)
    step_grads = both_sums * ratio + heads_ref[1:2] * log_grads * slopes
    head_sums_ref[0:1] += jnp.sum(step_grads, axis=0, keepdims=True)
    head_sums_ref[1:2] += jnp.sum(log_grads * steps, axis=0, keepdims=True)

    @pl.when(part * pl.num_programs(0) + step == 2 * pl.num_programs(0) - 1)
    def _():
        skip_rows = jnp.broadcast_to(sums_ref[CONV + 1 : CONV + 2, :channels], (8, channels))
        head_sums_ref[2:3] = dot(skip_rows, of_head.astype(f32), precision=highest)[0:1]

    raw = raw_ref[:, :width]
    act_grads = jnp.concatenate(inner_grads + [write_grads, read_grads], axis=1)
    pre_grads = act_grads * (gate * (1.0 + pre * (1.0 - gate)))
    extended = jnp.concatenate([pre_grads, after[...]], axis=0)
    after[...] = pre_grads[:8]
    sums_ref[CONV : CONV + 1] += jnp.sum(pre_grads, axis=0, keepdims=True)
    raw_grads = taps_ref[CONV - 1 : CONV] * pre_grads
    sums_ref[CONV - 1 : CONV] += jnp.sum(raw * pre_grads, axis=0, keepdims=True)
    for tap in range(CONV - 1):
        moved = extended[CONV - 1 - tap : CONV - 1 - tap + CHUNK]
        raw_grads = raw_grads + taps_ref[tap : tap + 1] * moved
        sums_ref[tap : tap + 1] += jnp.sum(raw * moved, axis=0, keepdims=True)
    low_ref[:, :width] = raw_grads.astype(bf16)
    low_ref[:, width:] = step_grads.astype(bf16)


def stay(values):
    return pltpu.with_memory_space_constraint(values, pltpu.HBM)


def scan_forward(raw, taps, heads, skip, earlier):
    tokens, full = raw.shape
    channels = skip.shape[1]
    width = channels + 2 * STATE
    count = tokens // CHUNK
    by_chunk = lambda shape: pl.BlockSpec(shape, lambda s: (s, 0))
    whole = lambda v: pl.BlockSpec(v.shape, lambda s: (0, 0))
    return pl.pallas_call(
        forward_kernel,
        grid=(count,),
        in_specs=[by_chunk((CHUNK, full)), whole(taps), whole(heads), whole(skip)]
        + [pl.BlockSpec(memory_space=pl.ANY)] * len(earlier),
        out_specs=[
            by_chunk((CHUNK, channels)),
            by_chunk((CHUNK, width)),
            by_chunk((STATE, channels)),
        ],
        scratch_shapes=[pltpu.VMEM((STATE, channels), f32), pltpu.VMEM((8, width), f32)],
        out_shape=[
            pltpu.HBM((tokens, channels), f32),
            pltpu.HBM((tokens, width), f32),
            pltpu.HBM((count * STATE, channels), bf16),
        ],
        compiler_params=pltpu.CompilerParams(vmem_limit_bytes=20 << 20),
        name="scan_forward",
    )(stay(raw), taps, heads, skip, *earlier)


def scan_backward(part, raw, pre, grad, states, taps, heads, skip, held, earlier):
    tokens, full = raw.shape
    channels = skip.shape[1]
    width = channels + 2 * STATE
    count = tokens // CHUNK
    half = count // 2
    last = count - 1 - part * half
    by_chunk = lambda shape: pl.BlockSpec(shape, lambda s: (last - s, 0))
    whole = lambda shape: pl.BlockSpec(shape, lambda s: (0, 0))
    kept = [(8, width), (8, LANES), (STATE, channels), (8, width)]
    free = pl.BlockSpec(memory_space=pl.ANY)
    held = list(held) if part else []
    return pl.pallas_call(
        functools.partial(backward_kernel, part, len(earlier)),
        grid=(half,),
        in_specs=[
            by_chunk((CHUNK, full)),
            by_chunk((CHUNK, width)),
            by_chunk((CHUNK, channels)),
            by_chunk((STATE, channels)),
            whole(taps.shape),
            whole(heads.shape),
            whole(skip.shape),
        ]
        + ([free] + [whole(shape) for shape in kept] if part else [])
        + [free] * len(earlier),
        out_specs=[by_chunk((CHUNK, full))] + [whole(shape) for shape in kept],
        scratch_shapes=[pltpu.VMEM((5 * CHUNK, channels), bf16)],
        out_shape=[pltpu.HBM((tokens, full), bf16)] + [pltpu.HBM(shape, f32) for shape in kept],
        input_output_aliases={7: 0} if part else {},
        compiler_params=pltpu.CompilerParams(vmem_limit_bytes=20 << 20),
        name=f"scan_backward_{part}",
    )(stay(raw), stay(pre), stay(grad), stay(states), taps, heads, skip, *[stay(v) for v in held], *earlier)


BLOCK = 256
LIMIT = 24 << 20
SMALL = 16
anywhere = pl.BlockSpec(memory_space=pl.ANY)
in_vmem = pl.BlockSpec(memory_space=pltpu.VMEM)


def column_sums(values, count):
    rows = [
        jnp.sum(values[i * LANES : (i + 1) * LANES].T, axis=0, keepdims=True)
        for i in range(count // LANES)
    ]
    return jnp.concatenate(rows, axis=0)


def fold(values):
    total = values[:, :LANES]
    for start in range(LANES, values.shape[1], LANES):
        total = total + values[:, start : start + LANES]
    return total


def shard_rows(place, index, chips, height):
    core, chip = index // chips, index % chips
    return pl.multiple_of(((place[0] ^ chip) * 2 + (place[1] ^ core)) * height, height)


def row_start(place, start):
    if isinstance(start, int):
        return pl.multiple_of((start // BLOCK ^ place[2]) * BLOCK + start % BLOCK, LANES)
    return pl.multiple_of((start // BLOCK ^ place[2]) * BLOCK, BLOCK)


def product_kernel(layout, chips, epilogue, place, *refs):
    heights, keep_rows, n_extra, n_deps, n_out = layout
    n_rows, n_full = len(heights), 2 * chips
    row_refs, refs = refs[:n_rows], refs[n_rows:]
    full_refs, refs = refs[:n_full], refs[n_full:]
    extra, refs = refs[:n_extra], refs[n_extra + n_deps :]
    outs, refs = refs[:n_out], refs[n_out:]
    full_out, refs = refs[0], refs[1:]
    if keep_rows:
        rows_out, refs = refs[0], refs[1:]
    rows, full, sems, back = refs
    step = pl.program_id(0)
    starts = [sum(heights[:i]) for i in range(n_rows)]
    shard = full.shape[0] // n_full
    row_copies = [
        pltpu.make_async_copy(
            row_refs[i], rows.at[pl.ds(row_start(place, starts[i]), heights[i])], sems.at[i]
        )
        for i in range(n_rows)
    ]
    full_copies = [
        pltpu.make_async_copy(
            full_refs[i], full.at[pl.ds(shard_rows(place, i, chips, shard), shard)], sems.at[n_rows + i]
        )
        for i in range(n_full)
    ]
    backs = [pltpu.make_async_copy(full, full_out, back.at[0])]

    @pl.when(step == 0)
    def _():
        for copy in full_copies + row_copies:
            copy.start()
        for copy in full_copies:
            copy.wait()
        backs[0].start()

    for i in range(n_rows):

        @pl.when(step == starts[i] // BLOCK)
        def _(i=i):
            row_copies[i].wait()

    if keep_rows:
        backs.append(pltpu.make_async_copy(rows, rows_out, back.at[1]))

        @pl.when(step == starts[-1] // BLOCK)
        def _():
            backs[1].start()

    block = rows[pl.ds(row_start(place, step * BLOCK), BLOCK), :]
    epilogue(step ^ place[2], block, full, extra, outs)

    @pl.when(step == pl.num_programs(0) - 1)
    def _():
        for copy in backs:
            copy.wait()


def product(place, row_pieces, full_pieces, epilogue, extra, outs, name, earlier=()):
    chips = len(full_pieces) // 2
    heights = tuple(piece.shape[0] for piece in row_pieces)
    tokens, depth = sum(heights), row_pieces[0].shape[1]
    columns = full_pieces[0].shape[1]
    by_block = lambda cols: pl.BlockSpec((BLOCK, cols), lambda s, p: (s ^ p[2], 0))
    whole = lambda shape: pl.BlockSpec(shape, lambda s, p: (0, 0))
    out_specs, out_shape = [], []
    for cols, dtype in outs:
        if cols is None:
            out_specs.append(whole((dtype * tokens // LANES, LANES)))
            out_shape.append(jax.ShapeDtypeStruct((dtype * tokens // LANES, LANES), f32))
        else:
            out_specs.append(by_block(cols))
            out_shape.append((pltpu.HBM if name == "project" else NEAR)((tokens, cols), dtype))
    out_specs += [anywhere, anywhere]
    out_shape += [pltpu.HBM((depth, columns), bf16), pltpu.HBM((tokens, depth), bf16)]
    layout = (heights, True, len(extra), len(earlier), len(outs))
    return pl.pallas_call(
        functools.partial(product_kernel, layout, chips, epilogue),
        grid_spec=pltpu.PrefetchScalarGridSpec(
            num_scalar_prefetch=1,
            grid=(tokens // BLOCK,),
            in_specs=[anywhere] * (len(row_pieces) + len(full_pieces))
            + [by_block(v.shape[1]) if by else whole(v.shape) for v, by in extra]
            + [anywhere] * len(earlier),
            out_specs=out_specs,
            scratch_shapes=[
                pltpu.VMEM((tokens, depth), bf16),
                pltpu.VMEM((depth, columns), bf16),
                pltpu.SemaphoreType.DMA((len(row_pieces) + len(full_pieces),)),
                pltpu.SemaphoreType.DMA((2,)),
            ],
        ),
        out_shape=out_shape,
        compiler_params=pltpu.CompilerParams(vmem_limit_bytes=LIMIT),
        name=name,
    )(place, *[stay(v) for v in row_pieces + full_pieces], *[v for v, _ in extra], *earlier)


def slices(columns):
    return [slice(start, min(start + 256, columns)) for start in range(0, columns, 256)]


def raw_epilogue(index, block, full, extra, outs):
    (raw,) = outs
    for cols in slices(raw.shape[1]):
        raw[:, cols] = dot(block, full[:, cols])


def mix_epilogue(index, block, full, extra, outs):
    rows, scanned, gain = extra
    gate, gated, grad, sums = outs
    channels = gate.shape[1]
    squares = jnp.zeros((BLOCK, LANES), f32)
    dots = jnp.zeros((BLOCK, LANES), f32)
    for cols in slices(channels):
        value = dot(rows[...], full[:, cols])
        out = dot(block, full[:, channels + cols.start : channels + cols.stop])
        gate[:, cols] = value
        grad[:, cols] = out
        product = scanned[:, cols] * (value * sigmoid(value))
        gated[:, cols] = product
        squares = squares + fold(product * product)
        dots = dots + fold(out * gain[:, cols] * product)
    per = BLOCK // LANES
    half = sums.shape[0] // 2
    sums[pl.ds(index * per, per), :] = column_sums(squares, BLOCK)
    sums[pl.ds(half + index * per, per), :] = column_sums(dots, BLOCK)


def shard_kernel(gate_proj, out_proj, *refs):
    out = refs[-1]
    channels, height = out_proj.shape
    out[:, :channels] = gate_proj[...]
    place = [lax.broadcasted_iota(jnp.int32, (height, height), dim) for dim in range(2)]
    same = (place[0] == place[1]).astype(bf16)
    out[:, channels:] = dot(same, out_proj[...], 1, 1).astype(bf16)


def joint_shard(gate_proj, out_proj, earlier):
    return pl.pallas_call(
        shard_kernel,
        in_specs=[in_vmem] * 2 + [anywhere] * len(earlier),
        out_specs=in_vmem,
        out_shape=jax.ShapeDtypeStruct((gate_proj.shape[0], 2 * gate_proj.shape[1]), bf16),
        name="joint_shard",
    )(gate_proj, out_proj, *earlier)


def columns_of(row):
    return jnp.broadcast_to(row, (LANES, LANES)).T


def gating_kernel(grad_out, gated, scanned, gate, sums, gain, out_low, gate_back, scan_grad, gain_grad):
    step = pl.program_id(0)
    half = sums.shape[0] // 2

    @pl.when(step == 0)
    def _():
        gain_grad[...] = jnp.zeros_like(gain_grad)

    for part in range(BLOCK // LANES):
        rows = slice(part * LANES, (part + 1) * LANES)
        index = step * (BLOCK // LANES) + part
        ratio_row = lax.rsqrt(sums[pl.ds(index, 1), :] / DI + epsilon)
        dots = sums[pl.ds(half + index, 1), :]
        ratio = columns_of(ratio_row)
        pull = columns_of(ratio_row * ratio_row * ratio_row / DI * dots)
        for start in range(0, gate.shape[1], LANES):
            cols = slice(start, start + LANES)
            held, value = gated[rows, cols], gate[rows, cols]
            scaled = grad_out[rows, cols] * ratio
            out_low[rows, cols] = (gain[:, cols] * (held * ratio)).astype(bf16)
            gain_grad[0:1, cols] += jnp.sum(scaled * held, axis=0, keepdims=True)
            grad = gain[:, cols] * scaled - held * pull
            slope = sigmoid(value)
            scan_grad[rows, cols] = (grad * (value * slope)).astype(bf16)
            gate_grad = grad * scanned[rows, cols] * (slope * (1.0 + value * (1.0 - slope)))
            gate_back[rows, cols] = gate_grad.astype(bf16)


def gating(grad_out, gated, scanned, gate, sums, gain):
    tokens, columns = gated.shape
    block = pl.BlockSpec((BLOCK, columns), lambda s: (s, 0))
    whole = lambda v: pl.BlockSpec(v.shape, lambda s: (0, 0))
    return pl.pallas_call(
        gating_kernel,
        grid=(tokens // BLOCK,),
        in_specs=[block] * 4 + [whole(sums), whole(gain)],
        out_specs=[block] * 3 + [pl.BlockSpec((8, columns), lambda s: (0, 0))],
        out_shape=[NEAR((tokens, columns), bf16)] * 3 + [jax.ShapeDtypeStruct((8, columns), f32)],
        compiler_params=pltpu.CompilerParams(vmem_limit_bytes=LIMIT),
        name="gating",
    )(grad_out, gated, stay(scanned), gate, sums, gain)


def grads_kernel(n_rows, place, *refs):
    rows, lows = refs[:n_rows], refs[n_rows : 2 * n_rows]
    keep, give, acc = refs[-3:]
    wide = acc.shape[0]
    shard = wide // 2
    start = 0
    for row, low in zip(rows, lows, strict=True):
        for cols in slices(low.shape[1]):
            acc[:, start + cols.start : start + cols.stop] = dot(row[...], low[:, cols], 0, 0)
        start += low.shape[1]
    mine, other = (pl.multiple_of(core * shard, shard) for core in (place[1], 1 - place[1]))
    keep[0, :shard] = acc[pl.ds(mine, shard), :].astype(bf16)
    give[0, :shard] = acc[pl.ds(other, shard), :].astype(bf16)


def fill_small(small, sums, gain_grad, norm_grad, head_sums):
    rest = norm_grad.shape[1] - small.shape[1]
    small[...] = jnp.zeros_like(small)
    small[0:8, : sums.shape[1]] = sums[...]
    small[8:9, : gain_grad.shape[1]] = gain_grad[0:1, :]
    small[9:10, :] = norm_grad[0:1, : small.shape[1]]
    small[10:11, :rest] = norm_grad[0:1, small.shape[1] :]
    small[11:14, :LANES] = head_sums[0:3, :]


def small_kernel(n_rows, place, *refs):
    keep, give, small = refs[-4], refs[-3], refs[-1]
    grads_kernel(n_rows, place, *refs[:-1])
    fill_small(small, *refs[2 * n_rows : 2 * n_rows + 4])
    low = small[...].astype(bf16)
    shard = keep.shape[1] - SMALL
    keep[0, shard:] = low
    give[0, shard:] = low


def whole_grads_kernel(chips, n_rows, n_small, place, *refs):
    rows, lows = refs[:n_rows], refs[n_rows : 2 * n_rows]
    keep, give, acc, small = refs[-4:]
    depth = acc.shape[0]
    shard = depth // (2 * chips)
    start = 0
    for row, low in zip(rows, lows, strict=True):
        cols = slice(start, start + low.shape[1])
        for lanes in slices(depth):
            acc[lanes, cols] = dot(row[:, lanes], low[...], 0, 0)
        start = cols.stop
    for k in range(chips):
        for out, core in ((keep, place[1]), (give, 1 - place[1])):
            at = pl.multiple_of(((place[0] ^ k) * 2 + core) * shard, shard)
            out[k, :shard] = acc[pl.ds(at, shard), :].astype(bf16)
    if n_small:
        fill_small(small, *refs[2 * n_rows : 2 * n_rows + n_small])
        for k in range(chips):
            keep[k, shard:] = small[...].astype(bf16)
            give[k, shard:] = small[...].astype(bf16)


def weight_grads(place, chips, rows, lows, small, name, earlier=()):
    tokens, depth = rows[0].shape
    columns = sum(v.shape[1] for v in lows)
    wide = depth // chips
    shard = wide // 2
    height = shard + (SMALL if small else 0)
    if wide % LANES:
        return pl.pallas_call(
            functools.partial(whole_grads_kernel, chips, len(rows), len(small)),
            in_specs=[pl.BlockSpec(memory_space=pltpu.SMEM)]
            + [in_vmem] * (2 * len(rows) + len(small))
            + [anywhere] * len(earlier),
            out_specs=[in_vmem] * 2,
            out_shape=[jax.ShapeDtypeStruct((chips, height, columns), bf16)] * 2,
            scratch_shapes=[pltpu.VMEM((depth, columns), f32), pltpu.VMEM((SMALL, columns), f32)],
            compiler_params=pltpu.CompilerParams(vmem_limit_bytes=2 * LIMIT),
            name=name,
        )(place, *rows, *lows, *small, *earlier)
    out = pl.BlockSpec((1, height, columns), lambda k, p: (k, 0, 0))
    whole = lambda v: pl.BlockSpec(v.shape, lambda k, p: (0, 0))
    return pl.pallas_call(
        functools.partial(small_kernel if small else grads_kernel, len(rows)),
        grid_spec=pltpu.PrefetchScalarGridSpec(
            num_scalar_prefetch=1,
            grid=(chips,),
            in_specs=[pl.BlockSpec((tokens, wide), lambda k, p: (0, k ^ p[0]))] * len(rows)
            + [whole(v) for v in lows]
            + [whole(v) for v in small]
            + [anywhere] * len(earlier),
            out_specs=[out, out],
            scratch_shapes=[pltpu.VMEM((wide, columns), f32)]
            + ([pltpu.VMEM((SMALL, columns), f32)] if small else []),
        ),
        out_shape=[jax.ShapeDtypeStruct((chips, height, columns), bf16)] * 2,
        compiler_params=pltpu.CompilerParams(vmem_limit_bytes=LIMIT),
        name=name,
    )(place, *[stay(v) for v in rows], *lows, *small, *earlier)


def pairs_kernel(chips, *refs):
    keep, come, own, others = refs[0], refs[1], refs[-chips], refs[1 - chips :]
    own[...] = keep[0].astype(f32) + come[0].astype(f32)
    for k in range(1, chips):
        others[k - 1][...] = (keep[k].astype(f32) + come[k].astype(f32)).astype(bf16)


def pairs(keep, come, earlier=()):
    chips, rows, columns = keep.shape
    out = pl.pallas_call(
        functools.partial(pairs_kernel, chips),
        in_specs=[in_vmem, in_vmem] + [anywhere] * len(earlier),
        out_specs=[in_vmem] * chips,
        out_shape=[pltpu.HBM((rows, columns), f32)] + [pltpu.HBM((rows, columns), bf16)] * (chips - 1),
        compiler_params=pltpu.CompilerParams(vmem_limit_bytes=LIMIT),
        name="pairs",
    )(keep, come, *earlier)
    return out[0], list(out[1:])


def back_kernel(count, with_rows, place, *refs):
    lows, fulls, refs = refs[:count], refs[count : 2 * count], refs[2 * count :]
    rows, out, sums = (refs[0], refs[-2], refs[-1]) if with_rows else (None, refs[-1], None)
    if with_rows:

        @pl.when(pl.program_id(0) == 0)
        def _():
            sums[...] = jnp.zeros_like(sums)

    for cols in slices(out.shape[1]):
        value = dot(lows[0][...], fulls[0][cols, :], 1, 1)
        for low, full in zip(lows[1:], fulls[1:], strict=True):
            value = value + dot(low[...], full[cols, :], 1, 1)
        out[:, cols] = value.astype(bf16)
        if with_rows:
            sums[0:1, cols] += jnp.sum(value * rows[:, cols].astype(f32), axis=0, keepdims=True)


def back(place, lows, fulls, rows, name, earlier=()):
    tokens, depth = lows[0].shape[0], fulls[0][0].shape[0]
    by_block = lambda cols: pl.BlockSpec((BLOCK, cols), lambda s, p: (s ^ p[2], 0))
    whole = lambda shape: pl.BlockSpec(shape, lambda s, p: (0, 0))
    columns = lambda cols, i: pl.BlockSpec((depth, cols), lambda s, p: (0, i))
    extra = [] if rows is None else [stay(rows)]
    out = pl.pallas_call(
        functools.partial(back_kernel, len(lows), rows is not None),
        grid_spec=pltpu.PrefetchScalarGridSpec(
            num_scalar_prefetch=1,
            grid=(tokens // BLOCK,),
            in_specs=[by_block(v.shape[1]) for v in lows]
            + [columns(v.shape[1], i) for v, (_, i) in zip(lows, fulls, strict=True)]
            + [by_block(depth) for _ in extra]
            + [anywhere] * len(earlier),
            out_specs=[pl.BlockSpec((BLOCK, depth), lambda s, p: (s, 0))] + [whole((8, depth)) for _ in extra],
        ),
        out_shape=[jax.ShapeDtypeStruct((tokens, depth), bf16)]
        + [jax.ShapeDtypeStruct((8, depth), f32) for _ in extra],
        compiler_params=pltpu.CompilerParams(vmem_limit_bytes=LIMIT),
        name=name,
    )(place, *lows, *[stay(v) for v, _ in fulls], *extra, *earlier)
    return out[0], out[1] if extra else None


def add_up(parts, rows, cols):
    value = parts[0][rows, cols].astype(f32)
    for part in parts[1:]:
        value = value + part[rows, cols].astype(f32)
    return value


def collect_kernel(count, n_deps, *refs):
    parts = refs[:count]
    inner, step, taps, bias, gain, heads, common, rest = refs[count + n_deps :]
    shard, channels = inner.shape
    full = parts[0].shape[1]
    own = slice(0, shard)
    for start in range(0, channels, 256):
        cols = slice(start, min(start + 256, channels))
        inner[:, cols] = add_up(parts, own, cols)
    step[...] = add_up(parts, own, slice(full - LANES, full))
    shared = slice(channels, channels + 2 * STATE)
    common[0:shard] = add_up(parts, own, shared).astype(bf16)
    small = add_up(parts, slice(shard, shard + SMALL), slice(0, full))
    taps[...] = small[0:CONV, :channels]
    bias[...] = small[CONV : CONV + 1, :channels]
    gain[...] = small[8:9, :channels]
    heads[...] = jnp.zeros_like(heads)
    heads[0:3] = small[11:14, :LANES]
    rest[...] = jnp.zeros_like(rest)
    rest[0:8] = small[0:8, shared]
    for piece in range(12):
        row, start = divmod(piece * LANES, full)
        target = slice(piece % 2 * LANES, (piece % 2 + 1) * LANES)
        rest[8 + piece // 2 : 9 + piece // 2, target] = small[9 + row : 10 + row, start : start + LANES]
    common[shard:] = rest[...].astype(bf16)


def collect(parts, channels, earlier):
    rows = parts[0].shape[0]
    shapes = [
        (rows - SMALL, channels), (rows - SMALL, LANES), (CONV, channels), (1, channels), (1, channels), (8, LANES)
    ]
    return pl.pallas_call(
        functools.partial(collect_kernel, len(parts), len(earlier)),
        in_specs=[in_vmem] * len(parts) + [anywhere] * len(earlier),
        out_specs=[in_vmem] * 7,
        out_shape=[jax.ShapeDtypeStruct(shape, f32) for shape in shapes]
        + [jax.ShapeDtypeStruct((rows, 2 * STATE), bf16)],
        scratch_shapes=[pltpu.VMEM((SMALL, 2 * STATE), f32)],
        compiler_params=pltpu.CompilerParams(vmem_limit_bytes=LIMIT),
        name="collect",
    )(*parts, *earlier)


def finish_kernel(count, *refs):
    parts, norm_gain, (shared, taps, bias, norm) = refs[:count], refs[count], refs[count + 1 :]
    shard = shared.shape[0]
    every = slice(0, 2 * STATE)
    shared[...] = add_up(parts, slice(0, shard), every)
    small = add_up(parts, slice(shard, shard + SMALL), every)
    taps[...] = small[0:CONV]
    bias[...] = small[CONV : CONV + 1]
    for row in range(6):
        cols = slice(row * 2 * STATE, (row + 1) * 2 * STATE)
        norm[:, cols] = small[8 + row : 9 + row] / norm_gain[:, cols]


def finish(parts, norm_gain):
    rows = parts[0].shape[0]
    shapes = [(rows - SMALL, 2 * STATE), (CONV, 2 * STATE), (1, 2 * STATE), norm_gain.shape]
    return pl.pallas_call(
        functools.partial(finish_kernel, len(parts)),
        in_specs=[in_vmem] * (len(parts) + 1),
        out_specs=[in_vmem] * 4,
        out_shape=[jax.ShapeDtypeStruct(shape, f32) for shape in shapes],
        name="finish",
    )(*parts, norm_gain)


def nothing(*refs):
    pass


def pinned(values, earlier):
    anywhere = pl.BlockSpec(memory_space=pl.ANY)
    held = pl.pallas_call(
        nothing,
        in_specs=[anywhere] * (len(values) + len(earlier)),
        out_specs=[anywhere] * len(values),
        out_shape=[jax.ShapeDtypeStruct(v.shape, v.dtype) for v in values],
        input_output_aliases={i: i for i in range(len(values))},
        name="pinned",
    )(*values, *earlier)
    return list(held)


def copy_kernel(source, *refs):
    refs[-1][...] = source[...]


def copied(value, earlier):
    whole = pl.BlockSpec(memory_space=pltpu.VMEM)
    return pl.pallas_call(
        copy_kernel,
        in_specs=[whole] + [pl.BlockSpec(memory_space=pl.ANY)] * len(earlier),
        out_specs=whole,
        out_shape=jax.ShapeDtypeStruct(value.shape, value.dtype),
        name="copied",
    )(value, *earlier)


def total_of(own, arrived):
    for value in arrived:
        own = own + value.astype(f32)
    return own


class Net:
    def __init__(self, dp, tensor):
        self.dp, self.tensor = dp, tensor
        self.chips = dp // 2
        rank = lax.axis_index("tensor")
        at = lax.axis_index("dp")
        shift = rank if tensor == 4 else jnp.zeros_like(rank)
        self.place = jnp.stack([at // 2, at % 2, shift]).astype(jnp.int32)

    def over_chips(self, values, k):
        return lax.ppermute(values, "dp", [(i, i ^ (2 * k)) for i in range(self.dp)])

    def over_core(self, values):
        return lax.ppermute(values, "dp", [(i, i ^ 1) for i in range(self.dp)])

    def over_tensor(self, values, k):
        return lax.ppermute(values, "tensor", [(i, i ^ k) for i in range(self.tensor)])

    def between(self, values, pairs):
        return lax.ppermute(values, "dp", [(2 * a + c, 2 * b + c) for a, b in pairs for c in range(2)])

    def gather_near(self, shard):
        if self.chips != 4:
            return [shard] + [self.over_chips(shard, k) for k in range(1, self.chips)]
        return [shard, self.over_chips(shard, 1), self.over_chips(shard, 2)]

    def gather_far(self, near, earlier):
        if self.chips != 4:
            return pinned(near, earlier) if earlier else near
        near = pinned(near, earlier)
        middle = self.between(near[0], [(1, 2), (2, 1)])
        return near + [middle + self.between(near[2], [(1, 0), (2, 3)])]

    def gather_cores(self, mine):
        return mine + [self.over_core(piece) for piece in mine]

    def scatter_far(self, others):
        if self.chips != 4:
            return []
        return [self.between(others[2], [(0, 1), (3, 2)]), self.between(others[2], [(1, 2), (2, 1)])]

    def scatter_join(self, others, came):
        if self.chips != 4:
            return others
        return [others[0], (others[1].astype(f32) + came[0].astype(f32)).astype(bf16)]

    def scatter_near(self, joined, came):
        return came[1:] + [self.over_chips(value, k + 1) for k, value in enumerate(joined)]

    def gather_first(self, shard):
        if self.tensor != 4:
            return [lax.all_gather(shard, "tensor", axis=0, tiled=True)]
        return [shard, self.over_tensor(shard, 1), self.over_tensor(shard, 2)]

    def gather_last(self, pieces, earlier):
        if self.tensor != 4:
            return pieces
        half = BLOCK // 2
        halves = [pieces[1][:half], pieces[2][half:]]
        if earlier:
            halves = pinned(halves, earlier)
        return pieces + [self.over_tensor(halves[0], 2), self.over_tensor(halves[1], 1)]

    def scatter_first(self, rows, earlier):
        if self.tensor != 4:
            return []
        half = BLOCK // 2
        halves = [rows[3 * BLOCK : 3 * BLOCK + half], rows[3 * BLOCK + half :]]
        if earlier:
            halves = pinned(halves, earlier)
        return [self.over_tensor(halves[0], 2), self.over_tensor(halves[1], 1)]

    def scatter_blocks(self, rows, came):
        if self.tensor != 4:
            return [rows]
        half = BLOCK // 2
        own, one, two = rows[:BLOCK], rows[BLOCK : 2 * BLOCK], rows[2 * BLOCK : 3 * BLOCK]
        one = jnp.concatenate([(one[:half].astype(f32) + came[0].astype(f32)).astype(bf16), one[half:]])
        two = jnp.concatenate([two[:half], (two[half:].astype(f32) + came[1].astype(f32)).astype(bf16)])
        return [own, one, two]

    def scatter_last(self, blocks, earlier):
        if self.tensor != 4:
            return [lax.psum_scatter(blocks[0], "tensor", scatter_dimension=0, tiled=True)]
        came = [self.over_tensor(blocks[k], k) for k in (1, 2)]
        return [blocks[0]] + (pinned(came, earlier) if earlier else came)

    def spread_tensor(self, values):
        return [values] + [self.over_tensor(values, k) for k in range(1, self.tensor)]

    def sum_tensor(self, values):
        k = 1
        while k < self.tensor:
            values = values + self.over_tensor(values, k)
            k *= 2
        return values


def local(
    net_of,
    tokens,
    norm_gain,
    gate_proj,
    inner_proj,
    shared_proj,
    step_proj,
    conv_inner,
    conv_inner_bias,
    conv_shared,
    conv_shared_bias,
    step_bias,
    decay_log,
    skip_gain,
    out_gain,
    out_proj,
    cotangent,
):
    net = net_of()
    place, chips = net.place, net.chips
    channels = gate_proj.shape[1]
    heads = step_proj.shape[1]
    width = channels + 2 * STATE
    token_rows = tokens.astype(f32)
    inverse = lax.rsqrt(jnp.mean(token_rows * token_rows, axis=-1, keepdims=True) + epsilon)
    unit = token_rows * inverse
    normed_low = (unit * norm_gain).astype(bf16)
    padding = jnp.zeros((step_proj.shape[0], LANES - heads), bf16)
    scan_shard = jnp.concatenate([inner_proj, shared_proj, step_proj, padding], axis=1)
    scan_mine = net.gather_far(net.gather_near(scan_shard), [])
    row_pieces = net.gather_first(normed_low)
    reached = scan_mine[1:]
    joint = joint_shard(gate_proj, out_proj, row_pieces[1:2])
    row_pieces = net.gather_last(row_pieces, [])
    scan_pieces = net.gather_cores(pinned(scan_mine, row_pieces[3:]) if row_pieces[3:] else scan_mine)
    cot_pieces = net.gather_first(copied(cotangent, row_pieces[3:] + scan_pieces[chips:]))
    joint_mine = net.gather_near(pinned([joint], reached)[0])

    taps = jnp.concatenate(
        [
            jnp.concatenate([conv_inner, conv_inner_bias[None]]),
            jnp.concatenate([conv_shared, conv_shared_bias[None]]),
        ],
        axis=1,
    )
    taps = jnp.pad(taps, ((0, 8 - CONV - 1), (0, 0)))
    rates = -jnp.exp(decay_log)
    head_rows = jnp.pad(jnp.stack([step_bias, rates]), ((0, 6), (0, LANES - heads)))
    skip_row = jnp.repeat(skip_gain, HEAD_DIM)[None]
    gain = out_gain[None]

    raw, scan_full, rows = product(
        place,
        row_pieces,
        scan_pieces,
        raw_epilogue,
        [],
        [(width + LANES, f32)],
        "project",
    )
    scanned, pre, states = scan_forward(raw, taps, head_rows, skip_row, [])
    cot_pieces = net.gather_last(cot_pieces, [scanned])
    joint_mine = net.gather_far(joint_mine, [scanned])
    gate, gated, grad_out, token_sums, joint_full, cot_rows = product(
        place,
        cot_pieces,
        net.gather_cores(pinned(joint_mine, cot_pieces[3:])),
        mix_epilogue,
        [(stay(rows), True), (stay(scanned), True), (gain, False)],
        [(channels, f32), (channels, f32), (channels, f32), (None, 2)],
        "mix",
    )
    token_sums = net.sum_tensor(token_sums)
    out_low, gate_back, scan_grad, gain_grad = gating(grad_out, gated, scanned, gate, token_sums, gain)
    keep, give = weight_grads(
        place, chips, [rows, cot_rows], [gate_back, out_low], [], "grad_joint_proj"
    )
    joint_come = net.over_core(give)
    branch, _ = back(place, [out_low], [(joint_full, 1)], None, "branch", [give])
    joint_own, joint_others = pairs(keep, joint_come, [branch])
    came = net.scatter_far(joint_others)
    branch_came = net.scatter_first(branch, joint_others[:1])
    held = scan_backward(
        0, raw, pre, scan_grad, states, taps, head_rows, skip_row, None, joint_others[:1]
    )
    if came:
        *came, one, two = pinned(came + branch_came, [held[1]])
        branch_came = [one, two]
    joint_arrived = net.scatter_near(net.scatter_join(joint_others, came), came)
    branch_parts = net.scatter_last(net.scatter_blocks(branch, branch_came), [])
    scan_back, sums, head_sums, _, _ = scan_backward(
        1, raw, pre, scan_grad, states, taps, head_rows, skip_row, held, came
    )
    norm_rows, norm_sums = back(
        place, [gate_back, stay(scan_back)], [(joint_full, 0), (scan_full, 0)], rows, "grad_normed"
    )
    keep, give = weight_grads(
        place,
        chips,
        [rows],
        [stay(scan_back)],
        [sums, gain_grad, norm_sums, head_sums],
        "grad_scan_proj",
        joint_arrived + branch_parts[1:],
    )
    norm_came = net.scatter_first(norm_rows, joint_arrived)
    scan_own, scan_others = pairs(keep, net.over_core(give))
    norm_came = pinned(norm_came, scan_others[:1]) if norm_came else norm_came
    came = net.scatter_far(scan_others)
    joined = net.scatter_join(scan_others, came)
    scan_arrived = net.scatter_near(joined, came)
    norm_parts = net.scatter_last(net.scatter_blocks(norm_rows, norm_came), joined[1:])
    grad_normed = total_of(norm_parts[0].astype(f32), norm_parts[1:])
    mixed = total_of(token_rows, branch_parts).astype(bf16)
    joint_total = total_of(joint_own, joint_arrived)
    grad_gate_proj, grad_out_proj = joint_total[:, :channels], joint_total[:, channels:].T
    spread = grad_normed * norm_gain
    grad_tokens = (
        cotangent.astype(f32)
        + inverse * spread
        - unit * (inverse * jnp.mean(spread * unit, axis=-1, keepdims=True))
    )
    grad_inner_proj, step_part, grad_conv_inner, inner_bias, gain_part, head_part, common = collect(
        [scan_own] + scan_arrived, channels, []
    )
    grad_shared_proj, grad_conv_shared, shared_bias, norm_part = finish(
        net.spread_tensor(common), norm_gain[None]
    )
    return (
        mixed,
        grad_tokens,
        norm_part[0],
        grad_gate_proj,
        grad_inner_proj,
        grad_shared_proj,
        step_part[:, :heads],
        grad_conv_inner,
        inner_bias[0],
        grad_conv_shared,
        shared_bias[0],
        head_part[0, :heads],
        head_part[1, :heads] * rates,
        head_part[2, :heads],
        gain_part[0],
        grad_out_proj,
    )


def solution(mesh):
    dp, tensor = mesh.shape["dp"], mesh.shape["tensor"]

    def on_device(*args):
        return local(lambda: Net(dp, tensor), *args)

    return jax.shard_map(
        on_device,
        mesh=mesh,
        in_specs=(
            P(("dp", "tensor"), None),
            P(),
            P("dp", "tensor"),
            P("dp", "tensor"),
            P("dp", None),
            P("dp", "tensor"),
            P(None, "tensor"),
            P("tensor"),
            P(),
            P(),
            P("tensor"),
            P("tensor"),
            P("tensor"),
            P("tensor"),
            P("tensor", "dp"),
            P(("dp", "tensor"), None),
        ),
        out_specs=(
            P(("dp", "tensor"), None),
            P(("dp", "tensor"), None),
            P(),
            P("dp", "tensor"),
            P("dp", "tensor"),
            P("dp", None),
            P("dp", "tensor"),
            P(None, "tensor"),
            P("tensor"),
            P(),
            P(),
            P("tensor"),
            P("tensor"),
            P("tensor"),
            P("tensor"),
            P("tensor", "dp"),
        ),
        check_vma=False,
    )
```

time: 365 us -> 284 us (0.78); the launches traced: 360 us -> 283 us
  local copies, waits for them, and re-layouts: 57.8 us -> 21.5 us
  waiting for transfers between devices: 91.1 us -> 65 us
  Pallas kernels: 98.8 us -> 117 us
  starting transfers between devices: 68.9 us -> 55 us
  between operations: 14.9 us -> 1.46 us
  other arithmetic: 28.4 us -> 22.6 us
    unnamed x170 -> x133, local copies, waits for them, and re-layouts: 47.7 us -> 12 us
    ppermute x21 -> x8, starting transfers between devices: 40.6 us -> 15.8 us  [over_chips(): return lax.ppermute(values, 'dp', [(i, i ^ 2 * k) for i in range(self.dp)])]
    ppermute x20 -> x21, waiting for transfers between devices: 35.1 us -> 16.3 us  [over_tensor(): lax.ppermute(values, 'tensor', [(i, i ^ k) for i in range(self.tensor)])]
    ppermute x21 -> x8, waiting for transfers between devices: 51.4 us -> 32.6 us  [over_chips(): return lax.ppermute(values, 'dp', [(i, i ^ 2 * k) for i in range(self.dp)])]
    ppermute x0 -> x8, starting transfers between devices: none -> 12.6 us  [between(): lax.ppermute(values, 'dp', [(2 * a + c, 2 * b + c) for a, b in pairs for...]
    ppermute x0 -> x8, waiting for transfers between devices: none -> 12.4 us  [between(): lax.ppermute(values, 'dp', [(2 * a + c, 2 * b + c) for a, b in pairs for...]
    another operation x5 -> x1, other arithmetic: 11.4 us -> 0.08 us  [__init__(): self.place = jnp.stack([at // 2, at % 2, shift]).astype(jnp.int32)]
    pallas_call x4 -> x7, Pallas kernels: 21.7 us -> 30 us  [the longest x2 18.6 us: weight_grads(): pl.pallas_call(functools.partial(small_kernel if small else grads_kernel,...]
  transfers between devices with their start and end apart: 59 -> 47, of which waited for: 28 -> 18; matrix products, arithmetic and copies ran while one was open for 9% -> 11% of each run, Pallas kernels for 27% -> 27%
where the time goes in v3:
time: 284 us; the launch traced here: 283 us
  Pallas kernels  117 us (41%)
  waiting for transfers between devices  65 us (23%)
  starting transfers between devices  55 us (19%)
  other arithmetic  22.6 us (8%)
  local copies, waits for them, and re-layouts  21.5 us (8%)
    ppermute x8, waiting for transfers between devices, over_chips(): return lax.ppermute(values, 'dp', [(i, i ^ 2 * k) for i in range(self.dp)])  32.6 us
    pallas_call x2, Pallas kernels, scan_backward(): pl.pallas_call(functools.partial(backward_kernel, part, len(earlier)), gr...  30.6 us
    ppermute x21, starting transfers between devices, over_tensor(): lax.ppermute(values, 'tensor', [(i, i ^ k) for i in range(self.tensor)])  24.3 us
    pallas_call x2, Pallas kernels, product(): pl.pallas_call(functools.partial(product_kernel, layout, chips, epilogue)...  22.5 us
    pallas_call x2, Pallas kernels, weight_grads(): pl.pallas_call(functools.partial(small_kernel if small else grads_kernel,...  18.6 us
    pallas_call x2, Pallas kernels, back(): pl.pallas_call(functools.partial(back_kernel, len(lows), rows is not None...  16.7 us
    ppermute x21, waiting for transfers between devices, over_tensor(): lax.ppermute(values, 'tensor', [(i, i ^ k) for i in range(self.tensor)])  16.3 us
    ppermute x8, starting transfers between devices, over_chips(): return lax.ppermute(values, 'dp', [(i, i ^ 2 * k) for i in range(self.dp)])  15.8 us
  transfers between devices with their start and end apart: 47, of which 18 were waited for; matrix products, arithmetic and copies ran while one was open for 11% of the time, Pallas kernels for 27%

profile of v3, /device:TPU:0, one launch (start us, length us, event | category | flops | bytes accessed | tf_op | source)
XLA Modules:
  0.0 282.9 jit_solution(12442558693189014980)
XLA Ops:
  3.5 3.0 %collective-permute-start = (bf16[256,1536]{1,0:T(8,128)(2,1)S(1)}, bf16[256,1536]{1,0:T(8,128)(2,1)S(1)}, u32[]{:S(2)}, u32[]{:S(2)}) collective-permute-start(bf16[256,1536]{1,0:T(8,128)(2,1)S(1)} %fusion.3.refs_0_), channel_id=1, source_target_pairs={{0,1},{1,0},{2,3},{3,2},{4,5},{5,4},{6,7},{7,6},{8,9},{9,8},{10,11... | collective-permute-start | bytes 2359304 | tf_op jit(solution)/shard_map/ppermute | solution.py:820
  10.0 2.6 collective-permute-start.5
  12.6 16.5 %collective-permute-done.4.refs_1_ = bf16[192,1152]{1,0:T(8,128)(2,1)S(1)} collective-permute-done((bf16[192,1152]{1,0:T(8,128)(2,1)S(1)}, bf16[192,1152]{1,0:T(8,128)(2,1)S(1)}, u32[]{:S(2)}, u32[]{:S(2)}) %collective-permute-start.4) | collective-permute-done | bytes 442400 | tf_op jit(solution)/shard_map/ppermute | solution.py:814
  46.8 5.1 %collective-permute-start.16 = (bf16[192,1536]{1,0:T(8,128)(2,1)S(1)}, bf16[192,1536]{1,0:T(8,128)(2,1)S(1)}, u32[]{:S(2)}, u32[]{:S(2)}) collective-permute-start(bf16[192,1536]{1,0:T(8,128)(2,1)S(1)} %copy-done.17), channel_id=1, source_target_pairs={{0,8},{4,12},{8,0},{12,4},{16,24},{20,28},{24,16},{28,20},{1,9},{5... | collective-permute-start | bytes 1769480 | tf_op jit(solution)/shard_map/ppermute | solution.py:814
  57.9 9.8 %project.1 = (f32[1024,1152]{1,0:T(8,128)}, bf16[1536,1152]{1,0:T(8,128)(2,1)}, bf16[1024,1536]{1,0:T(8,128)(2,1)}) custom-call(s32[3]{0:T(128)S(1)} %pad_add_fusion.place, bf16[256,1536]{1,0:T(8,128)(2,1)} %copy-done.27, bf16[256,1536]{1,0:T(8,128)(2,1)} %copy-done.24, bf16[256,1536]{1,0:T(8,128)(2,1)} %collective-permute-done.2.refs_2_, ...), custom_call_target="tpu_custom_call" | custom-call | tf_op jit(solution)/shard_map/project/pallas_call | solution.py:412
  67.7 11.3 %scan_forward.1 = (f32[1024,768]{1,0:T(8,128)}, f32[1024,1024]{1,0:T(8,128)}, bf16[1024,768]{1,0:T(8,128)(2,1)}) custom-call(f32[1024,1152]{1,0:T(8,128)} %get-tuple-element.100.raw_ref.refs_0_, f32[8,1024]{1,0:T(8,128)S(1)} %fusion.10.taps_ref.refs_4_, f32[8,128]{1,0:T(8,128)S(1)} %select_maximum_fusion.2.heads_ref.refs_5_, ...), custom_call_target="tpu_custom_call" | custom-call | tf_op jit(solution)/shard_map/scan_forward/pallas_call | solution.py:247
  88.0 10.6 %collective-permute-done.19 = bf16[192,1536]{1,0:T(8,128)(2,1)S(1)} collective-permute-done((bf16[192,1536]{1,0:T(8,128)(2,1)}, bf16[192,1536]{1,0:T(8,128)(2,1)S(1)}, u32[]{:S(2)}, u32[]{:S(2)}) %collective-permute-start.19) | collective-permute-done | bytes 589856 | tf_op jit(solution)/shard_map/ppermute | solution.py:823
  106.0 12.7 %mix.1 = (f32[1024,768]{1,0:T(8,128)S(1)}, f32[1024,768]{1,0:T(8,128)S(1)}, f32[1024,768]{1,0:T(8,128)S(1)}, f32[16,128]{1,0:T(8,128)S(1)}, bf16[1536,1536]{1,0:T(8,128)(2,1)}, /*index=5*/bf16[1024,1536]{1,0:T(8,128)(2,1)}) custom-call(s32[3]{0:T(128)S(1)} %pad_add_fusion.place, bf16[256,1536]{1,0:T(8,128)(2,1)} %copied.1.refs_0_, ...), custom_call_target="tpu_custom_call" | custom-call | tf_op jit(solution)/shard_map/mix/pallas_call | solution.py:412
  123.7 2.4 collective-permute-done.25
  126.1 4.3 %gating.1 = (bf16[1024,768]{1,0:T(8,128)(2,1)S(1)}, bf16[1024,768]{1,0:T(8,128)(2,1)S(1)}, bf16[1024,768]{1,0:T(8,128)(2,1)S(1)}, f32[8,768]{1,0:T(8,128)S(1)}) custom-call(f32[1024,768]{1,0:T(8,128)S(1)} %get-tuple-element.112.grad_out, f32[1024,768]{1,0:T(8,128)S(1)} %get-tuple-element.113.gated, ...), custom_call_target="tpu_custom_call" | custom-call | tf_op jit(solution)/shard_map/gating/pallas_call | solution.py:520
  130.4 8.8 %grad_joint_proj.1 = (bf16[4,192,1536]{2,1,0:T(8,128)(2,1)S(1)}, bf16[4,192,1536]{2,1,0:T(8,128)(2,1)S(1)}) custom-call(s32[3]{0:T(128)S(1)} %pad_add_fusion.place, bf16[1024,1536]{1,0:T(8,128)(2,1)} %get-tuple-element.111.refs_13_.refs_0_.refs_4_, bf16[1024,1536]{1,0:T(8,128)(2,1)} %get-tuple-element.118.refs_1_, ...), custom_call_target="tpu_custom_call" | custom-call | tf_op jit(solution)/shard_map/grad_joint_proj/pallas_call | solution.py:608
  139.3 5.5 %branch.1.refs_2_ = bf16[1024,1536]{1,0:T(8,128)(2,1)S(1)} custom-call(s32[3]{0:T(128)S(1)} %pad_add_fusion.place, bf16[1024,768]{1,0:T(8,128)(2,1)S(1)} %get-tuple-element.116.refs_3_.refs_0_, bf16[1536,1536]{1,0:T(8,128)(2,1)} %get-tuple-element.117.refs_1_.refs_2_, bf16[4,192,1536]{2,1,0:T(8,128)(2,1)S(1)} %get-tuple-element.120.refs_2_), custom_call_target="tpu_custom_call" | custom-call | tf_op jit(solution)/shard_map/branch/pallas_call | solution.py:671
  146.9 3.0 %collective-permute-start.27 = (bf16[192,1536]{1,0:T(8,128)(2,1)}, bf16[192,1536]{1,0:T(8,128)(2,1)}, u32[]{:S(2)}, u32[]{:S(2)}) collective-permute-start(bf16[192,1536]{1,0:T(8,128)(2,1)} %get-tuple-element.122), channel_id=1, source_target_pairs={{0,8},{4,12},{24,16},{28,20},{1,9},{5,13},{25,17},{29,21},{2,10},{... | collective-permute-start | bytes 1769480 | tf_op jit(solution)/shard_map/ppermute | solution.py:823
  156.3 14.9 %scan_backward_0.1 = (bf16[1024,1152]{1,0:T(8,128)(2,1)}, f32[8,1024]{1,0:T(8,128)}, f32[8,128]{1,0:T(8,128)}, f32[128,768]{1,0:T(8,128)}, f32[8,1024]{1,0:T(8,128)}) custom-call(f32[1024,1152]{1,0:T(8,128)} %get-tuple-element.100.raw_ref.refs_0_, f32[1024,1024]{1,0:T(8,128)} %get-tuple-element.126.refs_1_, bf16[1024,768]{1,0:T(8,128)(2,1)} %copy-done.2, ...), custom_call_target="tpu_custom_call" | custom-call | tf_op jit(solution)/shard_map/scan_backward_0/pallas_call | solution.py:280
  175.7 2.4 collective-permute-start.34
  178.1 15.7 %scan_backward_1.1 = (bf16[1024,1152]{1,0:T(8,128)(2,1)}, f32[8,1024]{1,0:T(8,128)}, f32[8,128]{1,0:T(8,128)}, f32[128,768]{1,0:T(8,128)}, f32[8,1024]{1,0:T(8,128)}) custom-call(f32[1024,1152]{1,0:T(8,128)} %get-tuple-element.100.raw_ref.refs_0_, f32[1024,1024]{1,0:T(8,128)} %get-tuple-element.126.refs_1_, ...), custom_call_target="tpu_custom_call", output_to_operand_aliasing={{0}: (7, {})} | custom-call | tf_op jit(solution)/shard_map/scan_backward_1/pallas_call | solution.py:280
  193.8 11.2 %grad_normed.1 = (bf16[1024,1536]{1,0:T(8,128)(2,1)S(1)}, f32[8,1536]{1,0:T(8,128)S(1)}) custom-call(s32[3]{0:T(128)S(1)} %pad_add_fusion.place, bf16[1024,768]{1,0:T(8,128)(2,1)S(1)} %copy-done.1, bf16[1024,1152]{1,0:T(8,128)(2,1)} %get-tuple-element.138.refs_1_, bf16[1536,1536]{1,0:T(8,128)(2,1)} %get-tuple-element.117.refs_1_.refs_2_, ...), custom_call_target="tpu_custom_call" | custom-call | tf_op jit(solution)/shard_map/grad_normed/pallas_call | solution.py:671
  205.1 9.8 %grad_scan_proj.1 = (bf16[4,208,1152]{2,1,0:T(8,128)(2,1)S(1)}, bf16[4,208,1152]{2,1,0:T(8,128)(2,1)}) custom-call(s32[3]{0:T(128)S(1)} %pad_add_fusion.place, bf16[1024,1536]{1,0:T(8,128)(2,1)} %get-tuple-element.111.refs_13_.refs_0_.refs_4_, bf16[1024,1152]{1,0:T(8,128)(2,1)} %get-tuple-element.138.refs_1_, f32[8,1024]{1,0:T(8,128)S(1)} %copy-done.15, ...), custom_call_target="tpu_custom_call" | custom-call | tf_op jit(solution)/shard_map/grad_scan_proj/pallas_call | solution.py:608
  221.4 3.1 %pairs.3 = (f32[208,1152]{1,0:T(8,128)}, bf16[208,1152]{1,0:T(8,128)(2,1)}, bf16[208,1152]{1,0:T(8,128)(2,1)}, bf16[208,1152]{1,0:T(8,128)(2,1)}) custom-call(bf16[4,208,1152]{2,1,0:T(8,128)(2,1)S(1)} %copy-done.12, bf16[4,208,1152]{2,1,0:T(8,128)(2,1)} %collective-permute-done.37.refs_1_), custom_call_target="tpu_custom_call" | custom-call | tf_op jit(solution)/shard_map/pairs/pallas_call | solution.py:636
  224.5 2.7 collective-permute-start.40
  241.7 7.6 %collective-permute-done.39.refs_1_ = bf16[256,1536]{1,0:T(8,128)(2,1)} collective-permute-done((bf16[256,1536]{1,0:T(8,128)(2,1)S(1)}, bf16[256,1536]{1,0:T(8,128)(2,1)}, u32[]{:S(2)}, u32[]{:S(2)}) %collective-permute-start.39) | collective-permute-done | bytes 786464 | tf_op jit(solution)/shard_map/ppermute | solution.py:820
  250.3 2.6 fusion.4
  253.1 4.2 %fusion.5 = (f32[256,1536]{1,0:T(8,128)}, bf16[256,1536]{1,0:T(8,128)(2,1)}) fusion(bf16[256,1536]{1,0:T(8,128)(2,1)S(1)} %copy-done.18, bf16[256,1536]{1,0:T(8,128)(2,1)S(1)} %copy-done.28, bf16[256,1536]{1,0:T(8,128)(2,1)} %get-tuple-element.156, bf16[256,1536]{1,0:T(8,128)(2,1)} %get-tuple-element.155, f32[256]{0:T(256)S(1)} %multiply_multiply_fusion, ...), kind=kLoop, calls=%fused_computation.8 | loop fusion | flops 7864320 | bytes 8658944 | tf_op jit(solution)/shard_map/sub | solution.py:1021
  257.3 12.3 %collective-permute-done.43.refs_3_ = bf16[208,1152]{1,0:T(8,128)(2,1)} collective-permute-done((bf16[208,1152]{1,0:T(8,128)(2,1)}, bf16[208,1152]{1,0:T(8,128)(2,1)}, u32[]{:S(2)}, u32[]{:S(2)}) %collective-permute-start.43) | collective-permute-done | bytes 479264 | tf_op jit(solution)/shard_map/ppermute | solution.py:814
  (272 shorter events, 99.6 us)
Async XLA Ops:
  3.5 30.7 %collective-permute-start = (bf16[256,1536]{1,0:T(8,128)(2,1)S(1)}, bf16[256,1536]{1,0:T(8,128)(2,1)S(1)}, u32[]{:S(2)}, u32[]{:S(2)}) collective-permute-start(bf16[256,1536]{1,0:T(8,128)(2,1)S(1)} %fusion.3.refs_0_), channel_id=1, source_target_pairs={{0,1},{1,0},{2,3},{3,2},{4,5},{5,4},{6,7},{7,6},{8,9},{9,8},{10,11... | collective-permute-start | bytes 2359304 | tf_op jit(solution)/shard_map/ppermute | solution.py:820
  6.5 29.1 %collective-permute-start.2 = (bf16[256,1536]{1,0:T(8,128)(2,1)S(1)}, bf16[256,1536]{1,0:T(8,128)(2,1)}, u32[]{:S(2)}, u32[]{:S(2)}) collective-permute-start(bf16[256,1536]{1,0:T(8,128)(2,1)S(1)} %fusion.3.refs_0_), channel_id=1, source_target_pairs={{0,2},{1,3},{2,0},{3,1},{4,6},{5,7},{6,4},{7,5},{8,10},{9,11},{10,... | collective-permute-start | bytes 2359304 | tf_op jit(solution)/shard_map/ppermute | solution.py:820
  8.3 20.8 %collective-permute-start.4 = (bf16[192,1152]{1,0:T(8,128)(2,1)S(1)}, bf16[192,1152]{1,0:T(8,128)(2,1)S(1)}, u32[]{:S(2)}, u32[]{:S(2)}) collective-permute-start(bf16[192,1152]{1,0:T(8,128)(2,1)S(1)} %concatenate.24.refs_0_), channel_id=1, source_target_pairs={{0,8},{4,12},{8,0},{12,4},{16,24},{20,28},{24,16},{28,20},{1,9},{5... | collective-permute-start | bytes 1327112 | tf_op jit(solution)/shard_map/ppermute | solution.py:814
  10.0 21.5 %collective-permute-start.5 = (bf16[192,1152]{1,0:T(8,128)(2,1)S(1)}, bf16[192,1152]{1,0:T(8,128)(2,1)S(1)}, u32[]{:S(2)}, u32[]{:S(2)}) collective-permute-start(bf16[192,1152]{1,0:T(8,128)(2,1)S(1)} %concatenate.24.refs_0_), channel_id=1, source_target_pairs={{0,16},{4,20},{8,24},{12,28},{16,0},{20,4},{24,8},{28,12},{1,17},{... | collective-permute-start | bytes 1327112 | tf_op jit(solution)/shard_map/ppermute | solution.py:814
  46.8 32.3 %collective-permute-start.16 = (bf16[192,1536]{1,0:T(8,128)(2,1)S(1)}, bf16[192,1536]{1,0:T(8,128)(2,1)S(1)}, u32[]{:S(2)}, u32[]{:S(2)}) collective-permute-start(bf16[192,1536]{1,0:T(8,128)(2,1)S(1)} %copy-done.17), channel_id=1, source_target_pairs={{0,8},{4,12},{8,0},{12,4},{16,24},{20,28},{24,16},{28,20},{1,9},{5... | collective-permute-start | bytes 1769480 | tf_op jit(solution)/shard_map/ppermute | solution.py:814
  51.8 28.6 %collective-permute-start.17 = (bf16[192,1536]{1,0:T(8,128)(2,1)S(1)}, bf16[192,1536]{1,0:T(8,128)(2,1)S(1)}, u32[]{:S(2)}, u32[]{:S(2)}) collective-permute-start(bf16[192,1536]{1,0:T(8,128)(2,1)S(1)} %copy-done.17), channel_id=1, source_target_pairs={{0,16},{4,20},{8,24},{12,28},{16,0},{20,4},{24,8},{28,12},{1,17},{... | collective-permute-start | bytes 1769480 | tf_op jit(solution)/shard_map/ppermute | solution.py:814
  55.8 27.4 %collective-permute-start.12 = (bf16[256,1536]{1,0:T(8,128)(2,1)}, bf16[256,1536]{1,0:T(8,128)(2,1)S(1)}, u32[]{:S(2)}, u32[]{:S(2)}) collective-permute-start(bf16[256,1536]{1,0:T(8,128)(2,1)} %copied.1.refs_0_), channel_id=1, source_target_pairs={{0,1},{1,0},{2,3},{3,2},{4,5},{5,4},{6,7},{7,6},{8,9},{9,8},{10,11... | collective-permute-start | bytes 2359304 | tf_op jit(solution)/shard_map/ppermute | solution.py:820
  56.4 27.8 %collective-permute-start.13 = (bf16[256,1536]{1,0:T(8,128)(2,1)}, bf16[256,1536]{1,0:T(8,128)(2,1)}, u32[]{:S(2)}, u32[]{:S(2)}) collective-permute-start(bf16[256,1536]{1,0:T(8,128)(2,1)} %copied.1.refs_0_), channel_id=1, source_target_pairs={{0,2},{1,3},{2,0},{3,1},{4,6},{5,7},{6,4},{7,5},{8,10},{9,11},{10,... | collective-permute-start | bytes 2359304 | tf_op jit(solution)/shard_map/ppermute | solution.py:820
  82.0 16.6 %collective-permute-start.19 = (bf16[192,1536]{1,0:T(8,128)(2,1)}, bf16[192,1536]{1,0:T(8,128)(2,1)S(1)}, u32[]{:S(2)}, u32[]{:S(2)}) collective-permute-start(bf16[192,1536]{1,0:T(8,128)(2,1)} %get-tuple-element.106.refs_2_), channel_id=1, source_target_pairs={{8,0},{12,4},{16,24},{20,28},{9,1},{13,5},{17,25},{21,29},{10,2},{... | collective-permute-start | bytes 1769480 | tf_op jit(solution)/shard_map/ppermute | solution.py:823
  85.9 13.6 %collective-permute-start.14 = (bf16[128,1536]{1,0:T(8,128)(2,1)}, bf16[128,1536]{1,0:T(8,128)(2,1)S(1)}, u32[]{:S(2)}, u32[]{:S(2)}) collective-permute-start(bf16[128,1536]{1,0:T(8,128)(2,1)} %get-tuple-element.102), channel_id=1, source_target_pairs={{0,2},{1,3},{2,0},{3,1},{4,6},{5,7},{6,4},{7,5},{8,10},{9,11},{10,... | collective-permute-start | bytes 1179656 | tf_op jit(solution)/shard_map/ppermute | solution.py:820
  146.9 24.4 %collective-permute-start.27 = (bf16[192,1536]{1,0:T(8,128)(2,1)}, bf16[192,1536]{1,0:T(8,128)(2,1)}, u32[]{:S(2)}, u32[]{:S(2)}) collective-permute-start(bf16[192,1536]{1,0:T(8,128)(2,1)} %get-tuple-element.122), channel_id=1, source_target_pairs={{0,8},{4,12},{24,16},{28,20},{1,9},{5,13},{25,17},{29,21},{2,10},{... | collective-permute-start | bytes 1769480 | tf_op jit(solution)/shard_map/ppermute | solution.py:823
  149.9 21.5 %collective-permute-start.28 = (bf16[192,1536]{1,0:T(8,128)(2,1)}, bf16[192,1536]{1,0:T(8,128)(2,1)}, u32[]{:S(2)}, u32[]{:S(2)}) collective-permute-start(bf16[192,1536]{1,0:T(8,128)(2,1)} %get-tuple-element.122), channel_id=1, source_target_pairs={{8,16},{12,20},{16,8},{20,12},{9,17},{13,21},{17,9},{21,13},{10,18... | collective-permute-start | bytes 1769480 | tf_op jit(solution)/shard_map/ppermute | solution.py:823
  152.6 18.7 %collective-permute-start.29 = (bf16[128,1536]{1,0:T(8,128)(2,1)}, bf16[128,1536]{1,0:T(8,128)(2,1)}, u32[]{:S(2)}, u32[]{:S(2)}) collective-permute-start(bf16[128,1536]{1,0:T(8,128)(2,1)} %get-tuple-element.124), channel_id=1, source_target_pairs={{0,2},{1,3},{2,0},{3,1},{4,6},{5,7},{6,4},{7,5},{8,10},{9,11},{10,... | collective-permute-start | bytes 1179656 | tf_op jit(solution)/shard_map/ppermute | solution.py:820
  153.2 18.1 %collective-permute-start.30 = (bf16[128,1536]{1,0:T(8,128)(2,1)}, bf16[128,1536]{1,0:T(8,128)(2,1)}, u32[]{:S(2)}, u32[]{:S(2)}) collective-permute-start(bf16[128,1536]{1,0:T(8,128)(2,1)} %get-tuple-element.125), channel_id=1, source_target_pairs={{0,1},{1,0},{2,3},{3,2},{4,5},{5,4},{6,7},{7,6},{8,9},{9,8},{10,11... | collective-permute-start | bytes 1179656 | tf_op jit(solution)/shard_map/ppermute | solution.py:820
  154.6 50.5 %collective-permute-start.33 = (bf16[192,1536]{1,0:T(8,128)(2,1)}, bf16[192,1536]{1,0:T(8,128)(2,1)}, u32[]{:S(2)}, u32[]{:S(2)}) collective-permute-start(bf16[192,1536]{1,0:T(8,128)(2,1)} %get-tuple-element.123.refs_2_.refs_7_), channel_id=1, source_target_pairs={{0,8},{4,12},{8,0},{12,4},{16,24},{20,28},{24,16},{28,20},{1,9},{5... | collective-permute-start | bytes 1769480 | tf_op jit(solution)/shard_map/ppermute | solution.py:814
  172.8 32.2 %collective-permute-start.32 = (bf16[256,1536]{1,0:T(8,128)(2,1)S(1)}, bf16[256,1536]{1,0:T(8,128)(2,1)S(1)}, u32[]{:S(2)}, u32[]{:S(2)}) collective-permute-start(bf16[256,1536]{1,0:T(8,128)(2,1)S(1)} %pad_maximum_fusion.1), channel_id=1, source_target_pairs={{0,2},{1,3},{2,0},{3,1},{4,6},{5,7},{6,4},{7,5},{8,10},{9,11},{10,... | collective-permute-start | bytes 2359304 | tf_op jit(solution)/shard_map/ppermute | solution.py:820
  173.8 31.3 %collective-permute-start.31 = (bf16[256,1536]{1,0:T(8,128)(2,1)S(1)}, bf16[256,1536]{1,0:T(8,128)(2,1)S(1)}, u32[]{:S(2)}, u32[]{:S(2)}) collective-permute-start(bf16[256,1536]{1,0:T(8,128)(2,1)S(1)} %pad_maximum_fusion), channel_id=1, source_target_pairs={{0,1},{1,0},{2,3},{3,2},{4,5},{5,4},{6,7},{7,6},{8,9},{9,8},{10,11... | collective-permute-start | bytes 2359304 | tf_op jit(solution)/shard_map/ppermute | solution.py:820
  175.7 29.3 %collective-permute-start.34 = (bf16[192,1536]{1,0:T(8,128)(2,1)S(1)}, bf16[192,1536]{1,0:T(8,128)(2,1)S(1)}, u32[]{:S(2)}, u32[]{:S(2)}) collective-permute-start(bf16[192,1536]{1,0:T(8,128)(2,1)S(1)} %add_convert_fusion), channel_id=1, source_target_pairs={{0,16},{4,20},{8,24},{12,28},{16,0},{20,4},{24,8},{28,12},{1,17},{... | collective-permute-start | bytes 1769480 | tf_op jit(solution)/shard_map/ppermute | solution.py:814
  224.5 14.5 %collective-permute-start.40 = (bf16[208,1152]{1,0:T(8,128)(2,1)}, bf16[208,1152]{1,0:T(8,128)(2,1)}, u32[]{:S(2)}, u32[]{:S(2)}) collective-permute-start(bf16[208,1152]{1,0:T(8,128)(2,1)} %get-tuple-element.154), channel_id=1, source_target_pairs={{0,8},{4,12},{24,16},{28,20},{1,9},{5,13},{25,17},{29,21},{2,10},{... | collective-permute-start | bytes 1437704 | tf_op jit(solution)/shard_map/ppermute | solution.py:823
  230.7 18.6 %collective-permute-start.39 = (bf16[256,1536]{1,0:T(8,128)(2,1)S(1)}, bf16[256,1536]{1,0:T(8,128)(2,1)}, u32[]{:S(2)}, u32[]{:S(2)}) collective-permute-start(bf16[256,1536]{1,0:T(8,128)(2,1)S(1)} %pad_maximum_fusion.3), channel_id=1, source_target_pairs={{0,2},{1,3},{2,0},{3,1},{4,6},{5,7},{6,4},{7,5},{8,10},{9,11},{10,... | collective-permute-start | bytes 2359304 | tf_op jit(solution)/shard_map/ppermute | solution.py:820
  231.7 18.6 %collective-permute-start.38 = (bf16[256,1536]{1,0:T(8,128)(2,1)S(1)}, bf16[256,1536]{1,0:T(8,128)(2,1)}, u32[]{:S(2)}, u32[]{:S(2)}) collective-permute-start(bf16[256,1536]{1,0:T(8,128)(2,1)S(1)} %pad_maximum_fusion.2), channel_id=1, source_target_pairs={{0,1},{1,0},{2,3},{3,2},{4,5},{5,4},{6,7},{7,6},{8,9},{9,8},{10,11... | collective-permute-start | bytes 2359304 | tf_op jit(solution)/shard_map/ppermute | solution.py:820
  235.9 21.4 %collective-permute-start.41 = (bf16[208,1152]{1,0:T(8,128)(2,1)}, bf16[208,1152]{1,0:T(8,128)(2,1)}, u32[]{:S(2)}, u32[]{:S(2)}) collective-permute-start(bf16[208,1152]{1,0:T(8,128)(2,1)} %get-tuple-element.154), channel_id=1, source_target_pairs={{8,16},{12,20},{16,8},{20,12},{9,17},{13,21},{17,9},{21,13},{10,18... | collective-permute-start | bytes 1437704 | tf_op jit(solution)/shard_map/ppermute | solution.py:823
  237.3 20.0 %collective-permute-start.42 = (bf16[208,1152]{1,0:T(8,128)(2,1)}, bf16[208,1152]{1,0:T(8,128)(2,1)}, u32[]{:S(2)}, u32[]{:S(2)}) collective-permute-start(bf16[208,1152]{1,0:T(8,128)(2,1)} %get-tuple-element.150.refs_2_), channel_id=1, source_target_pairs={{0,8},{4,12},{8,0},{12,4},{16,24},{20,28},{24,16},{28,20},{1,9},{5... | collective-permute-start | bytes 1437704 | tf_op jit(solution)/shard_map/ppermute | solution.py:814
  240.9 28.6 %collective-permute-start.43 = (bf16[208,1152]{1,0:T(8,128)(2,1)}, bf16[208,1152]{1,0:T(8,128)(2,1)}, u32[]{:S(2)}, u32[]{:S(2)}) collective-permute-start(bf16[208,1152]{1,0:T(8,128)(2,1)} %add_convert_fusion.1.refs_2_), channel_id=1, source_target_pairs={{0,16},{4,20},{8,24},{12,28},{16,0},{20,4},{24,8},{28,12},{1,17},{... | collective-permute-start | bytes 1437704 | tf_op jit(solution)/shard_map/ppermute | solution.py:814
  (88 other events, 526.4 us)

commit v4 on v3

--- a/solution.py
+++ b/solution.py
@@ -41,13 +41,21 @@
     return lax.broadcasted_iota(jnp.int32, (CHUNK, LANES), dim)
 
 
+def exact_dot(ones, values, parts):
+    split = []
+    for _ in range(parts):
+        split.append(values.astype(bf16))
+        values = values - split[-1].astype(f32)
+    result = dot(ones, jnp.concatenate(split, axis=1))
+    return sum(result[:, i * LANES : (i + 1) * LANES] for i in range(parts))
+
+
 def decays(step_raw, heads_ref):
     raw = step_raw + heads_ref[0:1]
     small = jnp.exp(-jnp.abs(raw))
     log_one = jnp.where(small < 1e-3, small - 0.5 * small * small, jnp.log(1.0 + small))
     steps = jnp.maximum(raw, 0.0) + log_one
-    upto = (places(0) >= places(1)).astype(f32)
-    summed = dot(upto, steps * heads_ref[1:2], precision=highest)
+    summed = exact_dot((places(0) >= places(1)).astype(bf16), steps * heads_ref[1:2], 3)
     return steps, sigmoid(raw), summed, summed - jnp.log(steps)
 
 
@@ -141,7 +149,7 @@
     suffix = (places(0) >= places(1)).astype(bf16)
     left = places(1) < HEAD_DIM
     score_grads = jnp.zeros((CHUNK, LANES), f32)
-    spans, inner_grads = [], []
+    spans, inner_grads, lasts = [], [], []
     for pair in range(channels // LANES):
         cols = slice(pair * LANES, (pair + 1) * LANES)
         values = act[:, cols].astype(f32)
@@ -183,30 +191,25 @@
         wide[4 * CHUNK : 5 * CHUNK, cols] = (values * both_grads).astype(bf16)
         held = jnp.sum(entering.astype(f32) * leaving, axis=0, keepdims=True) * factor[CHUNK - 1 :]
         sums_ref[CONV + 1 : CONV + 2, cols] += jnp.sum(grad * values, axis=0, keepdims=True)
-        sums_ref[CONV + 2 : CONV + 3, cols] = held
+        wide[5 * CHUNK :, cols] = jnp.broadcast_to(held, (16, LANES)).astype(bf16)
+        lasts.append(factor[CHUNK - 1 :])
     reads_t = reads.astype(f32).T.astype(bf16)
     score_low = score_grads.astype(bf16)
     spread_all = wide[0:CHUNK, :]
     read_grads = dot(score_low, writes, 0, 0) + dot(spread_all, states_ref[...], 1, 1)
     write_grads = dot(score_low, reads) + dot(wide[CHUNK : 2 * CHUNK, :], carry[...].astype(bf16), 1, 1)
-    last = jnp.exp(summed[CHUNK - 1 :])
     of_head = (
         lax.broadcasted_iota(jnp.int32, (channels, LANES), 0) // HEAD_DIM
         == lax.broadcasted_iota(jnp.int32, (channels, LANES), 1)
     )
-    reduced = dot(wide[2 * CHUNK : 5 * CHUNK, :], of_head.astype(bf16))
-    held_rows = jnp.broadcast_to(sums_ref[CONV + 2 : CONV + 3, :channels], (8, channels))
-    held_heads = dot(held_rows, of_head.astype(f32), precision=highest)[0:1]
-    lasts = dot(jnp.broadcast_to(last, (8, LANES)), of_head.astype(f32), 1, 1, precision=highest)[0:1]
-    carry[...] = carry[...] * lasts + dot(reads_t, spread_all)
-    across_sums, later_sums, both_sums = reduced[:CHUNK], reduced[CHUNK : 2 * CHUNK], reduced[2 * CHUNK :]
+    reduced = dot(wide[2 * CHUNK :, :], of_head.astype(bf16))
+    carry[...] = carry[...] * jnp.concatenate(lasts, axis=1) + dot(reads_t, spread_all)
+    both_sums = reduced[2 * CHUNK : 3 * CHUNK]
+    held_heads = reduced[3 * CHUNK : 3 * CHUNK + 1]
     span_rows = jnp.concatenate(spans + [jnp.zeros((LANES - len(spans), LANES), f32)], axis=0)
-    log_grads = (
-        dot((places(0) <= places(1)).astype(f32), across_sums, precision=highest)
-        + dot((places(0) > places(1)).astype(f32), later_sums, precision=highest)
-        + span_rows.T
-        + held_heads
-    )
+    upto = [places(0) <= places(1), places(0) > places(1)]
+    upto = jnp.concatenate([v.astype(bf16) for v in upto], axis=1)
+    log_grads = exact_dot(upto, reduced[: 2 * CHUNK], 2) + span_rows.T + held_heads
     ratio = jnp.where(steps > 1e-30, slopes / steps, 1.0)
     step_grads = both_sums * ratio + heads_ref[1:2] * log_grads * slopes
     head_sums_ref[0:1] += jnp.sum(step_grads, axis=0, keepdims=True)
@@ -260,7 +263,7 @@
             pltpu.HBM((tokens, width), f32),
             pltpu.HBM((count * STATE, channels), bf16),
         ],
-        compiler_params=pltpu.CompilerParams(vmem_limit_bytes=20 << 20),
+        compiler_params=pltpu.CompilerParams(vmem_limit_bytes=12 << 20),
         name="scan_forward",
     )(stay(raw), taps, heads, skip, *earlier)
 
@@ -292,16 +295,17 @@
         + ([free] + [whole(shape) for shape in kept] if part else [])
         + [free] * len(earlier),
         out_specs=[by_chunk((CHUNK, full))] + [whole(shape) for shape in kept],
-        scratch_shapes=[pltpu.VMEM((5 * CHUNK, channels), bf16)],
+        scratch_shapes=[pltpu.VMEM((5 * CHUNK + 16, channels), bf16)],
         out_shape=[pltpu.HBM((tokens, full), bf16)] + [pltpu.HBM(shape, f32) for shape in kept],
         input_output_aliases={7: 0} if part else {},
-        compiler_params=pltpu.CompilerParams(vmem_limit_bytes=20 << 20),
+        compiler_params=pltpu.CompilerParams(vmem_limit_bytes=12 << 20),
         name=f"scan_backward_{part}",
     )(stay(raw), stay(pre), stay(grad), stay(states), taps, heads, skip, *[stay(v) for v in held], *earlier)
 
 
 BLOCK = 256
-LIMIT = 24 << 20
+LIMIT = 16 << 20
+SMALL_LIMIT = 12 << 20
 SMALL = 16
 anywhere = pl.BlockSpec(memory_space=pl.ANY)
 in_vmem = pl.BlockSpec(memory_space=pltpu.VMEM)
@@ -333,17 +337,12 @@
     return pl.multiple_of((start // BLOCK ^ place[2]) * BLOCK, BLOCK)
 
 
-def product_kernel(layout, chips, epilogue, place, *refs):
-    heights, keep_rows, n_extra, n_deps, n_out = layout
+def product_kernel(heights, chips, epilogue, n_extra, n_deps, n_out, place, *refs):
     n_rows, n_full = len(heights), 2 * chips
     row_refs, refs = refs[:n_rows], refs[n_rows:]
     full_refs, refs = refs[:n_full], refs[n_full:]
     extra, refs = refs[:n_extra], refs[n_extra + n_deps :]
-    outs, refs = refs[:n_out], refs[n_out:]
-    full_out, refs = refs[0], refs[1:]
-    if keep_rows:
-        rows_out, refs = refs[0], refs[1:]
-    rows, full, sems, back = refs
+    outs, (full, rows, sems) = refs[:n_out], refs[n_out:]
     step = pl.program_id(0)
     starts = [sum(heights[:i]) for i in range(n_rows)]
     shard = full.shape[0] // n_full
@@ -359,7 +358,6 @@
         )
         for i in range(n_full)
     ]
-    backs = [pltpu.make_async_copy(full, full_out, back.at[0])]
 
     @pl.when(step == 0)
     def _():
@@ -367,7 +365,6 @@
             copy.start()
         for copy in full_copies:
             copy.wait()
-        backs[0].start()
 
     for i in range(n_rows):
 
@@ -375,20 +372,8 @@
         def _(i=i):
             row_copies[i].wait()
 
-    if keep_rows:
-        backs.append(pltpu.make_async_copy(rows, rows_out, back.at[1]))
-
-        @pl.when(step == starts[-1] // BLOCK)
-        def _():
-            backs[1].start()
-
     block = rows[pl.ds(row_start(place, step * BLOCK), BLOCK), :]
     epilogue(step ^ place[2], block, full, extra, outs)
-
-    @pl.when(step == pl.num_programs(0) - 1)
-    def _():
-        for copy in backs:
-            copy.wait()
 
 
 def product(place, row_pieces, full_pieces, epilogue, extra, outs, name, earlier=()):
@@ -397,35 +382,27 @@
     tokens, depth = sum(heights), row_pieces[0].shape[1]
     columns = full_pieces[0].shape[1]
     by_block = lambda cols: pl.BlockSpec((BLOCK, cols), lambda s, p: (s ^ p[2], 0))
-    whole = lambda shape: pl.BlockSpec(shape, lambda s, p: (0, 0))
     out_specs, out_shape = [], []
     for cols, dtype in outs:
         if cols is None:
-            out_specs.append(whole((dtype * tokens // LANES, LANES)))
-            out_shape.append(jax.ShapeDtypeStruct((dtype * tokens // LANES, LANES), f32))
+            shape = (dtype * tokens // LANES, LANES)
+            out_specs.append(pl.BlockSpec(shape, lambda s, p: (0, 0)))
+            out_shape.append(jax.ShapeDtypeStruct(shape, f32))
         else:
             out_specs.append(by_block(cols))
             out_shape.append((pltpu.HBM if name == "project" else NEAR)((tokens, cols), dtype))
-    out_specs += [anywhere, anywhere]
-    out_shape += [pltpu.HBM((depth, columns), bf16), pltpu.HBM((tokens, depth), bf16)]
-    layout = (heights, True, len(extra), len(earlier), len(outs))
     return pl.pallas_call(
-        functools.partial(product_kernel, layout, chips, epilogue),
+        functools.partial(product_kernel, heights, chips, epilogue, len(extra), len(earlier), len(outs)),
         grid_spec=pltpu.PrefetchScalarGridSpec(
             num_scalar_prefetch=1,
             grid=(tokens // BLOCK,),
             in_specs=[anywhere] * (len(row_pieces) + len(full_pieces))
-            + [by_block(v.shape[1]) if by else whole(v.shape) for v, by in extra]
+            + [by_block(v.shape[1]) if by else in_vmem for v, by in extra]
             + [anywhere] * len(earlier),
-            out_specs=out_specs,
-            scratch_shapes=[
-                pltpu.VMEM((tokens, depth), bf16),
-                pltpu.VMEM((depth, columns), bf16),
-                pltpu.SemaphoreType.DMA((len(row_pieces) + len(full_pieces),)),
-                pltpu.SemaphoreType.DMA((2,)),
-            ],
+            out_specs=out_specs + [in_vmem, in_vmem],
+            scratch_shapes=[pltpu.SemaphoreType.DMA((len(row_pieces) + len(full_pieces),))],
         ),
-        out_shape=out_shape,
+        out_shape=out_shape + [pltpu.VMEM((depth, columns), bf16), pltpu.VMEM((tokens, depth), bf16)],
         compiler_params=pltpu.CompilerParams(vmem_limit_bytes=LIMIT),
         name=name,
     )(place, *[stay(v) for v in row_pieces + full_pieces], *[v for v, _ in extra], *earlier)
@@ -447,8 +424,9 @@
     channels = gate.shape[1]
     squares = jnp.zeros((BLOCK, LANES), f32)
     dots = jnp.zeros((BLOCK, LANES), f32)
+    here = pl.ds(pl.multiple_of(index * BLOCK, BLOCK), BLOCK)
     for cols in slices(channels):
-        value = dot(rows[...], full[:, cols])
+        value = dot(rows[here, :], full[:, cols])
         out = dot(block, full[:, channels + cols.start : channels + cols.stop])
         gate[:, cols] = value
         grad[:, cols] = out
@@ -485,7 +463,7 @@
     return jnp.broadcast_to(row, (LANES, LANES)).T
 
 
-def gating_kernel(grad_out, gated, scanned, gate, sums, gain, out_low, gate_back, scan_grad, gain_grad):
+def gating_kernel(grad_out, gated, gate, sums, gain, scanned, out_low, gate_back, scan_grad, gain_grad):
     step = pl.program_id(0)
     half = sums.shape[0] // 2
 
@@ -496,14 +474,15 @@
     for part in range(BLOCK // LANES):
         rows = slice(part * LANES, (part + 1) * LANES)
         index = step * (BLOCK // LANES) + part
+        here = pl.ds(pl.multiple_of(index * LANES, LANES), LANES)
         ratio_row = lax.rsqrt(sums[pl.ds(index, 1), :] / DI + epsilon)
         dots = sums[pl.ds(half + index, 1), :]
         ratio = columns_of(ratio_row)
         pull = columns_of(ratio_row * ratio_row * ratio_row / DI * dots)
         for start in range(0, gate.shape[1], LANES):
             cols = slice(start, start + LANES)
-            held, value = gated[rows, cols], gate[rows, cols]
-            scaled = grad_out[rows, cols] * ratio
+            held, value = gated[here, cols], gate[here, cols]
+            scaled = grad_out[here, cols] * ratio
             out_low[rows, cols] = (gain[:, cols] * (held * ratio)).astype(bf16)
             gain_grad[0:1, cols] += jnp.sum(scaled * held, axis=0, keepdims=True)
             grad = gain[:, cols] * scaled - held * pull
@@ -516,31 +495,33 @@
 def gating(grad_out, gated, scanned, gate, sums, gain):
     tokens, columns = gated.shape
     block = pl.BlockSpec((BLOCK, columns), lambda s: (s, 0))
-    whole = lambda v: pl.BlockSpec(v.shape, lambda s: (0, 0))
     return pl.pallas_call(
         gating_kernel,
         grid=(tokens // BLOCK,),
-        in_specs=[block] * 4 + [whole(sums), whole(gain)],
+        in_specs=[in_vmem] * 5 + [block],
         out_specs=[block] * 3 + [pl.BlockSpec((8, columns), lambda s: (0, 0))],
-        out_shape=[NEAR((tokens, columns), bf16)] * 3 + [jax.ShapeDtypeStruct((8, columns), f32)],
-        compiler_params=pltpu.CompilerParams(vmem_limit_bytes=LIMIT),
+        out_shape=[NEAR((tokens, columns), bf16)] * 2
+        + [pltpu.HBM((tokens, columns), bf16)] + [jax.ShapeDtypeStruct((8, columns), f32)],
+        compiler_params=pltpu.CompilerParams(vmem_limit_bytes=SMALL_LIMIT),
         name="gating",
-    )(grad_out, gated, stay(scanned), gate, sums, gain)
-
-
-def grads_kernel(n_rows, place, *refs):
+    )(grad_out, gated, gate, sums, gain, stay(scanned))
+
+
+def grads_kernel(n_rows, wide, place, *refs):
     rows, lows = refs[:n_rows], refs[n_rows : 2 * n_rows]
-    keep, give, acc = refs[-3:]
-    wide = acc.shape[0]
+    keep, give = refs[-2:]
     shard = wide // 2
+    first = place[1] == 0
+    lanes = pl.ds(pl.multiple_of((pl.program_id(0) ^ place[0]) * wide, LANES), wide)
     start = 0
     for row, low in zip(rows, lows, strict=True):
         for cols in slices(low.shape[1]):
-            acc[:, start + cols.start : start + cols.stop] = dot(row[...], low[:, cols], 0, 0)
+            value = dot(row[:, lanes], low[:, cols], 0, 0)
+            one, two = value[:shard], value[shard:]
+            out = slice(start + cols.start, start + cols.stop)
+            keep[0, :shard, out] = jnp.where(first, one, two).astype(bf16)
+            give[0, :shard, out] = jnp.where(first, two, one).astype(bf16)
         start += low.shape[1]
-    mine, other = (pl.multiple_of(core * shard, shard) for core in (place[1], 1 - place[1]))
-    keep[0, :shard] = acc[pl.ds(mine, shard), :].astype(bf16)
-    give[0, :shard] = acc[pl.ds(other, shard), :].astype(bf16)
 
 
 def fill_small(small, sums, gain_grad, norm_grad, head_sums):
@@ -553,9 +534,9 @@
     small[11:14, :LANES] = head_sums[0:3, :]
 
 
-def small_kernel(n_rows, place, *refs):
-    keep, give, small = refs[-4], refs[-3], refs[-1]
-    grads_kernel(n_rows, place, *refs[:-1])
+def small_kernel(n_rows, wide, place, *refs):
+    keep, give, small = refs[-3:]
+    grads_kernel(n_rows, wide, place, *refs[:-1])
     fill_small(small, *refs[2 * n_rows : 2 * n_rows + 4])
     low = small[...].astype(bf16)
     shard = keep.shape[1] - SMALL
@@ -604,24 +585,20 @@
             name=name,
         )(place, *rows, *lows, *small, *earlier)
     out = pl.BlockSpec((1, height, columns), lambda k, p: (k, 0, 0))
-    whole = lambda v: pl.BlockSpec(v.shape, lambda k, p: (0, 0))
     return pl.pallas_call(
-        functools.partial(small_kernel if small else grads_kernel, len(rows)),
+        functools.partial(small_kernel if small else grads_kernel, len(rows), wide),
         grid_spec=pltpu.PrefetchScalarGridSpec(
             num_scalar_prefetch=1,
             grid=(chips,),
-            in_specs=[pl.BlockSpec((tokens, wide), lambda k, p: (0, k ^ p[0]))] * len(rows)
-            + [whole(v) for v in lows]
-            + [whole(v) for v in small]
+            in_specs=[in_vmem] * (2 * len(rows) + len(small))
             + [anywhere] * len(earlier),
             out_specs=[out, out],
-            scratch_shapes=[pltpu.VMEM((wide, columns), f32)]
-            + ([pltpu.VMEM((SMALL, columns), f32)] if small else []),
+            scratch_shapes=[pltpu.VMEM((SMALL, columns), f32)] if small else [],
         ),
         out_shape=[jax.ShapeDtypeStruct((chips, height, columns), bf16)] * 2,
-        compiler_params=pltpu.CompilerParams(vmem_limit_bytes=LIMIT),
+        compiler_params=pltpu.CompilerParams(vmem_limit_bytes=SMALL_LIMIT),
         name=name,
-    )(place, *[stay(v) for v in rows], *lows, *small, *earlier)
+    )(place, *rows, *lows, *small, *earlier)
 
 
 def pairs_kernel(chips, *refs):
@@ -638,52 +615,54 @@
         in_specs=[in_vmem, in_vmem] + [anywhere] * len(earlier),
         out_specs=[in_vmem] * chips,
         out_shape=[pltpu.HBM((rows, columns), f32)] + [pltpu.HBM((rows, columns), bf16)] * (chips - 1),
-        compiler_params=pltpu.CompilerParams(vmem_limit_bytes=LIMIT),
+        compiler_params=pltpu.CompilerParams(vmem_limit_bytes=SMALL_LIMIT),
         name="pairs",
     )(keep, come, *earlier)
     return out[0], list(out[1:])
 
 
-def back_kernel(count, with_rows, place, *refs):
+def back_kernel(parts, with_rows, place, *refs):
+    count = len(parts)
     lows, fulls, refs = refs[:count], refs[count : 2 * count], refs[2 * count :]
     rows, out, sums = (refs[0], refs[-2], refs[-1]) if with_rows else (None, refs[-1], None)
+    step = pl.program_id(0)
     if with_rows:
 
-        @pl.when(pl.program_id(0) == 0)
+        @pl.when(step == 0)
         def _():
             sums[...] = jnp.zeros_like(sums)
 
+    here = pl.ds(pl.multiple_of((step ^ place[2]) * BLOCK, BLOCK), BLOCK)
     for cols in slices(out.shape[1]):
-        value = dot(lows[0][...], fulls[0][cols, :], 1, 1)
-        for low, full in zip(lows[1:], fulls[1:], strict=True):
-            value = value + dot(low[...], full[cols, :], 1, 1)
+        value = 0.0
+        for low, full, part in zip(lows, fulls, parts, strict=True):
+            wide = low.shape[1]
+            value = value + dot(low[...], full[cols, part * wide : (part + 1) * wide], 1, 1)
         out[:, cols] = value.astype(bf16)
         if with_rows:
-            sums[0:1, cols] += jnp.sum(value * rows[:, cols].astype(f32), axis=0, keepdims=True)
+            sums[0:1, cols] += jnp.sum(value * rows[here, cols].astype(f32), axis=0, keepdims=True)
 
 
 def back(place, lows, fulls, rows, name, earlier=()):
     tokens, depth = lows[0].shape[0], fulls[0][0].shape[0]
     by_block = lambda cols: pl.BlockSpec((BLOCK, cols), lambda s, p: (s ^ p[2], 0))
-    whole = lambda shape: pl.BlockSpec(shape, lambda s, p: (0, 0))
-    columns = lambda cols, i: pl.BlockSpec((depth, cols), lambda s, p: (0, i))
-    extra = [] if rows is None else [stay(rows)]
+    extra = [] if rows is None else [rows]
     out = pl.pallas_call(
-        functools.partial(back_kernel, len(lows), rows is not None),
+        functools.partial(back_kernel, tuple(part for _, part in fulls), rows is not None),
         grid_spec=pltpu.PrefetchScalarGridSpec(
             num_scalar_prefetch=1,
             grid=(tokens // BLOCK,),
             in_specs=[by_block(v.shape[1]) for v in lows]
-            + [columns(v.shape[1], i) for v, (_, i) in zip(lows, fulls, strict=True)]
-            + [by_block(depth) for _ in extra]
+            + [in_vmem] * (len(fulls) + len(extra))
             + [anywhere] * len(earlier),
-            out_specs=[pl.BlockSpec((BLOCK, depth), lambda s, p: (s, 0))] + [whole((8, depth)) for _ in extra],
+            out_specs=[pl.BlockSpec((BLOCK, depth), lambda s, p: (s, 0))]
+            + [pl.BlockSpec((8, depth), lambda s, p: (0, 0)) for _ in extra],
         ),
         out_shape=[jax.ShapeDtypeStruct((tokens, depth), bf16)]
         + [jax.ShapeDtypeStruct((8, depth), f32) for _ in extra],
-        compiler_params=pltpu.CompilerParams(vmem_limit_bytes=LIMIT),
+        compiler_params=pltpu.CompilerParams(vmem_limit_bytes=SMALL_LIMIT),
         name=name,
-    )(place, *lows, *[stay(v) for v, _ in fulls], *extra, *earlier)
+    )(place, *lows, *[v for v, _ in fulls], *extra, *earlier)
     return out[0], out[1] if extra else None
 
 
@@ -733,7 +712,7 @@
         out_shape=[jax.ShapeDtypeStruct(shape, f32) for shape in shapes]
         + [jax.ShapeDtypeStruct((rows, 2 * STATE), bf16)],
         scratch_shapes=[pltpu.VMEM((SMALL, 2 * STATE), f32)],
-        compiler_params=pltpu.CompilerParams(vmem_limit_bytes=LIMIT),
+        compiler_params=pltpu.CompilerParams(vmem_limit_bytes=SMALL_LIMIT),
         name="collect",
     )(*parts, *earlier)
 
@@ -834,8 +813,10 @@
         middle = self.between(near[0], [(1, 2), (2, 1)])
         return near + [middle + self.between(near[2], [(1, 0), (2, 3)])]
 
-    def gather_cores(self, mine):
-        return mine + [self.over_core(piece) for piece in mine]
+    def gather_cores(self, mine, earlier, early):
+        first = pinned(mine[:-1], early)
+        last = pinned(mine[-1:], earlier)
+        return first + last + [self.over_core(piece) for piece in first + last]
 
     def scatter_far(self, others):
         if self.chips != 4:
@@ -845,7 +826,8 @@
     def scatter_join(self, others, came):
         if self.chips != 4:
             return others
-        return [others[0], (others[1].astype(f32) + came[0].astype(f32)).astype(bf16)]
+        one, two = pinned(others[:2], came)
+        return [one, (two.astype(f32) + came[0].astype(f32)).astype(bf16)]
 
     def scatter_near(self, joined, came):
         return came[1:] + [self.over_chips(value, k + 1) for k, value in enumerate(joined)]
@@ -892,11 +874,7 @@
         return [values] + [self.over_tensor(values, k) for k in range(1, self.tensor)]
 
     def sum_tensor(self, values):
-        k = 1
-        while k < self.tensor:
-            values = values + self.over_tensor(values, k)
-            k *= 2
-        return values
+        return sum(self.spread_tensor(values)[1:], values)
 
 
 def local(
@@ -932,10 +910,11 @@
     scan_mine = net.gather_far(net.gather_near(scan_shard), [])
     row_pieces = net.gather_first(normed_low)
     reached = scan_mine[1:]
-    joint = joint_shard(gate_proj, out_proj, row_pieces[1:2])
+    cot_copy = copied(cotangent, row_pieces[1:2])
+    joint = joint_shard(gate_proj, out_proj, [cot_copy])
     row_pieces = net.gather_last(row_pieces, [])
-    scan_pieces = net.gather_cores(pinned(scan_mine, row_pieces[3:]) if row_pieces[3:] else scan_mine)
-    cot_pieces = net.gather_first(copied(cotangent, row_pieces[3:] + scan_pieces[chips:]))
+    scan_pieces = net.gather_cores(scan_mine, row_pieces[3:], [])
+    cot_pieces = net.gather_first(pinned([cot_copy], row_pieces[3:] + scan_pieces[chips:])[0])
     joint_mine = net.gather_near(pinned([joint], reached)[0])
 
     taps = jnp.concatenate(
@@ -966,9 +945,9 @@
     gate, gated, grad_out, token_sums, joint_full, cot_rows = product(
         place,
         cot_pieces,
-        net.gather_cores(pinned(joint_mine, cot_pieces[3:])),
+        net.gather_cores(joint_mine, cot_pieces[3:], []),
         mix_epilogue,
-        [(stay(rows), True), (stay(scanned), True), (gain, False)],
+        [(rows, False), (stay(scanned), True), (gain, False)],
         [(channels, f32), (channels, f32), (channels, f32), (None, 2)],
         "mix",
     )
@@ -1007,9 +986,11 @@
     )
     norm_came = net.scatter_first(norm_rows, joint_arrived)
     scan_own, scan_others = pairs(keep, net.over_core(give))
+    came = net.scatter_far(scan_others)
+    came = pinned(came, []) if came else came
     norm_came = pinned(norm_came, scan_others[:1]) if norm_came else norm_came
-    came = net.scatter_far(scan_others)
     joined = net.scatter_join(scan_others, came)
+    *joint_arrived, = pinned(joint_arrived, joined[1:2])
     scan_arrived = net.scatter_near(joined, came)
     norm_parts = net.scatter_last(net.scatter_blocks(norm_rows, norm_came), joined[1:])
     grad_normed = total_of(norm_parts[0].astype(f32), norm_parts[1:])
@@ -1031,19 +1012,19 @@
     return (
         mixed,
         grad_tokens,
-        norm_part[0],
+        norm_part.reshape(-1),
         grad_gate_proj,
         grad_inner_proj,
         grad_shared_proj,
         step_part[:, :heads],
         grad_conv_inner,
-        inner_bias[0],
+        inner_bias.reshape(-1),
         grad_conv_shared,
-        shared_bias[0],
+        shared_bias.reshape(-1),
         head_part[0, :heads],
         head_part[1, :heads] * rates,
         head_part[2, :heads],
-        gain_part[0],
+        gain_part.reshape(-1),
         grad_out_proj,
     )
 

time: 284 us -> 272 us (0.958)
  Pallas kernels: 117 us -> 103 us
  waiting for transfers between devices: 65 us -> 54.7 us
  other arithmetic: 22.6 us -> 28.3 us
  local copies, waits for them, and re-layouts: 21.5 us -> 26.1 us
    pallas_call x5, Pallas kernels: 43.4 us -> 38.1 us  [the longest x2 19.8 us: product(): pl.pallas_call(functools.partial(product_kernel, heights, chips, epilogue...]
    ppermute x8, waiting for transfers between devices: 32.6 us -> 28.2 us  [over_chips(): return lax.ppermute(values, 'dp', [(i, i ^ 2 * k) for i in range(self.dp)])]
    ppermute x21 -> x22, waiting for transfers between devices: 16.3 us -> 12 us  [over_tensor(): lax.ppermute(values, 'tensor', [(i, i ^ k) for i in range(self.tensor)])]
    pallas_call x2, Pallas kernels: 18.6 us -> 14.5 us  [weight_grads(): pl.pallas_call(functools.partial(small_kernel if small else grads_kernel,...]
    unnamed x133 -> x117, local copies, waits for them, and re-layouts: 12 us -> 15.9 us
    pallas_call x2, Pallas kernels: 30.6 us -> 27.2 us  [scan_backward(): pl.pallas_call(functools.partial(backward_kernel, part, len(earlier)), gr...]
    ppermute x21 -> x22, starting transfers between devices: 24.3 us -> 26.2 us  [over_tensor(): lax.ppermute(values, 'tensor', [(i, i ^ k) for i in range(self.tensor)])]
  transfers between devices with their start and end apart: 47 -> 48, of which waited for: 18 -> 18; matrix products, arithmetic and copies ran while one was open for 11% -> 13% of each run, Pallas kernels for 27% -> 25%
where the time goes in v4:
time: 272 us; the launch traced here: 270 us
  Pallas kernels  103 us (38%)
  starting transfers between devices  56.7 us (21%)
  waiting for transfers between devices  54.7 us (20%)
  other arithmetic  28.3 us (10%)
  local copies, waits for them, and re-layouts  26.1 us (10%)
    ppermute x8, waiting for transfers between devices, over_chips(): return lax.ppermute(values, 'dp', [(i, i ^ 2 * k) for i in range(self.dp)])  28.2 us
    pallas_call x2, Pallas kernels, scan_backward(): pl.pallas_call(functools.partial(backward_kernel, part, len(earlier)), gr...  27.2 us
    ppermute x22, starting transfers between devices, over_tensor(): lax.ppermute(values, 'tensor', [(i, i ^ k) for i in range(self.tensor)])  26.2 us
    pallas_call x2, Pallas kernels, product(): pl.pallas_call(functools.partial(product_kernel, heights, chips, epilogue...  19.8 us
    unnamed x117, local copies, waits for them, and re-layouts  15.9 us
    ppermute x8, starting transfers between devices, over_chips(): return lax.ppermute(values, 'dp', [(i, i ^ 2 * k) for i in range(self.dp)])  15.1 us
    pallas_call x2, Pallas kernels, weight_grads(): pl.pallas_call(functools.partial(small_kernel if small else grads_kernel,...  14.5 us
    ppermute x8, starting transfers between devices, between(): lax.ppermute(values, 'dp', [(2 * a + c, 2 * b + c) for a, b in pairs for...  13.2 us
  transfers between devices with their start and end apart: 48, of which 18 were waited for; matrix products, arithmetic and copies ran while one was open for 13% of the time, Pallas kernels for 25%

profile of v4, /device:TPU:0, one launch (start us, length us, event | category | flops | bytes accessed | tf_op | source)
XLA Modules:
  0.0 270.2 jit_solution(18406841992936169924)
XLA Ops:
  3.5 3.0 %collective-permute-start = (bf16[256,1536]{1,0:T(8,128)(2,1)S(1)}, bf16[256,1536]{1,0:T(8,128)(2,1)S(1)}, u32[]{:S(2)}, u32[]{:S(2)}) collective-permute-start(bf16[256,1536]{1,0:T(8,128)(2,1)S(1)} %fusion.3.refs_0_), channel_id=1, source_target_pairs={{0,1},{1,0},{2,3},{3,2},{4,5},{5,4},{6,7},{7,6},{8,9},{9,8},{10,11... | collective-permute-start | bytes 2359304 | tf_op jit(solution)/shard_map/ppermute | solution.py:799
  10.0 2.6 collective-permute-start.5
  12.6 16.5 %collective-permute-done.4.refs_1_ = bf16[192,1152]{1,0:T(8,128)(2,1)S(1)} collective-permute-done((bf16[192,1152]{1,0:T(8,128)(2,1)S(1)}, bf16[192,1152]{1,0:T(8,128)(2,1)S(1)}, u32[]{:S(2)}, u32[]{:S(2)}) %collective-permute-start.4) | collective-permute-done | bytes 442400 | tf_op jit(solution)/shard_map/ppermute | solution.py:793
  29.1 2.4 collective-permute-done.5.refs_2_
  46.9 5.5 %collective-permute-start.16 = (bf16[192,1536]{1,0:T(8,128)(2,1)}, bf16[192,1536]{1,0:T(8,128)(2,1)}, u32[]{:S(2)}, u32[]{:S(2)}) collective-permute-start(bf16[192,1536]{1,0:T(8,128)(2,1)} %pinned.23.refs_0_), channel_id=1, source_target_pairs={{0,8},{4,12},{8,0},{12,4},{16,24},{20,28},{24,16},{28,20},{1,9},{5... | collective-permute-start | bytes 1769480 | tf_op jit(solution)/shard_map/ppermute | solution.py:793
  57.6 8.9 %project.1 = (f32[1024,1152]{1,0:T(8,128)}, bf16[1536,1152]{1,0:T(8,128)(2,1)S(1)}, bf16[1024,1536]{1,0:T(8,128)(2,1)S(1)}) custom-call(s32[3]{0:T(128)S(1)} %pad_add_fusion.place, bf16[256,1536]{1,0:T(8,128)(2,1)} %copy-done.27, bf16[256,1536]{1,0:T(8,128)(2,1)} %copy-done.24, bf16[256,1536]{1,0:T(8,128)(2,1)} %collective-permute-done.2.refs_2_, ...), custom_call_target="tpu_custom_call" | custom-call | tf_op jit(solution)/shard_map/project/pallas_call | solution.py:394
  66.4 11.4 %scan_forward.1 = (f32[1024,768]{1,0:T(8,128)}, f32[1024,1024]{1,0:T(8,128)}, bf16[1024,768]{1,0:T(8,128)(2,1)}) custom-call(f32[1024,1152]{1,0:T(8,128)} %get-tuple-element.106.raw_ref.refs_0_, f32[8,1024]{1,0:T(8,128)S(1)} %fusion.10.taps_ref.refs_4_, f32[8,128]{1,0:T(8,128)S(1)} %select_maximum_fusion.2.heads_ref.refs_5_, ...), custom_call_target="tpu_custom_call" | custom-call | tf_op jit(solution)/shard_map/scan_forward/pallas_call | solution.py:250
  77.9 3.4 %collective-permute-done.17.refs_2_ = bf16[192,1536]{1,0:T(8,128)(2,1)} collective-permute-done((bf16[192,1536]{1,0:T(8,128)(2,1)}, bf16[192,1536]{1,0:T(8,128)(2,1)}, u32[]{:S(2)}, u32[]{:S(2)}) %collective-permute-start.17) | collective-permute-done | bytes 589856 | tf_op jit(solution)/shard_map/ppermute | solution.py:793
  90.7 8.5 %collective-permute-done.19 = bf16[192,1536]{1,0:T(8,128)(2,1)} collective-permute-done((bf16[192,1536]{1,0:T(8,128)(2,1)}, bf16[192,1536]{1,0:T(8,128)(2,1)}, u32[]{:S(2)}, u32[]{:S(2)}) %collective-permute-start.19) | collective-permute-done | bytes 589856 | tf_op jit(solution)/shard_map/ppermute | solution.py:802
  105.2 11.0 %mix.1 = (f32[1024,768]{1,0:T(8,128)S(1)}, f32[1024,768]{1,0:T(8,128)S(1)}, f32[1024,768]{1,0:T(8,128)S(1)}, f32[16,128]{1,0:T(8,128)S(1)}, bf16[1536,1536]{1,0:...) custom-call(s32[3]{0:T(128)S(1)} %pad_add_fusion.place, bf16[256,1536]{1,0:T(8,128)(2,1)} %pinned.21.refs_0_, ...), custom_call_target="tpu_custom_call" | custom-call | tf_op jit(solution)/shard_map/mix/pallas_call | solution.py:394
  121.4 2.4 collective-permute-done.26
  123.8 5.2 %gating.1 = (bf16[1024,768]{1,0:T(8,128)(2,1)S(1)}, bf16[1024,768]{1,0:T(8,128)(2,1)S(1)}, bf16[1024,768]{1,0:T(8,128)(2,1)}, f32[8,768]{1,0:T(8,128)S(1)}) custom-call(f32[1024,768]{1,0:T(8,128)S(1)} %get-tuple-element.117.grad_out, f32[1024,768]{1,0:T(8,128)S(1)} %get-tuple-element.118.gated, f32[1024,768]{1,0:T(8,128)S(1)} %get-tuple-element.119.gate, ...), custom_call_target="tpu_custom_call" | custom-call | tf_op jit(solution)/shard_map/gating/pallas_call | solution.py:498
  129.1 6.5 %grad_joint_proj.1 = (bf16[4,192,1536]{2,1,0:T(8,128)(2,1)S(1)}, bf16[4,192,1536]{2,1,0:T(8,128)(2,1)S(1)}) custom-call(s32[3]{0:T(128)S(1)} %pad_add_fusion.place, bf16[1024,1536]{1,0:T(8,128)(2,1)S(1)} %get-tuple-element.116.refs_13_.refs_0_.refs_4_, bf16[1024,1536]{1,0:T(8,128)(2,1)S(1)} %get-tuple-element.123.refs_1_, ...), custom_call_target="tpu_custom_call" | custom-call | tf_op jit(solution)/shard_map/grad_joint_proj/pallas_call | solution.py:588
  135.7 3.8 %branch.1.refs_2_ = bf16[1024,1536]{1,0:T(8,128)(2,1)S(1)} custom-call(s32[3]{0:T(128)S(1)} %pad_add_fusion.place, bf16[1024,768]{1,0:T(8,128)(2,1)S(1)} %get-tuple-element.121.refs_3_.refs_0_, bf16[1536,1536]{1,0:T(8,128)(2,1)S(1)} %get-tuple-element.122.refs_1_.refs_2_, bf16[4,192,1536]{2,1,0:T(8,128)(2,1)S(1)} %get-tuple-element.125.refs_2_), custom_call_target="tpu_custom_call" | custom-call | tf_op jit(solution)/shard_map/branch/pallas_call | solution.py:650
  149.9 13.2 %scan_backward_0.1 = (bf16[1024,1152]{1,0:T(8,128)(2,1)}, f32[8,1024]{1,0:T(8,128)}, f32[8,128]{1,0:T(8,128)}, f32[128,768]{1,0:T(8,128)}, f32[8,1024]{1,0:T(8,128)}) custom-call(f32[1024,1152]{1,0:T(8,128)} %get-tuple-element.106.raw_ref.refs_0_, f32[1024,1024]{1,0:T(8,128)} %get-tuple-element.131.refs_1_, bf16[1024,768]{1,0:T(8,128)(2,1)} %get-tuple-element.132.refs_2_, ...), custom_call_target="tpu_custom_call" | custom-call | tf_op jit(solution)/shard_map/scan_backward_0/pallas_call | solution.py:283
  172.1 14.0 %scan_backward_1.1 = (bf16[1024,1152]{1,0:T(8,128)(2,1)}, f32[8,1024]{1,0:T(8,128)}, f32[8,128]{1,0:T(8,128)}, f32[128,768]{1,0:T(8,128)}, f32[8,1024]{1,0:T(8,128)}) custom-call(f32[1024,1152]{1,0:T(8,128)} %get-tuple-element.106.raw_ref.refs_0_, f32[1024,1024]{1,0:T(8,128)} %get-tuple-element.131.refs_1_, ...), custom_call_target="tpu_custom_call", output_to_operand_aliasing={{0}: (7, {})} | custom-call | tf_op jit(solution)/shard_map/scan_backward_1/pallas_call | solution.py:283
  186.2 9.2 %grad_normed.1 = (bf16[1024,1536]{1,0:T(8,128)(2,1)S(1)}, f32[8,1536]{1,0:T(8,128)S(1)}) custom-call(s32[3]{0:T(128)S(1)} %pad_add_fusion.place, bf16[1024,768]{1,0:T(8,128)(2,1)S(1)} %copy-done.5, bf16[1024,1152]{1,0:T(8,128)(2,1)} %get-tuple-element.143.refs_1_, bf16[1536,1536]{1,0:T(8,128)(2,1)S(1)} %bitcast.18, bf16[1536,1152]{1,0:T(8,128)(2,1)S(1)} %copy-done.11, ...), custom_call_target="tpu_custom_call" | custom-call | tf_op jit(solution)/shard_map/grad_normed/pallas_call | solution.py:650
  197.8 8.0 %grad_scan_proj.1 = (bf16[4,208,1152]{2,1,0:T(8,128)(2,1)S(1)}, bf16[4,208,1152]{2,1,0:T(8,128)(2,1)}) custom-call(s32[3]{0:T(128)S(1)} %pad_add_fusion.place, bf16[1024,1536]{1,0:T(8,128)(2,1)S(1)} %get-tuple-element.116.refs_13_.refs_0_.refs_4_, bf16[1024,1152]{1,0:T(8,128)(2,1)} %get-tuple-element.143.refs_1_, f32[8,1024]{1,0:T(8,128)S(1)} %copy-done.18, ...), custom_call_target="tpu_custom_call" | custom-call | tf_op jit(solution)/shard_map/grad_scan_proj/pallas_call | solution.py:588
  217.2 3.2 %collective-permute-start.41 = (bf16[208,1152]{1,0:T(8,128)(2,1)}, bf16[208,1152]{1,0:T(8,128)(2,1)}, u32[]{:S(2)}, u32[]{:S(2)}) collective-permute-start(bf16[208,1152]{1,0:T(8,128)(2,1)} %get-tuple-element.161), channel_id=1, source_target_pairs={{0,8},{4,12},{24,16},{28,20},{1,9},{5,13},{25,17},{29,21},{2,10},{... | collective-permute-start | bytes 1437704 | tf_op jit(solution)/shard_map/ppermute | solution.py:802
  227.6 2.8 %collective-permute-done.41.refs_0_ = bf16[208,1152]{1,0:T(8,128)(2,1)} collective-permute-done((bf16[208,1152]{1,0:T(8,128)(2,1)}, bf16[208,1152]{1,0:T(8,128)(2,1)}, u32[]{:S(2)}, u32[]{:S(2)}) %collective-permute-start.41) | collective-permute-done | bytes 479264 | tf_op jit(solution)/shard_map/ppermute | solution.py:802
  232.4 3.5 %collective-permute-start.44 = (bf16[208,1152]{1,0:T(8,128)(2,1)}, bf16[208,1152]{1,0:T(8,128)(2,1)}, u32[]{:S(2)}, u32[]{:S(2)}) collective-permute-start(bf16[208,1152]{1,0:T(8,128)(2,1)} %add_convert_fusion.1.refs_2_.refs_3_), channel_id=1, source_target_pairs={{0,16},{4,20},{8,24},{12,28},{16,0},{20,4},{24,8},{28,12},{1,17},{... | collective-permute-start | bytes 1437704 | tf_op jit(solution)/shard_map/ppermute | solution.py:793
  239.3 5.2 %collective-permute-done.40.refs_1_ = bf16[256,1536]{1,0:T(8,128)(2,1)} collective-permute-done((bf16[256,1536]{1,0:T(8,128)(2,1)}, bf16[256,1536]{1,0:T(8,128)(2,1)}, u32[]{:S(2)}, u32[]{:S(2)}) %collective-permute-start.40) | collective-permute-done | bytes 786464 | tf_op jit(solution)/shard_map/ppermute | solution.py:799
  248.7 4.6 %fusion.5 = (f32[256,1536]{1,0:T(8,128)}, bf16[256,1536]{1,0:T(8,128)(2,1)}) fusion(bf16[256,1536]{1,0:T(8,128)(2,1)S(1)} %copy-done.20, bf16[256,1536]{1,0:T(8,128)(2,1)S(1)} %copy-done.28, bf16[256,1536]{1,0:T(8,128)(2,1)} %get-tuple-element.166, bf16[256,1536]{1,0:T(8,128)(2,1)} %get-tuple-element.165, f32[256]{0:T(256)S(1)} %multiply_multiply_fusion, ...), kind=kLoop, calls=%fused_computation.8 | loop fusion | flops 7864320 | bytes 8658944 | tf_op jit(solution)/shard_map/sub | solution.py:1002
  253.4 3.6 %collective-permute-done.44.refs_3_ = bf16[208,1152]{1,0:T(8,128)(2,1)} collective-permute-done((bf16[208,1152]{1,0:T(8,128)(2,1)}, bf16[208,1152]{1,0:T(8,128)(2,1)}, u32[]{:S(2)}, u32[]{:S(2)}) %collective-permute-start.44) | collective-permute-done | bytes 479264 | tf_op jit(solution)/shard_map/ppermute | solution.py:793
  (265 shorter events, 110.4 us)
Async XLA Ops:
  3.5 30.7 %collective-permute-start = (bf16[256,1536]{1,0:T(8,128)(2,1)S(1)}, bf16[256,1536]{1,0:T(8,128)(2,1)S(1)}, u32[]{:S(2)}, u32[]{:S(2)}) collective-permute-start(bf16[256,1536]{1,0:T(8,128)(2,1)S(1)} %fusion.3.refs_0_), channel_id=1, source_target_pairs={{0,1},{1,0},{2,3},{3,2},{4,5},{5,4},{6,7},{7,6},{8,9},{9,8},{10,11... | collective-permute-start | bytes 2359304 | tf_op jit(solution)/shard_map/ppermute | solution.py:799
  6.5 29.1 %collective-permute-start.2 = (bf16[256,1536]{1,0:T(8,128)(2,1)S(1)}, bf16[256,1536]{1,0:T(8,128)(2,1)}, u32[]{:S(2)}, u32[]{:S(2)}) collective-permute-start(bf16[256,1536]{1,0:T(8,128)(2,1)S(1)} %fusion.3.refs_0_), channel_id=1, source_target_pairs={{0,2},{1,3},{2,0},{3,1},{4,6},{5,7},{6,4},{7,5},{8,10},{9,11},{10,... | collective-permute-start | bytes 2359304 | tf_op jit(solution)/shard_map/ppermute | solution.py:799
  8.3 20.8 %collective-permute-start.4 = (bf16[192,1152]{1,0:T(8,128)(2,1)S(1)}, bf16[192,1152]{1,0:T(8,128)(2,1)S(1)}, u32[]{:S(2)}, u32[]{:S(2)}) collective-permute-start(bf16[192,1152]{1,0:T(8,128)(2,1)S(1)} %concatenate.24.refs_0_), channel_id=1, source_target_pairs={{0,8},{4,12},{8,0},{12,4},{16,24},{20,28},{24,16},{28,20},{1,9},{5... | collective-permute-start | bytes 1327112 | tf_op jit(solution)/shard_map/ppermute | solution.py:793
  10.0 21.5 %collective-permute-start.5 = (bf16[192,1152]{1,0:T(8,128)(2,1)S(1)}, bf16[192,1152]{1,0:T(8,128)(2,1)S(1)}, u32[]{:S(2)}, u32[]{:S(2)}) collective-permute-start(bf16[192,1152]{1,0:T(8,128)(2,1)S(1)} %concatenate.24.refs_0_), channel_id=1, source_target_pairs={{0,16},{4,20},{8,24},{12,28},{16,0},{20,4},{24,8},{28,12},{1,17},{... | collective-permute-start | bytes 1327112 | tf_op jit(solution)/shard_map/ppermute | solution.py:793
  46.9 30.9 %collective-permute-start.16 = (bf16[192,1536]{1,0:T(8,128)(2,1)}, bf16[192,1536]{1,0:T(8,128)(2,1)}, u32[]{:S(2)}, u32[]{:S(2)}) collective-permute-start(bf16[192,1536]{1,0:T(8,128)(2,1)} %pinned.23.refs_0_), channel_id=1, source_target_pairs={{0,8},{4,12},{8,0},{12,4},{16,24},{20,28},{24,16},{28,20},{1,9},{5... | collective-permute-start | bytes 1769480 | tf_op jit(solution)/shard_map/ppermute | solution.py:793
  52.4 28.9 %collective-permute-start.17 = (bf16[192,1536]{1,0:T(8,128)(2,1)}, bf16[192,1536]{1,0:T(8,128)(2,1)}, u32[]{:S(2)}, u32[]{:S(2)}) collective-permute-start(bf16[192,1536]{1,0:T(8,128)(2,1)} %pinned.23.refs_0_), channel_id=1, source_target_pairs={{0,16},{4,20},{8,24},{12,28},{16,0},{20,4},{24,8},{28,12},{1,17},{... | collective-permute-start | bytes 1769480 | tf_op jit(solution)/shard_map/ppermute | solution.py:793
  54.2 29.9 %collective-permute-start.12 = (bf16[256,1536]{1,0:T(8,128)(2,1)}, bf16[256,1536]{1,0:T(8,128)(2,1)}, u32[]{:S(2)}, u32[]{:S(2)}) collective-permute-start(bf16[256,1536]{1,0:T(8,128)(2,1)} %pinned.21.refs_0_), channel_id=1, source_target_pairs={{0,1},{1,0},{2,3},{3,2},{4,5},{5,4},{6,7},{7,6},{8,9},{9,8},{10,11... | collective-permute-start | bytes 2359304 | tf_op jit(solution)/shard_map/ppermute | solution.py:799
  55.7 30.2 %collective-permute-start.13 = (bf16[256,1536]{1,0:T(8,128)(2,1)}, bf16[256,1536]{1,0:T(8,128)(2,1)}, u32[]{:S(2)}, u32[]{:S(2)}) collective-permute-start(bf16[256,1536]{1,0:T(8,128)(2,1)} %pinned.21.refs_0_), channel_id=1, source_target_pairs={{0,2},{1,3},{2,0},{3,1},{4,6},{5,7},{6,4},{7,5},{8,10},{9,11},{10,... | collective-permute-start | bytes 2359304 | tf_op jit(solution)/shard_map/ppermute | solution.py:799
  82.8 16.4 %collective-permute-start.19 = (bf16[192,1536]{1,0:T(8,128)(2,1)}, bf16[192,1536]{1,0:T(8,128)(2,1)}, u32[]{:S(2)}, u32[]{:S(2)}) collective-permute-start(bf16[192,1536]{1,0:T(8,128)(2,1)} %get-tuple-element.112.refs_2_), channel_id=1, source_target_pairs={{8,0},{12,4},{16,24},{20,28},{9,1},{13,5},{17,25},{21,29},{10,2},{... | collective-permute-start | bytes 1769480 | tf_op jit(solution)/shard_map/ppermute | solution.py:802
  87.7 14.3 %collective-permute-start.14 = (bf16[128,1536]{1,0:T(8,128)(2,1)}, bf16[128,1536]{1,0:T(8,128)(2,1)}, u32[]{:S(2)}, u32[]{:S(2)}) collective-permute-start(bf16[128,1536]{1,0:T(8,128)(2,1)} %get-tuple-element.108), channel_id=1, source_target_pairs={{0,2},{1,3},{2,0},{3,1},{4,6},{5,7},{6,4},{7,5},{8,10},{9,11},{10,... | collective-permute-start | bytes 1179656 | tf_op jit(solution)/shard_map/ppermute | solution.py:799
  142.2 21.0 %collective-permute-start.28 = (bf16[192,1536]{1,0:T(8,128)(2,1)}, bf16[192,1536]{1,0:T(8,128)(2,1)}, u32[]{:S(2)}, u32[]{:S(2)}) collective-permute-start(bf16[192,1536]{1,0:T(8,128)(2,1)} %get-tuple-element.127), channel_id=1, source_target_pairs={{0,8},{4,12},{24,16},{28,20},{1,9},{5,13},{25,17},{29,21},{2,10},{... | collective-permute-start | bytes 1769480 | tf_op jit(solution)/shard_map/ppermute | solution.py:802
  144.5 18.7 %collective-permute-start.29 = (bf16[192,1536]{1,0:T(8,128)(2,1)}, bf16[192,1536]{1,0:T(8,128)(2,1)}, u32[]{:S(2)}, u32[]{:S(2)}) collective-permute-start(bf16[192,1536]{1,0:T(8,128)(2,1)} %get-tuple-element.127), channel_id=1, source_target_pairs={{8,16},{12,20},{16,8},{20,12},{9,17},{13,21},{17,9},{21,13},{10,18... | collective-permute-start | bytes 1769480 | tf_op jit(solution)/shard_map/ppermute | solution.py:802
  147.2 16.0 %collective-permute-start.30 = (bf16[128,1536]{1,0:T(8,128)(2,1)}, bf16[128,1536]{1,0:T(8,128)(2,1)}, u32[]{:S(2)}, u32[]{:S(2)}) collective-permute-start(bf16[128,1536]{1,0:T(8,128)(2,1)} %get-tuple-element.129), channel_id=1, source_target_pairs={{0,2},{1,3},{2,0},{3,1},{4,6},{5,7},{6,4},{7,5},{8,10},{9,11},{10,... | collective-permute-start | bytes 1179656 | tf_op jit(solution)/shard_map/ppermute | solution.py:799
  148.3 14.8 %collective-permute-start.31 = (bf16[128,1536]{1,0:T(8,128)(2,1)}, bf16[128,1536]{1,0:T(8,128)(2,1)}, u32[]{:S(2)}, u32[]{:S(2)}) collective-permute-start(bf16[128,1536]{1,0:T(8,128)(2,1)} %get-tuple-element.130), channel_id=1, source_target_pairs={{0,1},{1,0},{2,3},{3,2},{4,5},{5,4},{6,7},{7,6},{8,9},{9,8},{10,11... | collective-permute-start | bytes 1179656 | tf_op jit(solution)/shard_map/ppermute | solution.py:799
  165.8 32.0 %collective-permute-start.33 = (bf16[256,1536]{1,0:T(8,128)(2,1)}, bf16[256,1536]{1,0:T(8,128)(2,1)}, u32[]{:S(2)}, u32[]{:S(2)}) collective-permute-start(bf16[256,1536]{1,0:T(8,128)(2,1)} %pad_maximum_fusion.1), channel_id=1, source_target_pairs={{0,2},{1,3},{2,0},{3,1},{4,6},{5,7},{6,4},{7,5},{8,10},{9,11},{10,... | collective-permute-start | bytes 2359304 | tf_op jit(solution)/shard_map/ppermute | solution.py:799
  167.6 30.2 %collective-permute-start.32 = (bf16[256,1536]{1,0:T(8,128)(2,1)}, bf16[256,1536]{1,0:T(8,128)(2,1)}, u32[]{:S(2)}, u32[]{:S(2)}) collective-permute-start(bf16[256,1536]{1,0:T(8,128)(2,1)} %pad_maximum_fusion), channel_id=1, source_target_pairs={{0,1},{1,0},{2,3},{3,2},{4,5},{5,4},{6,7},{7,6},{8,9},{9,8},{10,11... | collective-permute-start | bytes 2359304 | tf_op jit(solution)/shard_map/ppermute | solution.py:799
  170.5 26.8 %collective-permute-start.35 = (bf16[192,1536]{1,0:T(8,128)(2,1)S(1)}, bf16[192,1536]{1,0:T(8,128)(2,1)S(1)}, u32[]{:S(2)}, u32[]{:S(2)}) collective-permute-start(bf16[192,1536]{1,0:T(8,128)(2,1)S(1)} %add_convert_fusion), channel_id=1, source_target_pairs={{0,16},{4,20},{8,24},{12,28},{16,0},{20,4},{24,8},{28,12},{1,17},{... | collective-permute-start | bytes 1769480 | tf_op jit(solution)/shard_map/ppermute | solution.py:793
  171.2 26.5 %collective-permute-start.34 = (bf16[192,1536]{1,0:T(8,128)(2,1)S(1)}, bf16[192,1536]{1,0:T(8,128)(2,1)S(1)}, u32[]{:S(2)}, u32[]{:S(2)}) collective-permute-start(bf16[192,1536]{1,0:T(8,128)(2,1)S(1)} %copy-done.7), channel_id=1, source_target_pairs={{0,8},{4,12},{8,0},{12,4},{16,24},{20,28},{24,16},{28,20},{1,9},{5... | collective-permute-start | bytes 1769480 | tf_op jit(solution)/shard_map/ppermute | solution.py:793
  208.4 13.4 %collective-permute-start.36 = (bf16[128,1536]{1,0:T(8,128)(2,1)}, bf16[128,1536]{1,0:T(8,128)(2,1)S(1)}, u32[]{:S(2)}, u32[]{:S(2)}) collective-permute-start(bf16[128,1536]{1,0:T(8,128)(2,1)} %get-tuple-element.149), channel_id=1, source_target_pairs={{0,2},{1,3},{2,0},{3,1},{4,6},{5,7},{6,4},{7,5},{8,10},{9,11},{10,... | collective-permute-start | bytes 1179656 | tf_op jit(solution)/shard_map/ppermute | solution.py:799
  217.2 13.2 %collective-permute-start.41 = (bf16[208,1152]{1,0:T(8,128)(2,1)}, bf16[208,1152]{1,0:T(8,128)(2,1)}, u32[]{:S(2)}, u32[]{:S(2)}) collective-permute-start(bf16[208,1152]{1,0:T(8,128)(2,1)} %get-tuple-element.161), channel_id=1, source_target_pairs={{0,8},{4,12},{24,16},{28,20},{1,9},{5,13},{25,17},{29,21},{2,10},{... | collective-permute-start | bytes 1437704 | tf_op jit(solution)/shard_map/ppermute | solution.py:802
  224.9 19.6 %collective-permute-start.40 = (bf16[256,1536]{1,0:T(8,128)(2,1)}, bf16[256,1536]{1,0:T(8,128)(2,1)}, u32[]{:S(2)}, u32[]{:S(2)}) collective-permute-start(bf16[256,1536]{1,0:T(8,128)(2,1)} %pad_maximum_fusion.3), channel_id=1, source_target_pairs={{0,2},{1,3},{2,0},{3,1},{4,6},{5,7},{6,4},{7,5},{8,10},{9,11},{10,... | collective-permute-start | bytes 2359304 | tf_op jit(solution)/shard_map/ppermute | solution.py:799
  227.0 19.3 %collective-permute-start.39 = (bf16[256,1536]{1,0:T(8,128)(2,1)}, bf16[256,1536]{1,0:T(8,128)(2,1)}, u32[]{:S(2)}, u32[]{:S(2)}) collective-permute-start(bf16[256,1536]{1,0:T(8,128)(2,1)} %pad_maximum_fusion.2), channel_id=1, source_target_pairs={{0,1},{1,0},{2,3},{3,2},{4,5},{5,4},{6,7},{7,6},{8,9},{9,8},{10,11... | collective-permute-start | bytes 2359304 | tf_op jit(solution)/shard_map/ppermute | solution.py:799
  232.4 24.5 %collective-permute-start.44 = (bf16[208,1152]{1,0:T(8,128)(2,1)}, bf16[208,1152]{1,0:T(8,128)(2,1)}, u32[]{:S(2)}, u32[]{:S(2)}) collective-permute-start(bf16[208,1152]{1,0:T(8,128)(2,1)} %add_convert_fusion.1.refs_2_.refs_3_), channel_id=1, source_target_pairs={{0,16},{4,20},{8,24},{12,28},{16,0},{20,4},{24,8},{28,12},{1,17},{... | collective-permute-start | bytes 1437704 | tf_op jit(solution)/shard_map/ppermute | solution.py:793
  235.9 21.0 %collective-permute-start.43 = (bf16[208,1152]{1,0:T(8,128)(2,1)}, bf16[208,1152]{1,0:T(8,128)(2,1)}, u32[]{:S(2)}, u32[]{:S(2)}) collective-permute-start(bf16[208,1152]{1,0:T(8,128)(2,1)} %get-tuple-element.168), channel_id=1, source_target_pairs={{0,8},{4,12},{8,0},{12,4},{16,24},{20,28},{24,16},{28,20},{1,9},{5... | collective-permute-start | bytes 1437704 | tf_op jit(solution)/shard_map/ppermute | solution.py:793
  (81 other events, 548.1 us)

commit v5 on v4

--- a/solution.py
+++ b/solution.py
@@ -595,26 +595,38 @@
             out_specs=[out, out],
             scratch_shapes=[pltpu.VMEM((SMALL, columns), f32)] if small else [],
         ),
-        out_shape=[jax.ShapeDtypeStruct((chips, height, columns), bf16)] * 2,
+        out_shape=[(pltpu.HBM if small else NEAR)((chips, height, columns), bf16)] * 2,
         compiler_params=pltpu.CompilerParams(vmem_limit_bytes=SMALL_LIMIT),
         name=name,
     )(place, *rows, *lows, *small, *earlier)
 
 
-def pairs_kernel(chips, *refs):
-    keep, come, own, others = refs[0], refs[1], refs[-chips], refs[1 - chips :]
-    own[...] = keep[0].astype(f32) + come[0].astype(f32)
-    for k in range(1, chips):
-        others[k - 1][...] = (keep[k].astype(f32) + come[k].astype(f32)).astype(bf16)
-
-
-def pairs(keep, come, earlier=()):
+def pairs_kernel(chips, streamed, keep, come, *refs):
+    if streamed:
+        refs, (kept, arrived, sems) = refs[:-3], refs[-3:]
+        copies = []
+        for k in range(chips):
+            for i, (source, target) in enumerate(((keep, kept), (come, arrived))):
+                copies.append(pltpu.make_async_copy(source.at[k], target.at[k], sems.at[2 * k + i]))
+        for copy in copies:
+            copy.start()
+        keep, come = kept, arrived
+    for k, out in enumerate(refs[-chips:]):
+        if streamed:
+            copies[2 * k].wait()
+            copies[2 * k + 1].wait()
+        out[...] = (keep[k].astype(f32) + come[k].astype(f32)).astype(out.dtype)
+
+
+def pairs(keep, come, streamed, earlier=()):
     chips, rows, columns = keep.shape
+    scratch = [pltpu.VMEM(keep.shape, bf16)] * 2 + [pltpu.SemaphoreType.DMA((2 * chips,))]
     out = pl.pallas_call(
-        functools.partial(pairs_kernel, chips),
-        in_specs=[in_vmem, in_vmem] + [anywhere] * len(earlier),
+        functools.partial(pairs_kernel, chips, streamed),
+        in_specs=[anywhere if streamed else in_vmem] * 2 + [anywhere] * len(earlier),
         out_specs=[in_vmem] * chips,
         out_shape=[pltpu.HBM((rows, columns), f32)] + [pltpu.HBM((rows, columns), bf16)] * (chips - 1),
+        scratch_shapes=scratch if streamed else [],
         compiler_params=pltpu.CompilerParams(vmem_limit_bytes=SMALL_LIMIT),
         name="pairs",
     )(keep, come, *earlier)
@@ -725,9 +737,9 @@
     small = add_up(parts, slice(shard, shard + SMALL), every)
     taps[...] = small[0:CONV]
     bias[...] = small[CONV : CONV + 1]
-    for row in range(6):
-        cols = slice(row * 2 * STATE, (row + 1) * 2 * STATE)
-        norm[:, cols] = small[8 + row : 9 + row] / norm_gain[:, cols]
+    for piece in range(norm.shape[0]):
+        row, cols = 8 + piece // 2, slice(piece % 2 * LANES, (piece % 2 + 1) * LANES)
+        norm[piece : piece + 1] = small[row : row + 1, cols] / norm_gain[piece : piece + 1]
 
 
 def finish(parts, norm_gain):
@@ -869,6 +881,13 @@
             return [lax.psum_scatter(blocks[0], "tensor", scatter_dimension=0, tiled=True)]
         came = [self.over_tensor(blocks[k], k) for k in (1, 2)]
         return [blocks[0]] + (pinned(came, earlier) if earlier else came)
+
+    def scatter_direct(self, rows, earlier):
+        if self.tensor != 4:
+            return [lax.psum_scatter(rows, "tensor", scatter_dimension=0, tiled=True)]
+        own, *others = jnp.split(rows, 4)
+        others = pinned(others, earlier)
+        return [own] + [self.over_tensor(block, k + 1) for k, block in enumerate(others)]
 
     def spread_tensor(self, values):
         return [values] + [self.over_tensor(values, k) for k in range(1, self.tensor)]
@@ -958,17 +977,14 @@
     )
     joint_come = net.over_core(give)
     branch, _ = back(place, [out_low], [(joint_full, 1)], None, "branch", [give])
-    joint_own, joint_others = pairs(keep, joint_come, [branch])
+    joint_own, joint_others = pairs(keep, joint_come, False, [branch])
     came = net.scatter_far(joint_others)
-    branch_came = net.scatter_first(branch, joint_others[:1])
+    branch_parts = net.scatter_direct(branch, joint_others[:1])
     held = scan_backward(
         0, raw, pre, scan_grad, states, taps, head_rows, skip_row, None, joint_others[:1]
     )
-    if came:
-        *came, one, two = pinned(came + branch_came, [held[1]])
-        branch_came = [one, two]
+    came = pinned(came, [held[1]]) if came else came
     joint_arrived = net.scatter_near(net.scatter_join(joint_others, came), came)
-    branch_parts = net.scatter_last(net.scatter_blocks(branch, branch_came), [])
     scan_back, sums, head_sums, _, _ = scan_backward(
         1, raw, pre, scan_grad, states, taps, head_rows, skip_row, held, came
     )
@@ -985,7 +1001,7 @@
         joint_arrived + branch_parts[1:],
     )
     norm_came = net.scatter_first(norm_rows, joint_arrived)
-    scan_own, scan_others = pairs(keep, net.over_core(give))
+    scan_own, scan_others = pairs(stay(keep), stay(net.over_core(give)), True)
     came = net.scatter_far(scan_others)
     came = pinned(came, []) if came else came
     norm_came = pinned(norm_came, scan_others[:1]) if norm_came else norm_came
@@ -1007,7 +1023,7 @@
         [scan_own] + scan_arrived, channels, []
     )
     grad_shared_proj, grad_conv_shared, shared_bias, norm_part = finish(
-        net.spread_tensor(common), norm_gain[None]
+        net.spread_tensor(common), norm_gain.reshape(-1, LANES)
     )
     return (
         mixed,

time: 272 us -> 266 us (0.978)
  other arithmetic: 28.3 us -> 23.9 us
  local copies, waits for them, and re-layouts: 26.1 us -> 21.8 us
  Pallas kernels: 103 us -> 106 us
    ppermute x8, waiting for transfers between devices: 11.3 us -> 17.1 us  [between(): lax.ppermute(values, 'dp', [(2 * a + c, 2 * b + c) for a, b in pairs for...]
    unnamed x117 -> x105, local copies, waits for them, and re-layouts: 15.9 us -> 12 us
    ppermute x22 -> x21, starting transfers between devices: 26.2 us -> 23 us  [over_tensor(): lax.ppermute(values, 'tensor', [(i, i ^ k) for i in range(self.tensor)])]
    ppermute x22 -> x21, waiting for transfers between devices: 12 us -> 10.6 us  [over_tensor(): lax.ppermute(values, 'tensor', [(i, i ^ k) for i in range(self.tensor)])]
  transfers between devices with their start and end apart: 48 -> 47, of which waited for: 18 -> 22; matrix products, arithmetic and copies ran while one was open for 13% -> 13% of each run, Pallas kernels for 25% -> 26%
where the time goes in v5:
time: 266 us; the launch traced here: 264 us
  Pallas kernels  106 us (40%)
  waiting for transfers between devices  57 us (21%)
  starting transfers between devices  54.7 us (21%)
  other arithmetic  23.9 us (9%)
  local copies, waits for them, and re-layouts  21.8 us (8%)
    pallas_call x2, Pallas kernels, scan_backward(): pl.pallas_call(functools.partial(backward_kernel, part, len(earlier)), gr...  27.2 us
    ppermute x8, waiting for transfers between devices, over_chips(): return lax.ppermute(values, 'dp', [(i, i ^ 2 * k) for i in range(self.dp)])  26 us
    ppermute x21, starting transfers between devices, over_tensor(): lax.ppermute(values, 'tensor', [(i, i ^ k) for i in range(self.tensor)])  23 us
    pallas_call x2, Pallas kernels, product(): pl.pallas_call(functools.partial(product_kernel, heights, chips, epilogue...  20 us
    ppermute x8, waiting for transfers between devices, between(): lax.ppermute(values, 'dp', [(2 * a + c, 2 * b + c) for a, b in pairs for...  17.1 us
    ppermute x8, starting transfers between devices, between(): lax.ppermute(values, 'dp', [(2 * a + c, 2 * b + c) for a, b in pairs for...  15.1 us
    pallas_call x2, Pallas kernels, weight_grads(): pl.pallas_call(functools.partial(small_kernel if small else grads_kernel,...  14.7 us
    ppermute x8, starting transfers between devices, over_chips(): return lax.ppermute(values, 'dp', [(i, i ^ 2 * k) for i in range(self.dp)])  14.3 us
  transfers between devices with their start and end apart: 47, of which 22 were waited for; matrix products, arithmetic and copies ran while one was open for 13% of the time, Pallas kernels for 26%

profile of v5, /device:TPU:0, one launch (start us, length us, event | category | flops | bytes accessed | tf_op | source)
XLA Modules:
  0.0 264.5 jit_solution(6270556825137203954)
XLA Ops:
  3.5 3.0 %collective-permute-start.2 = (bf16[256,1536]{1,0:T(8,128)(2,1)S(1)}, bf16[256,1536]{1,0:T(8,128)(2,1)}, u32[]{:S(2)}, u32[]{:S(2)}) collective-permute-start(bf16[256,1536]{1,0:T(8,128)(2,1)S(1)} %fusion.3.refs_0_), channel_id=1, source_target_pairs={{0,2},{1,3},{2,0},{3,1},{4,6},{5,7},{6,4},{7,5},{8,10},{9,11},{10,... | collective-permute-start | bytes 2359304 | tf_op jit(solution)/shard_map/ppermute | solution.py:811
  8.3 2.7 %collective-permute-start.5 = (bf16[192,1152]{1,0:T(8,128)(2,1)S(1)}, bf16[192,1152]{1,0:T(8,128)(2,1)S(1)}, u32[]{:S(2)}, u32[]{:S(2)}) collective-permute-start(bf16[192,1152]{1,0:T(8,128)(2,1)S(1)} %concatenate.18.refs_0_), channel_id=1, source_target_pairs={{0,16},{4,20},{8,24},{12,28},{16,0},{20,4},{24,8},{28,12},{1,17},{... | collective-permute-start | bytes 1327112 | tf_op jit(solution)/shard_map/ppermute | solution.py:805
  12.6 17.7 %collective-permute-done.5.refs_2_ = bf16[192,1152]{1,0:T(8,128)(2,1)S(1)} collective-permute-done((bf16[192,1152]{1,0:T(8,128)(2,1)S(1)}, bf16[192,1152]{1,0:T(8,128)(2,1)S(1)}, u32[]{:S(2)}, u32[]{:S(2)}) %collective-permute-start.5) | collective-permute-done | bytes 442400 | tf_op jit(solution)/shard_map/ppermute | solution.py:805
  42.9 3.2 %collective-permute-done.10 = bf16[192,1152]{1,0:T(8,128)(2,1)S(1)} collective-permute-done((bf16[192,1152]{1,0:T(8,128)(2,1)}, bf16[192,1152]{1,0:T(8,128)(2,1)S(1)}, u32[]{:S(2)}, u32[]{:S(2)}) %collective-permute-start.10) | collective-permute-done | bytes 442400 | tf_op jit(solution)/shard_map/ppermute | solution.py:814
  49.6 3.2 %collective-permute-start.17 = (bf16[192,1536]{1,0:T(8,128)(2,1)}, bf16[192,1536]{1,0:T(8,128)(2,1)}, u32[]{:S(2)}, u32[]{:S(2)}) collective-permute-start(bf16[192,1536]{1,0:T(8,128)(2,1)} %pinned.23.refs_0_), channel_id=1, source_target_pairs={{0,16},{4,20},{8,24},{12,28},{16,0},{20,4},{24,8},{28,12},{1,17},{... | collective-permute-start | bytes 1769480 | tf_op jit(solution)/shard_map/ppermute | solution.py:805
  57.2 9.0 %project.1 = (f32[1024,1152]{1,0:T(8,128)}, bf16[1536,1152]{1,0:T(8,128)(2,1)S(1)}, bf16[1024,1536]{1,0:T(8,128)(2,1)S(1)}) custom-call(s32[3]{0:T(128)S(1)} %pad_add_fusion.place, bf16[256,1536]{1,0:T(8,128)(2,1)} %copy-done.24, bf16[256,1536]{1,0:T(8,128)(2,1)} %copy-done.20, bf16[256,1536]{1,0:T(8,128)(2,1)} %collective-permute-done.2.refs_2_, ...), custom_call_target="tpu_custom_call" | custom-call | tf_op jit(solution)/shard_map/project/pallas_call | solution.py:394
  66.2 11.5 %scan_forward.1 = (f32[1024,768]{1,0:T(8,128)}, f32[1024,1024]{1,0:T(8,128)}, bf16[1024,768]{1,0:T(8,128)(2,1)}) custom-call(f32[1024,1152]{1,0:T(8,128)} %get-tuple-element.105.raw_ref.refs_0_, f32[8,1024]{1,0:T(8,128)S(1)} %fusion.11.taps_ref.refs_4_, f32[8,128]{1,0:T(8,128)S(1)} %select_maximum_fusion.2.heads_ref.refs_5_, ...), custom_call_target="tpu_custom_call" | custom-call | tf_op jit(solution)/shard_map/scan_forward/pallas_call | solution.py:250
  88.7 10.2 %collective-permute-done.19 = bf16[192,1536]{1,0:T(8,128)(2,1)} collective-permute-done((bf16[192,1536]{1,0:T(8,128)(2,1)}, bf16[192,1536]{1,0:T(8,128)(2,1)}, u32[]{:S(2)}, u32[]{:S(2)}) %collective-permute-start.19) | collective-permute-done | bytes 589856 | tf_op jit(solution)/shard_map/ppermute | solution.py:814
  104.9 11.0 %mix.1 = (f32[1024,768]{1,0:T(8,128)S(1)}, f32[1024,768]{1,0:T(8,128)S(1)}, f32[1024,768]{1,0:T(8,128)S(1)}, f32[16,128]{1,0:T(8,128)S(1)}, bf16[1536,1536]{1,0:...) custom-call(s32[3]{0:T(128)S(1)} %pad_add_fusion.place, bf16[256,1536]{1,0:T(8,128)(2,1)} %pinned.21.refs_0_, ...), custom_call_target="tpu_custom_call" | custom-call | tf_op jit(solution)/shard_map/mix/pallas_call | solution.py:394
  122.4 5.2 %gating.1 = (bf16[1024,768]{1,0:T(8,128)(2,1)S(1)}, bf16[1024,768]{1,0:T(8,128)(2,1)S(1)}, bf16[1024,768]{1,0:T(8,128)(2,1)}, f32[8,768]{1,0:T(8,128)S(1)}) custom-call(f32[1024,768]{1,0:T(8,128)S(1)} %get-tuple-element.116.grad_out, f32[1024,768]{1,0:T(8,128)S(1)} %get-tuple-element.117.gated, f32[1024,768]{1,0:T(8,128)S(1)} %get-tuple-element.118.gate, ...), custom_call_target="tpu_custom_call" | custom-call | tf_op jit(solution)/shard_map/gating/pallas_call | solution.py:498
  127.6 6.5 %grad_joint_proj.1 = (bf16[4,192,1536]{2,1,0:T(8,128)(2,1)S(1)}, bf16[4,192,1536]{2,1,0:T(8,128)(2,1)S(1)}) custom-call(s32[3]{0:T(128)S(1)} %pad_add_fusion.place, bf16[1024,1536]{1,0:T(8,128)(2,1)S(1)} %get-tuple-element.115.refs_13_.refs_0_.refs_4_, bf16[1024,1536]{1,0:T(8,128)(2,1)S(1)} %get-tuple-element.122.refs_1_, ...), custom_call_target="tpu_custom_call" | custom-call | tf_op jit(solution)/shard_map/grad_joint_proj/pallas_call | solution.py:588
  134.2 3.8 %branch.1.refs_0_ = bf16[1024,1536]{1,0:T(8,128)(2,1)S(1)} custom-call(s32[3]{0:T(128)S(1)} %pad_add_fusion.place, bf16[1024,768]{1,0:T(8,128)(2,1)S(1)} %get-tuple-element.120.refs_3_.refs_0_, bf16[1536,1536]{1,0:T(8,128)(2,1)S(1)} %get-tuple-element.121.refs_1_.refs_2_, bf16[4,192,1536]{2,1,0:T(8,128)(2,1)S(1)} %get-tuple-element.124.refs_2_), custom_call_target="tpu_custom_call" | custom-call | tf_op jit(solution)/shard_map/branch/pallas_call | solution.py:662
  142.2 3.4 %collective-permute-start.31 = (bf16[192,1536]{1,0:T(8,128)(2,1)}, bf16[192,1536]{1,0:T(8,128)(2,1)}, u32[]{:S(2)}, u32[]{:S(2)}) collective-permute-start(bf16[192,1536]{1,0:T(8,128)(2,1)} %get-tuple-element.138), channel_id=1, source_target_pairs={{0,8},{4,12},{24,16},{28,20},{1,9},{5,13},{25,17},{29,21},{2,10},{... | collective-permute-start | bytes 1769480 | tf_op jit(solution)/shard_map/ppermute | solution.py:814
  151.6 13.2 %scan_backward_0.1 = (bf16[1024,1152]{1,0:T(8,128)(2,1)}, f32[8,1024]{1,0:T(8,128)}, f32[8,128]{1,0:T(8,128)}, f32[128,768]{1,0:T(8,128)}, f32[8,1024]{1,0:T(8,128)}) custom-call(f32[1024,1152]{1,0:T(8,128)} %get-tuple-element.105.raw_ref.refs_0_, f32[1024,1024]{1,0:T(8,128)} %get-tuple-element.130.refs_1_, bf16[1024,768]{1,0:T(8,128)(2,1)} %get-tuple-element.131.refs_2_, ...), custom_call_target="tpu_custom_call" | custom-call | tf_op jit(solution)/shard_map/scan_backward_0/pallas_call | solution.py:283
  166.4 2.8 %collective-permute-start.33 = (bf16[192,1536]{1,0:T(8,128)(2,1)S(1)}, bf16[192,1536]{1,0:T(8,128)(2,1)S(1)}, u32[]{:S(2)}, u32[]{:S(2)}) collective-permute-start(bf16[192,1536]{1,0:T(8,128)(2,1)S(1)} %copy-done.7), channel_id=1, source_target_pairs={{0,8},{4,12},{8,0},{12,4},{16,24},{20,28},{24,16},{28,20},{1,9},{5... | collective-permute-start | bytes 1769480 | tf_op jit(solution)/shard_map/ppermute | solution.py:805
  169.3 14.0 %scan_backward_1.1 = (bf16[1024,1152]{1,0:T(8,128)(2,1)}, f32[8,1024]{1,0:T(8,128)}, f32[8,128]{1,0:T(8,128)}, f32[128,768]{1,0:T(8,128)}, f32[8,1024]{1,0:T(8,128)}) custom-call(f32[1024,1152]{1,0:T(8,128)} %get-tuple-element.105.raw_ref.refs_0_, f32[1024,1024]{1,0:T(8,128)} %get-tuple-element.130.refs_1_, ...), custom_call_target="tpu_custom_call", output_to_operand_aliasing={{0}: (7, {})} | custom-call | tf_op jit(solution)/shard_map/scan_backward_1/pallas_call | solution.py:283
  183.4 9.2 %grad_normed.1 = (bf16[1024,1536]{1,0:T(8,128)(2,1)S(1)}, f32[8,1536]{1,0:T(8,128)S(1)}) custom-call(s32[3]{0:T(128)S(1)} %pad_add_fusion.place, bf16[1024,768]{1,0:T(8,128)(2,1)S(1)} %copy-done.5, bf16[1024,1152]{1,0:T(8,128)(2,1)} %get-tuple-element.141.refs_1_, bf16[1536,1536]{1,0:T(8,128)(2,1)S(1)} %bitcast.20, bf16[1536,1152]{1,0:T(8,128)(2,1)S(1)} %copy-done.11, ...), custom_call_target="tpu_custom_call" | custom-call | tf_op jit(solution)/shard_map/grad_normed/pallas_call | solution.py:662
  194.1 8.2 %grad_scan_proj.1 = (bf16[4,208,1152]{2,1,0:T(8,128)(2,1)}, bf16[4,208,1152]{2,1,0:T(8,128)(2,1)}) custom-call(s32[3]{0:T(128)S(1)} %pad_add_fusion.place, bf16[1024,1536]{1,0:T(8,128)(2,1)S(1)} %get-tuple-element.115.refs_13_.refs_0_.refs_4_, bf16[1024,1152]{1,0:T(8,128)(2,1)} %get-tuple-element.141.refs_1_, f32[8,1024]{1,0:T(8,128)S(1)} %copy-done.14, ...), custom_call_target="tpu_custom_call" | custom-call | tf_op jit(solution)/shard_map/grad_scan_proj/pallas_call | solution.py:588
  207.8 3.7 %pairs.3 = (f32[208,1152]{1,0:T(8,128)}, bf16[208,1152]{1,0:T(8,128)(2,1)}, bf16[208,1152]{1,0:T(8,128)(2,1)}, bf16[208,1152]{1,0:T(8,128)(2,1)}) custom-call(bf16[4,208,1152]{2,1,0:T(8,128)(2,1)} %get-tuple-element.153.keep, bf16[4,208,1152]{2,1,0:T(8,128)(2,1)} %copy-done.25), custom_call_target="tpu_custom_call" | custom-call | tf_op jit(solution)/shard_map/pairs/pallas_call | solution.py:624
  212.9 4.1 %collective-permute-start.40 = (bf16[208,1152]{1,0:T(8,128)(2,1)}, bf16[208,1152]{1,0:T(8,128)(2,1)}, u32[]{:S(2)}, u32[]{:S(2)}) collective-permute-start(bf16[208,1152]{1,0:T(8,128)(2,1)} %get-tuple-element.159), channel_id=1, source_target_pairs={{0,8},{4,12},{24,16},{28,20},{1,9},{5,13},{25,17},{29,21},{2,10},{... | collective-permute-start | bytes 1437704 | tf_op jit(solution)/shard_map/ppermute | solution.py:814
  223.1 3.6 %collective-permute-done.40.refs_0_ = bf16[208,1152]{1,0:T(8,128)(2,1)} collective-permute-done((bf16[208,1152]{1,0:T(8,128)(2,1)}, bf16[208,1152]{1,0:T(8,128)(2,1)}, u32[]{:S(2)}, u32[]{:S(2)}) %collective-permute-start.40) | collective-permute-done | bytes 479264 | tf_op jit(solution)/shard_map/ppermute | solution.py:814
  234.5 4.9 %collective-permute-done.38.refs_0_ = bf16[256,1536]{1,0:T(8,128)(2,1)} collective-permute-done((bf16[256,1536]{1,0:T(8,128)(2,1)}, bf16[256,1536]{1,0:T(8,128)(2,1)}, u32[]{:S(2)}, u32[]{:S(2)}) %collective-permute-start.38) | collective-permute-done | bytes 786464 | tf_op jit(solution)/shard_map/ppermute | solution.py:811
  243.4 5.0 %fusion.5 = (f32[256,1536]{1,0:T(8,128)}, bf16[256,1536]{1,0:T(8,128)(2,1)}) fusion(bf16[256,1536]{1,0:T(8,128)(2,1)S(1)} %copy-done.16, bf16[256,1536]{1,0:T(8,128)(2,1)S(1)} %copy-done.23, bf16[256,1536]{1,0:T(8,128)(2,1)} %get-tuple-element.164, bf16[256,1536]{1,0:T(8,128)(2,1)} %get-tuple-element.163, f32[256]{0:T(256)S(1)} %multiply_multiply_fusion, ...), kind=kLoop, calls=%fused_computation.8 | loop fusion | flops 8650752 | bytes 9445376 | tf_op jit(solution)/shard_map/sub | solution.py:1018
  248.3 3.7 %collective-permute-done.43.refs_3_ = bf16[208,1152]{1,0:T(8,128)(2,1)} collective-permute-done((bf16[208,1152]{1,0:T(8,128)(2,1)}, bf16[208,1152]{1,0:T(8,128)(2,1)}, u32[]{:S(2)}, u32[]{:S(2)}) %collective-permute-start.43) | collective-permute-done | bytes 479264 | tf_op jit(solution)/shard_map/ppermute | solution.py:805
  (246 shorter events, 100.4 us)
Async XLA Ops:
  3.5 30.3 %collective-permute-start.2 = (bf16[256,1536]{1,0:T(8,128)(2,1)S(1)}, bf16[256,1536]{1,0:T(8,128)(2,1)}, u32[]{:S(2)}, u32[]{:S(2)}) collective-permute-start(bf16[256,1536]{1,0:T(8,128)(2,1)S(1)} %fusion.3.refs_0_), channel_id=1, source_target_pairs={{0,2},{1,3},{2,0},{3,1},{4,6},{5,7},{6,4},{7,5},{8,10},{9,11},{10,... | collective-permute-start | bytes 2359304 | tf_op jit(solution)/shard_map/ppermute | solution.py:811
  6.5 29.6 %collective-permute-start = (bf16[256,1536]{1,0:T(8,128)(2,1)S(1)}, bf16[256,1536]{1,0:T(8,128)(2,1)S(1)}, u32[]{:S(2)}, u32[]{:S(2)}) collective-permute-start(bf16[256,1536]{1,0:T(8,128)(2,1)S(1)} %fusion.3.refs_0_), channel_id=1, source_target_pairs={{0,1},{1,0},{2,3},{3,2},{4,5},{5,4},{6,7},{7,6},{8,9},{9,8},{10,11... | collective-permute-start | bytes 2359304 | tf_op jit(solution)/shard_map/ppermute | solution.py:811
  8.3 21.9 %collective-permute-start.5 = (bf16[192,1152]{1,0:T(8,128)(2,1)S(1)}, bf16[192,1152]{1,0:T(8,128)(2,1)S(1)}, u32[]{:S(2)}, u32[]{:S(2)}) collective-permute-start(bf16[192,1152]{1,0:T(8,128)(2,1)S(1)} %concatenate.18.refs_0_), channel_id=1, source_target_pairs={{0,16},{4,20},{8,24},{12,28},{16,0},{20,4},{24,8},{28,12},{1,17},{... | collective-permute-start | bytes 1327112 | tf_op jit(solution)/shard_map/ppermute | solution.py:805
  11.0 19.4 %collective-permute-start.4 = (bf16[192,1152]{1,0:T(8,128)(2,1)S(1)}, bf16[192,1152]{1,0:T(8,128)(2,1)S(1)}, u32[]{:S(2)}, u32[]{:S(2)}) collective-permute-start(bf16[192,1152]{1,0:T(8,128)(2,1)S(1)} %concatenate.18.refs_0_), channel_id=1, source_target_pairs={{0,8},{4,12},{8,0},{12,4},{16,24},{20,28},{24,16},{28,20},{1,9},{5... | collective-permute-start | bytes 1327112 | tf_op jit(solution)/shard_map/ppermute | solution.py:805
  32.5 13.6 %collective-permute-start.10 = (bf16[192,1152]{1,0:T(8,128)(2,1)}, bf16[192,1152]{1,0:T(8,128)(2,1)S(1)}, u32[]{:S(2)}, u32[]{:S(2)}) collective-permute-start(bf16[192,1152]{1,0:T(8,128)(2,1)} %get-tuple-element.101.refs_2_), channel_id=1, source_target_pairs={{8,0},{12,4},{16,24},{20,28},{9,1},{13,5},{17,25},{21,29},{10,2},{... | collective-permute-start | bytes 1327112 | tf_op jit(solution)/shard_map/ppermute | solution.py:814
  49.6 30.2 %collective-permute-start.17 = (bf16[192,1536]{1,0:T(8,128)(2,1)}, bf16[192,1536]{1,0:T(8,128)(2,1)}, u32[]{:S(2)}, u32[]{:S(2)}) collective-permute-start(bf16[192,1536]{1,0:T(8,128)(2,1)} %pinned.23.refs_0_), channel_id=1, source_target_pairs={{0,16},{4,20},{8,24},{12,28},{16,0},{20,4},{24,8},{28,12},{1,17},{... | collective-permute-start | bytes 1769480 | tf_op jit(solution)/shard_map/ppermute | solution.py:805
  52.8 27.8 %collective-permute-start.16 = (bf16[192,1536]{1,0:T(8,128)(2,1)}, bf16[192,1536]{1,0:T(8,128)(2,1)}, u32[]{:S(2)}, u32[]{:S(2)}) collective-permute-start(bf16[192,1536]{1,0:T(8,128)(2,1)} %pinned.23.refs_0_), channel_id=1, source_target_pairs={{0,8},{4,12},{8,0},{12,4},{16,24},{20,28},{24,16},{28,20},{1,9},{5... | collective-permute-start | bytes 1769480 | tf_op jit(solution)/shard_map/ppermute | solution.py:805
  55.9 27.6 %collective-permute-start.13 = (bf16[256,1536]{1,0:T(8,128)(2,1)}, bf16[256,1536]{1,0:T(8,128)(2,1)}, u32[]{:S(2)}, u32[]{:S(2)}) collective-permute-start(bf16[256,1536]{1,0:T(8,128)(2,1)} %pinned.21.refs_0_), channel_id=1, source_target_pairs={{0,2},{1,3},{2,0},{3,1},{4,6},{5,7},{6,4},{7,5},{8,10},{9,11},{10,... | collective-permute-start | bytes 2359304 | tf_op jit(solution)/shard_map/ppermute | solution.py:811
  56.4 28.9 %collective-permute-start.12 = (bf16[256,1536]{1,0:T(8,128)(2,1)}, bf16[256,1536]{1,0:T(8,128)(2,1)}, u32[]{:S(2)}, u32[]{:S(2)}) collective-permute-start(bf16[256,1536]{1,0:T(8,128)(2,1)} %pinned.21.refs_0_), channel_id=1, source_target_pairs={{0,1},{1,0},{2,3},{3,2},{4,5},{5,4},{6,7},{7,6},{8,9},{9,8},{10,11... | collective-permute-start | bytes 2359304 | tf_op jit(solution)/shard_map/ppermute | solution.py:811
  82.2 16.8 %collective-permute-start.19 = (bf16[192,1536]{1,0:T(8,128)(2,1)}, bf16[192,1536]{1,0:T(8,128)(2,1)}, u32[]{:S(2)}, u32[]{:S(2)}) collective-permute-start(bf16[192,1536]{1,0:T(8,128)(2,1)} %get-tuple-element.111.refs_2_), channel_id=1, source_target_pairs={{8,0},{12,4},{16,24},{20,28},{9,1},{13,5},{17,25},{21,29},{10,2},{... | collective-permute-start | bytes 1769480 | tf_op jit(solution)/shard_map/ppermute | solution.py:814
  87.0 14.7 %collective-permute-start.14 = (bf16[128,1536]{1,0:T(8,128)(2,1)}, bf16[128,1536]{1,0:T(8,128)(2,1)}, u32[]{:S(2)}, u32[]{:S(2)}) collective-permute-start(bf16[128,1536]{1,0:T(8,128)(2,1)} %get-tuple-element.107), channel_id=1, source_target_pairs={{0,2},{1,3},{2,0},{3,1},{4,6},{5,7},{6,4},{7,5},{8,10},{9,11},{10,... | collective-permute-start | bytes 1179656 | tf_op jit(solution)/shard_map/ppermute | solution.py:811
  87.5 14.2 %collective-permute-start.15 = (bf16[128,1536]{1,0:T(8,128)(2,1)}, bf16[128,1536]{1,0:T(8,128)(2,1)}, u32[]{:S(2)}, u32[]{:S(2)}) collective-permute-start(bf16[128,1536]{1,0:T(8,128)(2,1)} %get-tuple-element.108), channel_id=1, source_target_pairs={{0,1},{1,0},{2,3},{3,2},{4,5},{5,4},{6,7},{7,6},{8,9},{9,8},{10,11... | collective-permute-start | bytes 1179656 | tf_op jit(solution)/shard_map/ppermute | solution.py:811
  140.7 24.1 %collective-permute-start.32 = (bf16[192,1536]{1,0:T(8,128)(2,1)}, bf16[192,1536]{1,0:T(8,128)(2,1)}, u32[]{:S(2)}, u32[]{:S(2)}) collective-permute-start(bf16[192,1536]{1,0:T(8,128)(2,1)} %get-tuple-element.138), channel_id=1, source_target_pairs={{8,16},{12,20},{16,8},{20,12},{9,17},{13,21},{17,9},{21,13},{10,18... | collective-permute-start | bytes 1769480 | tf_op jit(solution)/shard_map/ppermute | solution.py:814
  142.2 22.6 %collective-permute-start.31 = (bf16[192,1536]{1,0:T(8,128)(2,1)}, bf16[192,1536]{1,0:T(8,128)(2,1)}, u32[]{:S(2)}, u32[]{:S(2)}) collective-permute-start(bf16[192,1536]{1,0:T(8,128)(2,1)} %get-tuple-element.138), channel_id=1, source_target_pairs={{0,8},{4,12},{24,16},{28,20},{1,9},{5,13},{25,17},{29,21},{2,10},{... | collective-permute-start | bytes 1769480 | tf_op jit(solution)/shard_map/ppermute | solution.py:814
  147.1 45.5 %collective-permute-start.28 = (bf16[256,1536]{1,0:T(8,128)(2,1)}, bf16[256,1536]{1,0:T(8,128)(2,1)}, u32[]{:S(2)}, u32[]{:S(2)}) collective-permute-start(bf16[256,1536]{1,0:T(8,128)(2,1)} %get-tuple-element.127), channel_id=1, source_target_pairs={{0,1},{1,0},{2,3},{3,2},{4,5},{5,4},{6,7},{7,6},{8,9},{9,8},{10,11... | collective-permute-start | bytes 2359304 | tf_op jit(solution)/shard_map/ppermute | solution.py:811
  148.7 44.0 %collective-permute-start.29 = (bf16[256,1536]{1,0:T(8,128)(2,1)}, bf16[256,1536]{1,0:T(8,128)(2,1)}, u32[]{:S(2)}, u32[]{:S(2)}) collective-permute-start(bf16[256,1536]{1,0:T(8,128)(2,1)} %get-tuple-element.128), channel_id=1, source_target_pairs={{0,2},{1,3},{2,0},{3,1},{4,6},{5,7},{6,4},{7,5},{8,10},{9,11},{10,... | collective-permute-start | bytes 2359304 | tf_op jit(solution)/shard_map/ppermute | solution.py:811
  149.8 42.8 %collective-permute-start.30 = (bf16[256,1536]{1,0:T(8,128)(2,1)}, bf16[256,1536]{1,0:T(8,128)(2,1)}, u32[]{:S(2)}, u32[]{:S(2)}) collective-permute-start(bf16[256,1536]{1,0:T(8,128)(2,1)} %get-tuple-element.129), channel_id=1, source_target_pairs={{0,3},{1,2},{2,1},{3,0},{4,7},{5,6},{6,5},{7,4},{8,11},{9,10},{10,... | collective-permute-start | bytes 2359304 | tf_op jit(solution)/shard_map/ppermute | solution.py:811
  166.4 27.5 %collective-permute-start.34 = (bf16[192,1536]{1,0:T(8,128)(2,1)S(1)}, bf16[192,1536]{1,0:T(8,128)(2,1)S(1)}, u32[]{:S(2)}, u32[]{:S(2)}) collective-permute-start(bf16[192,1536]{1,0:T(8,128)(2,1)S(1)} %add_convert_fusion), channel_id=1, source_target_pairs={{0,16},{4,20},{8,24},{12,28},{16,0},{20,4},{24,8},{28,12},{1,17},{... | collective-permute-start | bytes 1769480 | tf_op jit(solution)/shard_map/ppermute | solution.py:805
  166.4 27.6 %collective-permute-start.33 = (bf16[192,1536]{1,0:T(8,128)(2,1)S(1)}, bf16[192,1536]{1,0:T(8,128)(2,1)S(1)}, u32[]{:S(2)}, u32[]{:S(2)}) collective-permute-start(bf16[192,1536]{1,0:T(8,128)(2,1)S(1)} %copy-done.7), channel_id=1, source_target_pairs={{0,8},{4,12},{8,0},{12,4},{16,24},{20,28},{24,16},{28,20},{1,9},{5... | collective-permute-start | bytes 1769480 | tf_op jit(solution)/shard_map/ppermute | solution.py:805
  212.9 13.8 %collective-permute-start.40 = (bf16[208,1152]{1,0:T(8,128)(2,1)}, bf16[208,1152]{1,0:T(8,128)(2,1)}, u32[]{:S(2)}, u32[]{:S(2)}) collective-permute-start(bf16[208,1152]{1,0:T(8,128)(2,1)} %get-tuple-element.159), channel_id=1, source_target_pairs={{0,8},{4,12},{24,16},{28,20},{1,9},{5,13},{25,17},{29,21},{2,10},{... | collective-permute-start | bytes 1437704 | tf_op jit(solution)/shard_map/ppermute | solution.py:814
  220.0 19.3 %collective-permute-start.38 = (bf16[256,1536]{1,0:T(8,128)(2,1)}, bf16[256,1536]{1,0:T(8,128)(2,1)}, u32[]{:S(2)}, u32[]{:S(2)}) collective-permute-start(bf16[256,1536]{1,0:T(8,128)(2,1)} %pad_maximum_fusion), channel_id=1, source_target_pairs={{0,1},{1,0},{2,3},{3,2},{4,5},{5,4},{6,7},{7,6},{8,9},{9,8},{10,11... | collective-permute-start | bytes 2359304 | tf_op jit(solution)/shard_map/ppermute | solution.py:811
  221.9 19.1 %collective-permute-start.39 = (bf16[256,1536]{1,0:T(8,128)(2,1)}, bf16[256,1536]{1,0:T(8,128)(2,1)}, u32[]{:S(2)}, u32[]{:S(2)}) collective-permute-start(bf16[256,1536]{1,0:T(8,128)(2,1)} %pad_maximum_fusion.1), channel_id=1, source_target_pairs={{0,2},{1,3},{2,0},{3,1},{4,6},{5,7},{6,4},{7,5},{8,10},{9,11},{10,... | collective-permute-start | bytes 2359304 | tf_op jit(solution)/shard_map/ppermute | solution.py:811
  228.7 23.3 %collective-permute-start.43 = (bf16[208,1152]{1,0:T(8,128)(2,1)}, bf16[208,1152]{1,0:T(8,128)(2,1)}, u32[]{:S(2)}, u32[]{:S(2)}) collective-permute-start(bf16[208,1152]{1,0:T(8,128)(2,1)} %add_convert_fusion.1.refs_2_.refs_3_), channel_id=1, source_target_pairs={{0,16},{4,20},{8,24},{12,28},{16,0},{20,4},{24,8},{28,12},{1,17},{... | collective-permute-start | bytes 1437704 | tf_op jit(solution)/shard_map/ppermute | solution.py:805
  231.4 20.7 %collective-permute-start.42 = (bf16[208,1152]{1,0:T(8,128)(2,1)}, bf16[208,1152]{1,0:T(8,128)(2,1)}, u32[]{:S(2)}, u32[]{:S(2)}) collective-permute-start(bf16[208,1152]{1,0:T(8,128)(2,1)} %get-tuple-element.166), channel_id=1, source_target_pairs={{0,8},{4,12},{8,0},{12,4},{16,24},{20,28},{24,16},{28,20},{1,9},{5... | collective-permute-start | bytes 1437704 | tf_op jit(solution)/shard_map/ppermute | solution.py:805
  (74 other events, 497.3 us)

commit v6 on v5

--- a/solution.py
+++ b/solution.py
@@ -849,6 +849,11 @@
             return [lax.all_gather(shard, "tensor", axis=0, tiled=True)]
         return [shard, self.over_tensor(shard, 1), self.over_tensor(shard, 2)]
 
+    def gather_direct(self, shard):
+        if self.tensor != 4:
+            return self.gather_first(shard)
+        return [shard] + [self.over_tensor(shard, k) for k in range(1, 4)]
+
     def gather_last(self, pieces, earlier):
         if self.tensor != 4:
             return pieces
@@ -933,7 +938,7 @@
     joint = joint_shard(gate_proj, out_proj, [cot_copy])
     row_pieces = net.gather_last(row_pieces, [])
     scan_pieces = net.gather_cores(scan_mine, row_pieces[3:], [])
-    cot_pieces = net.gather_first(pinned([cot_copy], row_pieces[3:] + scan_pieces[chips:])[0])
+    cot_pieces = net.gather_direct(pinned([cot_copy], row_pieces[3:] + scan_pieces[chips:])[0])
     joint_mine = net.gather_near(pinned([joint], reached)[0])
 
     taps = jnp.concatenate(
@@ -959,12 +964,11 @@
         "project",
     )
     scanned, pre, states = scan_forward(raw, taps, head_rows, skip_row, [])
-    cot_pieces = net.gather_last(cot_pieces, [scanned])
     joint_mine = net.gather_far(joint_mine, [scanned])
     gate, gated, grad_out, token_sums, joint_full, cot_rows = product(
         place,
         cot_pieces,
-        net.gather_cores(joint_mine, cot_pieces[3:], []),
+        net.gather_cores(joint_mine, cot_pieces[1:], []),
         mix_epilogue,
         [(rows, False), (stay(scanned), True), (gain, False)],
         [(channels, f32), (channels, f32), (channels, f32), (None, 2)],

time: 266 us -> 264 us (level)
  starting transfers between devices: 54.7 us -> 59.3 us
  waiting for transfers between devices: 57 us -> 53.7 us
    ppermute x8, waiting for transfers between devices: 26 us -> 21.2 us  [over_chips(): return lax.ppermute(values, 'dp', [(i, i ^ 2 * k) for i in range(self.dp)])]
    ppermute x21 -> x20, starting transfers between devices: 23 us -> 26.2 us  [over_tensor(): lax.ppermute(values, 'tensor', [(i, i ^ k) for i in range(self.tensor)])]
    slice x4 -> x2, local copies, waits for them, and re-layouts: 5.35 us -> 2.62 us  [gather_last(): halves = [pieces[1][:half], pieces[2][half:]]]
    unnamed x105 -> x103, local copies, waits for them, and re-layouts: 12 us -> 12.9 us
    ppermute x21 -> x20, waiting for transfers between devices: 10.6 us -> 10.8 us  [over_tensor(): lax.ppermute(values, 'tensor', [(i, i ^ k) for i in range(self.tensor)])]
  transfers between devices with their start and end apart: 47 -> 46, of which waited for: 22 -> 22; matrix products, arithmetic and copies ran while one was open for 13% -> 12% of each run, Pallas kernels for 26% -> 26%
where the time goes in v6:
time: 264 us; the launch traced here: 262 us
  Pallas kernels  106 us (40%)
  starting transfers between devices  59.3 us (22%)
  waiting for transfers between devices  53.7 us (20%)
  other arithmetic  21.5 us (8%)
  local copies, waits for them, and re-layouts  21 us (8%)
    pallas_call x2, Pallas kernels, scan_backward(): pl.pallas_call(functools.partial(backward_kernel, part, len(earlier)), gr...  27.2 us
    ppermute x20, starting transfers between devices, over_tensor(): lax.ppermute(values, 'tensor', [(i, i ^ k) for i in range(self.tensor)])  26.2 us
    ppermute x8, waiting for transfers between devices, over_chips(): return lax.ppermute(values, 'dp', [(i, i ^ 2 * k) for i in range(self.dp)])  21.2 us
    pallas_call x2, Pallas kernels, product(): pl.pallas_call(functools.partial(product_kernel, heights, chips, epilogue...  20 us
    ppermute x8, waiting for transfers between devices, between(): lax.ppermute(values, 'dp', [(2 * a + c, 2 * b + c) for a, b in pairs for...  18.7 us
    ppermute x8, starting transfers between devices, over_chips(): return lax.ppermute(values, 'dp', [(i, i ^ 2 * k) for i in range(self.dp)])  15.6 us
    ppermute x8, starting transfers between devices, between(): lax.ppermute(values, 'dp', [(2 * a + c, 2 * b + c) for a, b in pairs for...  15.2 us
    pallas_call x2, Pallas kernels, weight_grads(): pl.pallas_call(functools.partial(small_kernel if small else grads_kernel,...  14.7 us
  transfers between devices with their start and end apart: 46, of which 22 were waited for; matrix products, arithmetic and copies ran while one was open for 12% of the time, Pallas kernels for 26%

profile of v6, /device:TPU:0, one launch (start us, length us, event | category | flops | bytes accessed | tf_op | source)
XLA Modules:
  0.0 262.4 jit_solution(4184735312669040256)
XLA Ops:
  2.7 4.1 %collective-permute-start.5 = (bf16[192,1152]{1,0:T(8,128)(2,1)S(1)}, bf16[192,1152]{1,0:T(8,128)(2,1)S(1)}, u32[]{:S(2)}, u32[]{:S(2)}) collective-permute-start(bf16[192,1152]{1,0:T(8,128)(2,1)S(1)} %concatenate.18.refs_0_), channel_id=1, source_target_pairs={{0,16},{4,20},{8,24},{12,28},{16,0},{20,4},{24,8},{28,12},{1,17},{... | collective-permute-start | bytes 1327112 | tf_op jit(solution)/shard_map/ppermute | solution.py:805
  12.0 14.6 %collective-permute-done.5.refs_2_ = bf16[192,1152]{1,0:T(8,128)(2,1)S(1)} collective-permute-done((bf16[192,1152]{1,0:T(8,128)(2,1)S(1)}, bf16[192,1152]{1,0:T(8,128)(2,1)S(1)}, u32[]{:S(2)}, u32[]{:S(2)}) %collective-permute-start.5) | collective-permute-done | bytes 442400 | tf_op jit(solution)/shard_map/ppermute | solution.py:805
  46.0 4.3 %collective-permute-start.16 = (bf16[192,1536]{1,0:T(8,128)(2,1)}, bf16[192,1536]{1,0:T(8,128)(2,1)}, u32[]{:S(2)}, u32[]{:S(2)}) collective-permute-start(bf16[192,1536]{1,0:T(8,128)(2,1)} %pinned.21.refs_0_), channel_id=1, source_target_pairs={{0,16},{4,20},{8,24},{12,28},{16,0},{20,4},{24,8},{28,12},{1,17},{... | collective-permute-start | bytes 1769480 | tf_op jit(solution)/shard_map/ppermute | solution.py:805
  56.1 9.0 %project.1 = (f32[1024,1152]{1,0:T(8,128)}, bf16[1536,1152]{1,0:T(8,128)(2,1)S(1)}, bf16[1024,1536]{1,0:T(8,128)(2,1)S(1)}) custom-call(s32[3]{0:T(128)S(1)} %pad_add_fusion.place, bf16[256,1536]{1,0:T(8,128)(2,1)} %copy-done.25, bf16[256,1536]{1,0:T(8,128)(2,1)} %copy-done.21, bf16[256,1536]{1,0:T(8,128)(2,1)} %collective-permute-done.2.refs_2_, ...), custom_call_target="tpu_custom_call" | custom-call | tf_op jit(solution)/shard_map/project/pallas_call | solution.py:394
  65.1 11.4 %scan_forward.1 = (f32[1024,768]{1,0:T(8,128)}, f32[1024,1024]{1,0:T(8,128)}, bf16[1024,768]{1,0:T(8,128)(2,1)}) custom-call(f32[1024,1152]{1,0:T(8,128)} %get-tuple-element.103.raw_ref.refs_0_, f32[8,1024]{1,0:T(8,128)S(1)} %fusion.11.taps_ref.refs_4_, f32[8,128]{1,0:T(8,128)S(1)} %select_maximum_fusion.2.heads_ref.refs_5_, ...), custom_call_target="tpu_custom_call" | custom-call | tf_op jit(solution)/shard_map/scan_forward/pallas_call | solution.py:250
  81.4 15.5 %collective-permute-done.18 = bf16[192,1536]{1,0:T(8,128)(2,1)} collective-permute-done((bf16[192,1536]{1,0:T(8,128)(2,1)}, bf16[192,1536]{1,0:T(8,128)(2,1)}, u32[]{:S(2)}, u32[]{:S(2)}) %collective-permute-start.18) | collective-permute-done | bytes 589856 | tf_op jit(solution)/shard_map/ppermute | solution.py:814
  103.5 11.0 %mix.1 = (f32[1024,768]{1,0:T(8,128)S(1)}, f32[1024,768]{1,0:T(8,128)S(1)}, f32[1024,768]{1,0:T(8,128)S(1)}, f32[16,128]{1,0:T(8,128)S(1)}, bf16[1536,1536]{1,0:...) custom-call(s32[3]{0:T(128)S(1)} %pad_add_fusion.place, bf16[256,1536]{1,0:T(8,128)(2,1)} %pinned.20.refs_0_, ...), custom_call_target="tpu_custom_call" | custom-call | tf_op jit(solution)/shard_map/mix/pallas_call | solution.py:394
  120.1 5.2 %gating.1 = (bf16[1024,768]{1,0:T(8,128)(2,1)S(1)}, bf16[1024,768]{1,0:T(8,128)(2,1)S(1)}, bf16[1024,768]{1,0:T(8,128)(2,1)}, f32[8,768]{1,0:T(8,128)S(1)}) custom-call(f32[1024,768]{1,0:T(8,128)S(1)} %get-tuple-element.112.grad_out, f32[1024,768]{1,0:T(8,128)S(1)} %get-tuple-element.113.gated, f32[1024,768]{1,0:T(8,128)S(1)} %get-tuple-element.114.gate, ...), custom_call_target="tpu_custom_call" | custom-call | tf_op jit(solution)/shard_map/gating/pallas_call | solution.py:498
  125.3 6.5 %grad_joint_proj.1 = (bf16[4,192,1536]{2,1,0:T(8,128)(2,1)S(1)}, bf16[4,192,1536]{2,1,0:T(8,128)(2,1)S(1)}) custom-call(s32[3]{0:T(128)S(1)} %pad_add_fusion.place, bf16[1024,1536]{1,0:T(8,128)(2,1)S(1)} %get-tuple-element.111.refs_12_.refs_0_.refs_4_, bf16[1024,1536]{1,0:T(8,128)(2,1)S(1)} %get-tuple-element.118.refs_1_, ...), custom_call_target="tpu_custom_call" | custom-call | tf_op jit(solution)/shard_map/grad_joint_proj/pallas_call | solution.py:588
  131.9 3.8 %branch.1.refs_0_ = bf16[1024,1536]{1,0:T(8,128)(2,1)S(1)} custom-call(s32[3]{0:T(128)S(1)} %pad_add_fusion.place, bf16[1024,768]{1,0:T(8,128)(2,1)S(1)} %get-tuple-element.116.refs_3_.refs_0_, bf16[1536,1536]{1,0:T(8,128)(2,1)S(1)} %get-tuple-element.117.refs_1_.refs_2_, bf16[4,192,1536]{2,1,0:T(8,128)(2,1)S(1)} %get-tuple-element.120.refs_2_), custom_call_target="tpu_custom_call" | custom-call | tf_op jit(solution)/shard_map/branch/pallas_call | solution.py:662
  140.0 3.5 %collective-permute-start.30 = (bf16[192,1536]{1,0:T(8,128)(2,1)}, bf16[192,1536]{1,0:T(8,128)(2,1)}, u32[]{:S(2)}, u32[]{:S(2)}) collective-permute-start(bf16[192,1536]{1,0:T(8,128)(2,1)} %get-tuple-element.134), channel_id=1, source_target_pairs={{0,8},{4,12},{24,16},{28,20},{1,9},{5,13},{25,17},{29,21},{2,10},{... | collective-permute-start | bytes 1769480 | tf_op jit(solution)/shard_map/ppermute | solution.py:814
  149.5 13.2 %scan_backward_0.1 = (bf16[1024,1152]{1,0:T(8,128)(2,1)}, f32[8,1024]{1,0:T(8,128)}, f32[8,128]{1,0:T(8,128)}, f32[128,768]{1,0:T(8,128)}, f32[8,1024]{1,0:T(8,128)}) custom-call(f32[1024,1152]{1,0:T(8,128)} %get-tuple-element.103.raw_ref.refs_0_, f32[1024,1024]{1,0:T(8,128)} %get-tuple-element.126.refs_1_, bf16[1024,768]{1,0:T(8,128)(2,1)} %get-tuple-element.127.refs_2_, ...), custom_call_target="tpu_custom_call" | custom-call | tf_op jit(solution)/shard_map/scan_backward_0/pallas_call | solution.py:283
  164.2 2.7 %collective-permute-start.32 = (bf16[192,1536]{1,0:T(8,128)(2,1)S(1)}, bf16[192,1536]{1,0:T(8,128)(2,1)S(1)}, u32[]{:S(2)}, u32[]{:S(2)}) collective-permute-start(bf16[192,1536]{1,0:T(8,128)(2,1)S(1)} %copy-done.7), channel_id=1, source_target_pairs={{0,8},{4,12},{8,0},{12,4},{16,24},{20,28},{24,16},{28,20},{1,9},{5... | collective-permute-start | bytes 1769480 | tf_op jit(solution)/shard_map/ppermute | solution.py:805
  167.0 14.0 %scan_backward_1.1 = (bf16[1024,1152]{1,0:T(8,128)(2,1)}, f32[8,1024]{1,0:T(8,128)}, f32[8,128]{1,0:T(8,128)}, f32[128,768]{1,0:T(8,128)}, f32[8,1024]{1,0:T(8,128)}) custom-call(f32[1024,1152]{1,0:T(8,128)} %get-tuple-element.103.raw_ref.refs_0_, f32[1024,1024]{1,0:T(8,128)} %get-tuple-element.126.refs_1_, ...), custom_call_target="tpu_custom_call", output_to_operand_aliasing={{0}: (7, {})} | custom-call | tf_op jit(solution)/shard_map/scan_backward_1/pallas_call | solution.py:283
  181.1 9.2 %grad_normed.1 = (bf16[1024,1536]{1,0:T(8,128)(2,1)S(1)}, f32[8,1536]{1,0:T(8,128)S(1)}) custom-call(s32[3]{0:T(128)S(1)} %pad_add_fusion.place, bf16[1024,768]{1,0:T(8,128)(2,1)S(1)} %copy-done.5, bf16[1024,1152]{1,0:T(8,128)(2,1)} %get-tuple-element.137.refs_1_, bf16[1536,1536]{1,0:T(8,128)(2,1)S(1)} %bitcast.20, bf16[1536,1152]{1,0:T(8,128)(2,1)S(1)} %copy-done.11, ...), custom_call_target="tpu_custom_call" | custom-call | tf_op jit(solution)/shard_map/grad_normed/pallas_call | solution.py:662
  191.8 8.2 %grad_scan_proj.1 = (bf16[4,208,1152]{2,1,0:T(8,128)(2,1)}, bf16[4,208,1152]{2,1,0:T(8,128)(2,1)}) custom-call(s32[3]{0:T(128)S(1)} %pad_add_fusion.place, bf16[1024,1536]{1,0:T(8,128)(2,1)S(1)} %get-tuple-element.111.refs_12_.refs_0_.refs_4_, bf16[1024,1152]{1,0:T(8,128)(2,1)} %get-tuple-element.137.refs_1_, f32[8,1024]{1,0:T(8,128)S(1)} %copy-done.14, ...), custom_call_target="tpu_custom_call" | custom-call | tf_op jit(solution)/shard_map/grad_scan_proj/pallas_call | solution.py:588
  205.8 3.7 %pairs.3 = (f32[208,1152]{1,0:T(8,128)}, bf16[208,1152]{1,0:T(8,128)(2,1)}, bf16[208,1152]{1,0:T(8,128)(2,1)}, bf16[208,1152]{1,0:T(8,128)(2,1)}) custom-call(bf16[4,208,1152]{2,1,0:T(8,128)(2,1)} %get-tuple-element.149.keep, bf16[4,208,1152]{2,1,0:T(8,128)(2,1)} %copy-done.26), custom_call_target="tpu_custom_call" | custom-call | tf_op jit(solution)/shard_map/pairs/pallas_call | solution.py:624
  210.9 4.0 %collective-permute-start.39 = (bf16[208,1152]{1,0:T(8,128)(2,1)}, bf16[208,1152]{1,0:T(8,128)(2,1)}, u32[]{:S(2)}, u32[]{:S(2)}) collective-permute-start(bf16[208,1152]{1,0:T(8,128)(2,1)} %get-tuple-element.155), channel_id=1, source_target_pairs={{0,8},{4,12},{24,16},{28,20},{1,9},{5,13},{25,17},{29,21},{2,10},{... | collective-permute-start | bytes 1437704 | tf_op jit(solution)/shard_map/ppermute | solution.py:814
  221.9 2.6 collective-permute-done.39.refs_0_
  226.6 2.6 %collective-permute-start.42 = (bf16[208,1152]{1,0:T(8,128)(2,1)}, bf16[208,1152]{1,0:T(8,128)(2,1)}, u32[]{:S(2)}, u32[]{:S(2)}) collective-permute-start(bf16[208,1152]{1,0:T(8,128)(2,1)} %add_convert_fusion.1.refs_2_.refs_3_), channel_id=1, source_target_pairs={{0,16},{4,20},{8,24},{12,28},{16,0},{20,4},{24,8},{28,12},{1,17},{... | collective-permute-start | bytes 1437704 | tf_op jit(solution)/shard_map/ppermute | solution.py:805
  232.3 4.9 %collective-permute-done.37.refs_0_ = bf16[256,1536]{1,0:T(8,128)(2,1)} collective-permute-done((bf16[256,1536]{1,0:T(8,128)(2,1)}, bf16[256,1536]{1,0:T(8,128)(2,1)}, u32[]{:S(2)}, u32[]{:S(2)}) %collective-permute-start.37) | collective-permute-done | bytes 786464 | tf_op jit(solution)/shard_map/ppermute | solution.py:811
  241.8 5.0 %fusion.5 = (f32[256,1536]{1,0:T(8,128)}, bf16[256,1536]{1,0:T(8,128)(2,1)}) fusion(bf16[256,1536]{1,0:T(8,128)(2,1)S(1)} %copy-done.17, bf16[256,1536]{1,0:T(8,128)(2,1)S(1)} %copy-done.24, bf16[256,1536]{1,0:T(8,128)(2,1)} %get-tuple-element.160, bf16[256,1536]{1,0:T(8,128)(2,1)} %get-tuple-element.159, f32[256]{0:T(256)S(1)} %multiply_multiply_fusion, ...), kind=kLoop, calls=%fused_computation.8 | loop fusion | flops 8650752 | bytes 9445376 | tf_op jit(solution)/shard_map/sub | solution.py:1022
  246.8 2.8 %collective-permute-done.42.refs_3_ = bf16[208,1152]{1,0:T(8,128)(2,1)} collective-permute-done((bf16[208,1152]{1,0:T(8,128)(2,1)}, bf16[208,1152]{1,0:T(8,128)(2,1)}, u32[]{:S(2)}, u32[]{:S(2)}) %collective-permute-start.42) | collective-permute-done | bytes 479264 | tf_op jit(solution)/shard_map/ppermute | solution.py:805
  252.0 2.8 %collective-permute-start.45 = (bf16[208,256]{1,0:T(8,128)(2,1)S(1)}, bf16[208,256]{1,0:T(8,128)(2,1)S(1)}, u32[]{:S(2)}, u32[]{:S(2)}) collective-permute-start(bf16[208,256]{1,0:T(8,128)(2,1)S(1)} %get-tuple-element.163.refs_0_), channel_id=1, source_target_pairs={{0,3},{1,2},{2,1},{3,0},{4,7},{5,6},{6,5},{7,4},{8,11},{9,10},{10,... | collective-permute-start | bytes 319496 | tf_op jit(solution)/shard_map/ppermute | solution.py:811
  (239 shorter events, 96.4 us)
Async XLA Ops:
  2.7 23.9 %collective-permute-start.5 = (bf16[192,1152]{1,0:T(8,128)(2,1)S(1)}, bf16[192,1152]{1,0:T(8,128)(2,1)S(1)}, u32[]{:S(2)}, u32[]{:S(2)}) collective-permute-start(bf16[192,1152]{1,0:T(8,128)(2,1)S(1)} %concatenate.18.refs_0_), channel_id=1, source_target_pairs={{0,16},{4,20},{8,24},{12,28},{16,0},{20,4},{24,8},{28,12},{1,17},{... | collective-permute-start | bytes 1327112 | tf_op jit(solution)/shard_map/ppermute | solution.py:805
  6.8 19.9 %collective-permute-start.4 = (bf16[192,1152]{1,0:T(8,128)(2,1)S(1)}, bf16[192,1152]{1,0:T(8,128)(2,1)S(1)}, u32[]{:S(2)}, u32[]{:S(2)}) collective-permute-start(bf16[192,1152]{1,0:T(8,128)(2,1)S(1)} %concatenate.18.refs_0_), channel_id=1, source_target_pairs={{0,8},{4,12},{8,0},{12,4},{16,24},{20,28},{24,16},{28,20},{1,9},{5... | collective-permute-start | bytes 1327112 | tf_op jit(solution)/shard_map/ppermute | solution.py:805
  8.9 21.2 %collective-permute-start.2 = (bf16[256,1536]{1,0:T(8,128)(2,1)S(1)}, bf16[256,1536]{1,0:T(8,128)(2,1)}, u32[]{:S(2)}, u32[]{:S(2)}) collective-permute-start(bf16[256,1536]{1,0:T(8,128)(2,1)S(1)} %fusion.3.refs_0_), channel_id=1, source_target_pairs={{0,2},{1,3},{2,0},{3,1},{4,6},{5,7},{6,4},{7,5},{8,10},{9,11},{10,... | collective-permute-start | bytes 2359304 | tf_op jit(solution)/shard_map/ppermute | solution.py:811
  10.5 22.9 %collective-permute-start = (bf16[256,1536]{1,0:T(8,128)(2,1)S(1)}, bf16[256,1536]{1,0:T(8,128)(2,1)S(1)}, u32[]{:S(2)}, u32[]{:S(2)}) collective-permute-start(bf16[256,1536]{1,0:T(8,128)(2,1)S(1)} %fusion.3.refs_0_), channel_id=1, source_target_pairs={{0,1},{1,0},{2,3},{3,2},{4,5},{5,4},{6,7},{7,6},{8,9},{9,8},{10,11... | collective-permute-start | bytes 2359304 | tf_op jit(solution)/shard_map/ppermute | solution.py:811
  28.1 13.8 %collective-permute-start.9 = (bf16[192,1152]{1,0:T(8,128)(2,1)}, bf16[192,1152]{1,0:T(8,128)(2,1)S(1)}, u32[]{:S(2)}, u32[]{:S(2)}) collective-permute-start(bf16[192,1152]{1,0:T(8,128)(2,1)} %get-tuple-element.97.refs_0_), channel_id=1, source_target_pairs={{8,16},{12,20},{16,8},{20,12},{9,17},{13,21},{17,9},{21,13},{10,18... | collective-permute-start | bytes 1327112 | tf_op jit(solution)/shard_map/ppermute | solution.py:814
  28.8 13.7 %collective-permute-start.10 = (bf16[192,1152]{1,0:T(8,128)(2,1)}, bf16[192,1152]{1,0:T(8,128)(2,1)S(1)}, u32[]{:S(2)}, u32[]{:S(2)}) collective-permute-start(bf16[192,1152]{1,0:T(8,128)(2,1)} %get-tuple-element.99.refs_2_), channel_id=1, source_target_pairs={{8,0},{12,4},{16,24},{20,28},{9,1},{13,5},{17,25},{21,29},{10,2},{... | collective-permute-start | bytes 1327112 | tf_op jit(solution)/shard_map/ppermute | solution.py:814
  46.0 31.0 %collective-permute-start.16 = (bf16[192,1536]{1,0:T(8,128)(2,1)}, bf16[192,1536]{1,0:T(8,128)(2,1)}, u32[]{:S(2)}, u32[]{:S(2)}) collective-permute-start(bf16[192,1536]{1,0:T(8,128)(2,1)} %pinned.21.refs_0_), channel_id=1, source_target_pairs={{0,16},{4,20},{8,24},{12,28},{16,0},{20,4},{24,8},{28,12},{1,17},{... | collective-permute-start | bytes 1769480 | tf_op jit(solution)/shard_map/ppermute | solution.py:805
  50.3 28.3 %collective-permute-start.15 = (bf16[192,1536]{1,0:T(8,128)(2,1)}, bf16[192,1536]{1,0:T(8,128)(2,1)}, u32[]{:S(2)}, u32[]{:S(2)}) collective-permute-start(bf16[192,1536]{1,0:T(8,128)(2,1)} %pinned.21.refs_0_), channel_id=1, source_target_pairs={{0,8},{4,12},{8,0},{12,4},{16,24},{20,28},{24,16},{28,20},{1,9},{5... | collective-permute-start | bytes 1769480 | tf_op jit(solution)/shard_map/ppermute | solution.py:805
  52.5 47.2 %collective-permute-start.14 = (bf16[256,1536]{1,0:T(8,128)(2,1)}, bf16[256,1536]{1,0:T(8,128)(2,1)}, u32[]{:S(2)}, u32[]{:S(2)}) collective-permute-start(bf16[256,1536]{1,0:T(8,128)(2,1)} %pinned.20.refs_0_), channel_id=1, source_target_pairs={{0,3},{1,2},{2,1},{3,0},{4,7},{5,6},{6,5},{7,4},{8,11},{9,10},{10,... | collective-permute-start | bytes 2359304 | tf_op jit(solution)/shard_map/ppermute | solution.py:811
  54.9 44.7 %collective-permute-start.13 = (bf16[256,1536]{1,0:T(8,128)(2,1)}, bf16[256,1536]{1,0:T(8,128)(2,1)}, u32[]{:S(2)}, u32[]{:S(2)}) collective-permute-start(bf16[256,1536]{1,0:T(8,128)(2,1)} %pinned.20.refs_0_), channel_id=1, source_target_pairs={{0,2},{1,3},{2,0},{3,1},{4,6},{5,7},{6,4},{7,5},{8,10},{9,11},{10,... | collective-permute-start | bytes 2359304 | tf_op jit(solution)/shard_map/ppermute | solution.py:811
  55.4 44.2 %collective-permute-start.12 = (bf16[256,1536]{1,0:T(8,128)(2,1)}, bf16[256,1536]{1,0:T(8,128)(2,1)}, u32[]{:S(2)}, u32[]{:S(2)}) collective-permute-start(bf16[256,1536]{1,0:T(8,128)(2,1)} %pinned.20.refs_0_), channel_id=1, source_target_pairs={{0,1},{1,0},{2,3},{3,2},{4,5},{5,4},{6,7},{7,6},{8,9},{9,8},{10,11... | collective-permute-start | bytes 2359304 | tf_op jit(solution)/shard_map/ppermute | solution.py:811
  80.1 16.8 %collective-permute-start.18 = (bf16[192,1536]{1,0:T(8,128)(2,1)}, bf16[192,1536]{1,0:T(8,128)(2,1)}, u32[]{:S(2)}, u32[]{:S(2)}) collective-permute-start(bf16[192,1536]{1,0:T(8,128)(2,1)} %get-tuple-element.107.refs_2_), channel_id=1, source_target_pairs={{8,0},{12,4},{16,24},{20,28},{9,1},{13,5},{17,25},{21,29},{10,2},{... | collective-permute-start | bytes 1769480 | tf_op jit(solution)/shard_map/ppermute | solution.py:814
  138.5 24.2 %collective-permute-start.31 = (bf16[192,1536]{1,0:T(8,128)(2,1)}, bf16[192,1536]{1,0:T(8,128)(2,1)}, u32[]{:S(2)}, u32[]{:S(2)}) collective-permute-start(bf16[192,1536]{1,0:T(8,128)(2,1)} %get-tuple-element.134), channel_id=1, source_target_pairs={{8,16},{12,20},{16,8},{20,12},{9,17},{13,21},{17,9},{21,13},{10,18... | collective-permute-start | bytes 1769480 | tf_op jit(solution)/shard_map/ppermute | solution.py:814
  140.0 22.7 %collective-permute-start.30 = (bf16[192,1536]{1,0:T(8,128)(2,1)}, bf16[192,1536]{1,0:T(8,128)(2,1)}, u32[]{:S(2)}, u32[]{:S(2)}) collective-permute-start(bf16[192,1536]{1,0:T(8,128)(2,1)} %get-tuple-element.134), channel_id=1, source_target_pairs={{0,8},{4,12},{24,16},{28,20},{1,9},{5,13},{25,17},{29,21},{2,10},{... | collective-permute-start | bytes 1769480 | tf_op jit(solution)/shard_map/ppermute | solution.py:814
  144.9 45.4 %collective-permute-start.27 = (bf16[256,1536]{1,0:T(8,128)(2,1)}, bf16[256,1536]{1,0:T(8,128)(2,1)}, u32[]{:S(2)}, u32[]{:S(2)}) collective-permute-start(bf16[256,1536]{1,0:T(8,128)(2,1)} %get-tuple-element.123), channel_id=1, source_target_pairs={{0,1},{1,0},{2,3},{3,2},{4,5},{5,4},{6,7},{7,6},{8,9},{9,8},{10,11... | collective-permute-start | bytes 2359304 | tf_op jit(solution)/shard_map/ppermute | solution.py:811
  146.4 43.9 %collective-permute-start.28 = (bf16[256,1536]{1,0:T(8,128)(2,1)}, bf16[256,1536]{1,0:T(8,128)(2,1)}, u32[]{:S(2)}, u32[]{:S(2)}) collective-permute-start(bf16[256,1536]{1,0:T(8,128)(2,1)} %get-tuple-element.124), channel_id=1, source_target_pairs={{0,2},{1,3},{2,0},{3,1},{4,6},{5,7},{6,4},{7,5},{8,10},{9,11},{10,... | collective-permute-start | bytes 2359304 | tf_op jit(solution)/shard_map/ppermute | solution.py:811
  147.9 42.4 %collective-permute-start.29 = (bf16[256,1536]{1,0:T(8,128)(2,1)}, bf16[256,1536]{1,0:T(8,128)(2,1)}, u32[]{:S(2)}, u32[]{:S(2)}) collective-permute-start(bf16[256,1536]{1,0:T(8,128)(2,1)} %get-tuple-element.125), channel_id=1, source_target_pairs={{0,3},{1,2},{2,1},{3,0},{4,7},{5,6},{6,5},{7,4},{8,11},{9,10},{10,... | collective-permute-start | bytes 2359304 | tf_op jit(solution)/shard_map/ppermute | solution.py:811
  164.1 27.5 %collective-permute-start.33 = (bf16[192,1536]{1,0:T(8,128)(2,1)S(1)}, bf16[192,1536]{1,0:T(8,128)(2,1)S(1)}, u32[]{:S(2)}, u32[]{:S(2)}) collective-permute-start(bf16[192,1536]{1,0:T(8,128)(2,1)S(1)} %add_convert_fusion), channel_id=1, source_target_pairs={{0,16},{4,20},{8,24},{12,28},{16,0},{20,4},{24,8},{28,12},{1,17},{... | collective-permute-start | bytes 1769480 | tf_op jit(solution)/shard_map/ppermute | solution.py:805
  164.2 27.6 %collective-permute-start.32 = (bf16[192,1536]{1,0:T(8,128)(2,1)S(1)}, bf16[192,1536]{1,0:T(8,128)(2,1)S(1)}, u32[]{:S(2)}, u32[]{:S(2)}) collective-permute-start(bf16[192,1536]{1,0:T(8,128)(2,1)S(1)} %copy-done.7), channel_id=1, source_target_pairs={{0,8},{4,12},{8,0},{12,4},{16,24},{20,28},{24,16},{28,20},{1,9},{5... | collective-permute-start | bytes 1769480 | tf_op jit(solution)/shard_map/ppermute | solution.py:805
  201.2 13.7 %collective-permute-start.34 = (bf16[128,1536]{1,0:T(8,128)(2,1)}, bf16[128,1536]{1,0:T(8,128)(2,1)S(1)}, u32[]{:S(2)}, u32[]{:S(2)}) collective-permute-start(bf16[128,1536]{1,0:T(8,128)(2,1)} %get-tuple-element.143), channel_id=1, source_target_pairs={{0,2},{1,3},{2,0},{3,1},{4,6},{5,7},{6,4},{7,5},{8,10},{9,11},{10,... | collective-permute-start | bytes 1179656 | tf_op jit(solution)/shard_map/ppermute | solution.py:811
  218.1 19.1 %collective-permute-start.37 = (bf16[256,1536]{1,0:T(8,128)(2,1)}, bf16[256,1536]{1,0:T(8,128)(2,1)}, u32[]{:S(2)}, u32[]{:S(2)}) collective-permute-start(bf16[256,1536]{1,0:T(8,128)(2,1)} %pad_maximum_fusion), channel_id=1, source_target_pairs={{0,1},{1,0},{2,3},{3,2},{4,5},{5,4},{6,7},{7,6},{8,9},{9,8},{10,11... | collective-permute-start | bytes 2359304 | tf_op jit(solution)/shard_map/ppermute | solution.py:811
  220.4 19.1 %collective-permute-start.38 = (bf16[256,1536]{1,0:T(8,128)(2,1)}, bf16[256,1536]{1,0:T(8,128)(2,1)}, u32[]{:S(2)}, u32[]{:S(2)}) collective-permute-start(bf16[256,1536]{1,0:T(8,128)(2,1)} %pad_maximum_fusion.1), channel_id=1, source_target_pairs={{0,2},{1,3},{2,0},{3,1},{4,6},{5,7},{6,4},{7,5},{8,10},{9,11},{10,... | collective-permute-start | bytes 2359304 | tf_op jit(solution)/shard_map/ppermute | solution.py:811
  226.6 23.1 %collective-permute-start.42 = (bf16[208,1152]{1,0:T(8,128)(2,1)}, bf16[208,1152]{1,0:T(8,128)(2,1)}, u32[]{:S(2)}, u32[]{:S(2)}) collective-permute-start(bf16[208,1152]{1,0:T(8,128)(2,1)} %add_convert_fusion.1.refs_2_.refs_3_), channel_id=1, source_target_pairs={{0,16},{4,20},{8,24},{12,28},{16,0},{20,4},{24,8},{28,12},{1,17},{... | collective-permute-start | bytes 1437704 | tf_op jit(solution)/shard_map/ppermute | solution.py:805
  229.2 20.5 %collective-permute-start.41 = (bf16[208,1152]{1,0:T(8,128)(2,1)}, bf16[208,1152]{1,0:T(8,128)(2,1)}, u32[]{:S(2)}, u32[]{:S(2)}) collective-permute-start(bf16[208,1152]{1,0:T(8,128)(2,1)} %get-tuple-element.162), channel_id=1, source_target_pairs={{0,8},{4,12},{8,0},{12,4},{16,24},{20,28},{24,16},{28,20},{1,9},{5... | collective-permute-start | bytes 1437704 | tf_op jit(solution)/shard_map/ppermute | solution.py:805
  (72 other events, 468.4 us)
